TPU v7x, 32 devices: a whole 2x2x4 slice. The times are simulated.
32 devices in a mesh: gx: 4 (over z), gy: 8 (over y, x, core).
Axes of the slice: x: 2, y: 2, z: 4, core: 2. Of those that a mesh axis runs over, the one named last changes fastest.
Arguments:
- rhs: float32 [2048, 2048], P('gx', 'gy'), may hold values from -6 to 6, as said below
- pressure: float32 [2048, 2048], P('gx', 'gy'), may hold values from -6 to 6
- wet_mask: int32 [2048, 2048], P('gx', 'gy'), may hold values 0 or 1
- bathy_class: int32 [2048, 2048], P('gx', 'gy'), may hold values from 0 to 7
Outputs:
- new_pressure: float32 [2048, 2048], P('gx', 'gy')
- final_residual: float32 [2048, 2048], P('gx', 'gy')
Inputs may be any that keep to these rules, and one draw needn't show every extreme that they name: `rhs`: real-valued and rough from cell to cell.
All inputs are finite; a program needn't handle non-finite values. No bound on the sum of `wet_mask` on one device may be relied on, other than what follows from the above.
Results may differ from a plain program's by a relative error of at most 0.0003.
Values sent between devices are 32-bit elements; how exact they have to be, the bound alone decides.
No kernel may reach another device: no remote copies, remote signals or barrier semaphores. Data moves between devices by JAX's collectives and lax.ppermute only.
A program may use at most 128 MiB of HBM per device.

v0:
```python
import jax
import jax.numpy as jnp
from jax import lax
from jax.experimental import pallas as pl
from jax.experimental.pallas import tpu as pltpu
from jax.sharding import PartitionSpec as P

LEVELS = 4
SWEEPS = 12

damping = 0.01
relaxation = 0.8

HALO = 24
LANES = 128
INNER = LANES // 2 - HALO
TOP = 32
GUARD = 8
PIECES = 5
TALL = 16
VMEM_LIMIT = 40 * 1024 * 1024


def lane_of(x):
    return lax.broadcasted_iota(jnp.int32, x.shape, x.ndim - 1)


def roll(x, amount):
    amount %= LANES
    return x if amount == 0 else pltpu.roll(x, amount, x.ndim - 1)


def from_west(tiles, step):
    moved = [roll(t, step) for t in tiles]
    if len(tiles) == 1:
        return moved
    edge = lane_of(tiles[0]) < step
    return [jnp.where(edge, moved[i - 1], moved[i]) for i in range(len(tiles))]


def from_east(tiles, step):
    moved = [roll(t, -step) for t in tiles]
    count = len(tiles)
    if count == 1:
        return moved
    edge = lane_of(tiles[0]) >= LANES - step
    return [jnp.where(edge, moved[(i + 1) % count], moved[i]) for i in range(count)]


def clear_rim(ref):
    rim = GUARD + TOP - HALO
    zeros = jnp.zeros((rim, LANES), jnp.float32)
    for t in range(ref.shape[0]):
        ref[t, 0:rim, :] = zeros
        ref[t, ref.shape[1] - rim :, :] = zeros


def spread(tiles, step):
    second = (lane_of(tiles[0]) // step) % 2 == 1
    return [jnp.where(second, roll(t, step), t) for t in tiles]


def for_parts(start, size, body, part):
    for offset in range(0, size, part):
        body(start + offset, min(part, size - offset))


def for_chunks(rows, body, largest, part):
    sizes = [size for size in range(8, largest + 1, 8) if rows % size == 0]
    if rows <= largest or not sizes:
        for_parts(0, rows, body, part)
        return

    def step(i, carry):
        for_parts(i * sizes[-1], sizes[-1], body, part)
        return carry

    lax.fori_loop(0, rows // sizes[-1], step, 0)


def load(ref, start, size):
    return [ref[t, pl.ds(GUARD + start, size), :] for t in range(ref.shape[0])]


def store(ref, start, size, tiles):
    for t, tile in enumerate(tiles):
        ref[t, pl.ds(GUARD + start, size), :] = tile


def store_twice(ref, start, size, tiles):
    for t, tile in enumerate(tiles):
        ref[t, pl.ds(GUARD + 2 * start, size, stride=2), :] = tile
        ref[t, pl.ds(GUARD + 2 * start + 1, size, stride=2), :] = tile


def clear_guards(ref, rows):
    zeros = jnp.zeros((GUARD, LANES), jnp.float32)
    for t in range(ref.shape[0]):
        ref[t, 0:GUARD, :] = zeros
        ref[t, GUARD + rows : 2 * GUARD + rows, :] = zeros


def beside(mid, north, south, c_west, c_north, c_south, step):
    west = from_west(mid, step)
    east = from_east([c * m for c, m in zip(c_west, mid)], step)
    return [
        (c_west[t] * west[t] + east[t]) + (c_north[t] * north[t] + c_south[t] * south[t]) for t in range(len(mid))
    ]


def beside_of(ref, coeffs, start, size, step):
    c_west_ref, c_north_ref = coeffs
    mid = load(ref, start, size)
    north, south = load(ref, start - 1, size), load(ref, start + 1, size)
    c_west, c_north = load(c_west_ref, start, size), load(c_north_ref, start, size)
    return mid, beside(mid, north, south, c_west, c_north, load(c_north_ref, start + 1, size), step)


def pool_rows(ref, start, size, step):
    out = []
    for t in range(ref.shape[0]):
        even = ref[t, pl.ds(GUARD + start, size // 2, stride=2), :]
        odd = ref[t, pl.ds(GUARD + start + 1, size // 2, stride=2), :]
        both = even + odd
        out.append(both + roll(both, -step))
    return out


def descend(level, height, weight, source, guess, state, diagonal_ref, field, resid, next_weight, next_source, largest, part):
    step = 2**level
    c_west_ref, c_north_ref, scale_ref, smooth_ref = state
    for ref in (weight, field, c_north_ref):
        clear_guards(ref, height)

    def first_pass(start, size):
        w, w_north, w_south = (load(weight, start + k, size) for k in (0, -1, 1))
        c_north = [jnp.minimum(a, b) for a, b in zip(w, w_north)]
        c_south = [jnp.minimum(a, b) for a, b in zip(w, w_south)]
        c_west = [jnp.minimum(a, b) for a, b in zip(w, from_west(w, step))]
        c_east = from_east(c_west, step)
        diagonal = [damping + c_north[t] + c_south[t] + c_west[t] + c_east[t] for t in range(len(w))]
        scale = [relaxation / d for d in diagonal]
        store(c_north_ref, start, size, c_north)
        store(c_west_ref, start, size, c_west)
        store(scale_ref, start, size, scale)
        store(diagonal_ref, start, size, diagonal)
        value = load(source, start, size)
        if guess is None:
            value = [scale[t] * value[t] for t in range(len(w))]
        else:
            mid, north, south = (load(guess, start + k, size) for k in (0, -1, 1))
            around = beside(mid, north, south, c_west, c_north, c_south, step)
            value = [
                (1.0 - relaxation) * mid[t] + scale[t] * (value[t] + around[t]) for t in range(len(w))
            ]
        store(field, start, size, value)
        if next_weight is not None:
            pooled = [0.125 * p for p in pool_rows(weight, start, size, step)]
            store(next_weight, start // 2, size // 2, pooled)

    def second_pass(start, size):
        mid, around = beside_of(field, (c_west_ref, c_north_ref), start, size, step)
        b, scale, diagonal = (load(ref, start, size) for ref in (source, scale_ref, diagonal_ref))
        rest = [(b[t] + around[t]) - diagonal[t] * mid[t] for t in range(len(b))]
        store(smooth_ref, start, size, [mid[t] + scale[t] * rest[t] for t in range(len(b))])
        store(resid, start, size, rest)
        if next_source is not None:
            pooled = [0.25 * p for p in pool_rows(resid, start, size, step)]
            store(next_source, start // 2, size // 2, pooled)

    for_chunks(height, first_pass, largest, part)
    for_chunks(height, second_pass, largest, part)


def descend_all(rows, sources, guess, weights, states, diagonal, field, resid, largest, part):
    for level in range(LEVELS - 1):
        descend(
            level,
            rows >> level,
            weights[level],
            sources[level],
            guess if level == 0 else None,
            states[4 * level : 4 * level + 4],
            diagonal[level],
            field,
            resid,
            weights[level + 1],
            sources[level + 1],
            largest,
            part,
        )


def to_sides(west, east, cross_ref, pair_ref, k, rows):
    even = lax.axis_index("gy") % 2 == 0
    cross_ref[k, rows, :] = jnp.where(even, west, east)
    pair_ref[k, rows, :] = jnp.where(even, east, west)


def layout_kernel(source, guess, weight, own_source, own_guess, own_weight, cross_ref, pair_ref, *inner):
    rows = source.shape[0]
    piece = cross_ref.shape[1]
    tail = rows - (PIECES - 1) * piece
    for k, (block, own) in enumerate(zip((source, guess, weight), (own_source, own_guess, own_weight))):
        clear_rim(own)
        sides = []
        for t in range(2):
            own[t, GUARD + TOP : GUARD + TOP + rows, :] = block[:, t * LANES : (t + 1) * LANES]
        for tile, first in ((0, 0), (1, LANES - HALO)):
            columns = slice(tile * LANES, (tile + 1) * LANES)
            last = roll(block[(PIECES - 1) * piece :, columns], (PIECES - 1) * HALO - first)
            packed = jnp.concatenate((last, jnp.zeros((piece - tail, LANES), jnp.float32)), axis=0)
            for p in range(PIECES - 1):
                part = block[p * piece : (p + 1) * piece, columns]
                packed = jnp.where(lane_of(part) // HALO == p, roll(part, p * HALO - first), packed)
            sides.append(packed)
        to_sides(*sides, cross_ref, pair_ref, k, slice(0, piece))
    weights, start, height = (own_weight, *inner), TOP, rows
    for level in range(LEVELS):
        pooled = [0.125 * w for w in pool_rows(weights[level], start, height, 2**level)]
        start, height = start // 2, height // 2
        if level < LEVELS - 1:
            store(weights[level + 1], start, height, pooled)
    lane = lane_of(pooled[0])
    free = PIECES * HALO
    index = jnp.clip(lane - free, 0, LANES - 1 - free) * 2**LEVELS
    for t in range(2):
        taken = jnp.take_along_axis(pooled[t], index, axis=1)
        span = slice(t * height, (t + 1) * height)
        for ref in (cross_ref, pair_ref):
            ref[0, span, :] = jnp.where(lane >= free, taken, ref[0, span, :])


def halo_kernel(*refs):
    first_rows, second_rows, *own, cross_ref, pair_ref = refs[5:]
    total = own[0].shape[1] - 2 * GUARD
    piece = cross_ref.shape[1]
    even = lax.axis_index("gx") % 2 == 0
    shift = (PIECES - 1) * HALO
    for k in range(3):
        above = jnp.where(even, first_rows[k], second_rows[k])
        below = jnp.where(even, second_rows[k], first_rows[k])
        for rows, row, first in ((above, TOP - HALO, piece - 2 * HALO), (below, total - TOP, piece - HALO)):
            body = [rows[:, t * LANES : (t + 1) * LANES] for t in range(2)]
            for t in range(2):
                own[k][t, GUARD + row : GUARD + row + HALO, :] = body[t]
            span = slice(first, first + HALO)
            here = lane_of(body[0]) // HALO == PIECES - 1
            cross, pair = cross_ref[k, span, :], pair_ref[k, span, :]
            west, east = roll(body[0], shift), roll(body[1], shift + HALO - LANES)
            even_y = lax.axis_index("gy") % 2 == 0
            cross_ref[k, span, :] = jnp.where(here, jnp.where(even_y, west, east), cross)
            pair_ref[k, span, :] = jnp.where(here, jnp.where(even_y, east, west), pair)


def body_kernel(source, guess, weight, *refs):
    states = refs[: 4 * (LEVELS - 1)]
    last_weight, last_source, first_diagonal, *refs = refs[4 * (LEVELS - 1) :]
    frames, (field, resid, weight_in, *inner) = refs[:3], refs[3:]
    rows = source.shape[1] - 2 * GUARD
    depth = LEVELS - 2
    weights = (weight_in, *inner[:depth], last_weight)
    sources = (source, *inner[depth : 2 * depth], last_source)
    diagonal = (first_diagonal, *inner[2 * depth :])
    weights[0][...] = weight[...]
    descend_all(rows, sources, guess, weights, states, diagonal, field, resid, 144, 144)
    for own, frame in zip((source, guess, weight), frames):
        tiles = [own[t] for t in range(2)]
        frame[0] = jnp.where(lane_of(tiles[0]) < LANES // 2, roll(tiles[0], HALO), roll(tiles[1], -HALO))


def frame_kernel(_a, _b, _c, from_cross, from_pair, body_weight, body_source, *refs):
    even = lax.axis_index("gy") % 2 == 0
    frames, states, refs = refs[:3], refs[3 : 3 + 4 * (LEVELS - 1)], refs[3 + 4 * (LEVELS - 1) :]
    frame_source, frame_guess, frame_weight = frames
    first_diagonal, ring_state, dense_ref, chunks_ref, field, resid, *refs = refs[0], refs[1:5], *refs[5:]
    ring_weight, ring_source, ring_field, ring_resid, ring_diagonal, *inner = refs
    rows = frame_source.shape[1] - 2 * GUARD
    depth = LEVELS - 1
    weights = (frame_weight, *inner[:depth])
    sources = (frame_source, *inner[depth : 2 * depth])
    diagonals = (first_diagonal, *inner[2 * depth :])
    piece = from_cross.shape[1]
    for k, frame in enumerate(frames):
        left = jnp.where(even, from_cross[k], from_pair[k])
        right = jnp.where(even, from_pair[k], from_cross[k])
        spans = [(p, 0, TOP + p * piece, piece) for p in range(PIECES - 1)]
        spans.append((PIECES - 1, 0, TOP + (PIECES - 1) * piece, piece - 2 * HALO))
        spans += [(PIECES - 1, piece - 2 * HALO, TOP - HALO, HALO), (PIECES - 1, piece - HALO, rows - TOP, HALO)]
        for p, first, start, size in spans:
            span = slice(GUARD + start, GUARD + start + size)
            west = roll(left[first : first + size], -p * HALO)
            east = roll(right[first : first + size], -(p + 1) * HALO)
            lane = lane_of(west)
            inside = jnp.where(lane < HALO, west, frame[0, span, :])
            frame[0, span, :] = jnp.where(lane >= LANES - HALO, east, inside)
    descend_all(rows, sources, frame_guess, weights, states, diagonals, field, resid, 288, 288)

    level = LEVELS - 1
    step, halo, height = 2**level, TOP >> level, rows >> level
    for body, frame, ring in (
        (body_weight, weights[level], ring_weight),
        (body_source, sources[level], ring_source),
    ):
        middle = load(body, 0, height)
        around = load(frame, 0, height)[0]
        lane = lane_of(around)
        ahead, back = roll(around, HALO), roll(around, -HALO)
        store(
            ring,
            0,
            height,
            [
                jnp.where(lane < 2 * step, back, middle[0]),
                jnp.where(lane >= LANES - 2 * step, ahead, middle[1]),
                jnp.where(lane < LANES // 2, ahead, back),
            ],
        )
    descend(
        level,
        height,
        ring_weight,
        ring_source,
        None,
        ring_state,
        ring_diagonal,
        ring_field,
        ring_resid,
        None,
        None,
        height,
        height,
    )

    coarse_rows = (height - 2 * halo) // 2
    dense = jnp.zeros((8, LANES), jnp.float32)
    lane = lane_of(dense)
    per_tile = LANES // 2**LEVELS
    pooled_b = pool_rows(ring_resid, halo, 2 * coarse_rows, step)
    pooled_w = pool_rows(ring_weight, halo, 2 * coarse_rows, step)
    index = (lane % per_tile) * 2**LEVELS
    place = lane // per_tile
    for g in range(coarse_rows // 8):
        for group, (values, factor) in enumerate(((pooled_b, 0.25), (pooled_w, 0.125))):
            for t in range(2):
                taken = jnp.take_along_axis(factor * values[t][8 * g : 8 * g + 8], index, axis=1)
                dense = jnp.where(place == 4 * g + 2 * group + t, taken, dense)
    dense_ref[...] = dense

    index = jnp.minimum(2 * (lane - lane % (2 * per_tile)) + lane % (2 * per_tile), LANES - 1)
    level_with, above, below = (fold(x) for x in (jnp.take_along_axis(dense, index, axis=1), dense, roll(dense, -LANES // 2)))
    x = lax.axis_index("gx")
    for i in range(chunks_ref.shape[0]):
        chunk = jnp.where(i == x, level_with, jnp.where(i < x, above, below))
        chunks_ref[i] = jnp.broadcast_to(chunk[None], chunks_ref.shape[1:])


def fold(x):
    return jnp.where(lane_of(x) < LANES // 2, x, pltpu.roll(roll(x, LANES // 2), 4, 0))[:4]


def unfold(x):
    return jnp.concatenate((x, roll(x, LANES // 2)), axis=0)


def coarse_solve(all_ref, dense_ref, from_cross, from_pair, e_ref, width, groups):
    x, nx = lax.axis_index("gx"), lax.axis_size("gx")
    y, ny = lax.axis_index("gy"), lax.axis_size("gy")
    tiles = {}
    for dx in (-1, 0, 1):
        for dy in (-1, 0, 1):
            if dx or dy:
                inside = (x + dx >= 0) & (x + dx < nx) & (y + dy >= 0) & (y + dy < ny)
                tile = unfold(all_ref[jnp.where(inside, x + dx, 0), jnp.where(inside, y + dy, 0)])
                tiles[dx, dy] = jnp.where(inside, tile, 0.0)
    dense = dense_ref[...]
    lane = lane_of(dense)
    even = y % 2 == 0
    height = 8 * groups
    cross, pair = from_cross[0, : 2 * height, :], from_pair[0, : 2 * height, :]
    weights = {-1: jnp.where(even, cross, pair), 1: jnp.where(even, pair, cross)}
    bands = [(-1, g) for g in range(TALL // 8)] + [(0, g) for g in range(groups)] + [(1, g) for g in range(TALL // 8)]
    b, w = [], []
    for dx, g in bands:
        b_rows = w_rows = jnp.zeros_like(dense)
        for dy in (-1, 0, 1):
            first = (dy + 1) * width
            here = (lane >= first) & (lane < first + width)
            if dx or not dy:
                tile = tiles[dx, dy] if dx else dense
                b_part, w_part = roll(tile, first - 2 * g * width), roll(tile, first - (2 * g + 1) * width)
            else:
                b_part = roll(tiles[dx, dy], first - g * width)
                free = PIECES * HALO
                parts = [weights[dy][t * height + 8 * g : t * height + 8 * g + 8] for t in range(2)]
                parts = [roll(part, first + t * width // 2 - free) for t, part in enumerate(parts)]
                w_part = jnp.where(lane < first + width // 2, *parts)
            b_rows = jnp.where(here, b_part, b_rows)
            w_rows = jnp.where(here, w_part, w_rows)
        b.append(b_rows)
        w.append(w_rows)
    b, w = jnp.concatenate(b, axis=0), jnp.concatenate(w, axis=0)

    rows = b.shape[0]
    zeros = jnp.zeros((GUARD, LANES), jnp.float32)
    e_ref[0:GUARD, :] = zeros
    e_ref[GUARD + rows :, :] = zeros

    def shifted(by):
        return e_ref[GUARD + by : GUARD + by + rows, :]

    e_ref[GUARD : GUARD + rows, :] = w
    c_west = jnp.minimum(w, roll(w, 1))
    c_north, c_south = jnp.minimum(w, shifted(-1)), jnp.minimum(w, shifted(1))
    c_east = roll(c_west, -1)
    scale = relaxation / (damping + c_north + c_south + c_west + c_east)
    first = scale * b
    c_west, c_east, c_north, c_south = (scale * c for c in (c_west, c_east, c_north, c_south))
    e_ref[GUARD : GUARD + rows, :] = first

    def sweep(_, carry):
        e = shifted(0)
        around = (c_west * roll(e, 1) + c_east * roll(e, -1)) + (c_north * shifted(-1) + c_south * shifted(1))
        e_ref[GUARD : GUARD + rows, :] = ((1.0 - relaxation) * e + first) + around
        return carry

    lax.fori_loop(0, SWEEPS - 1, sweep, 0)
    return shifted(0)


def up_kernel(all_ref, dense_ref, from_cross, from_pair, own_source, frame_source, own_diagonal, frame_diagonal, *refs):
    count = 4 * (LEVELS - 1)
    body_state, frame_state, ring_state = refs[:count], refs[count : 2 * count], refs[2 * count : 2 * count + 4]
    out_ref, resid_ref = refs[2 * count + 4 : 2 * count + 6]
    ring_pe, body_final, frame_final, sems, e_ref, *inner = refs[2 * count + 6 :]
    outs, inner = inner[:2], inner[2:]
    body_pe, frame_pe = inner[: LEVELS - 1], inner[LEVELS - 1 :]
    rows = out_ref.shape[0] + 2 * TOP
    width = out_ref.shape[1] >> LEVELS
    e = coarse_solve(all_ref, dense_ref, from_cross, from_pair, e_ref, width, (out_ref.shape[0] >> LEVELS) // 8)

    level = LEVELS - 1
    step, halo, height = 2**level, TOP >> level, rows >> level
    coarse_rows = (height - 2 * halo) // 2
    picked = e[TALL - 8 : TALL + coarse_rows + 8]
    lane = lane_of(picked)
    for t in range(3):
        group = (lane + t * LANES) // 2**LEVELS
        if t == 2:
            group = jnp.where(lane < LANES // 2, group, group - 3 * LANES // 2**LEVELS)
        taken = jnp.take_along_axis(picked, jnp.clip(group + width, 0, LANES - 1), axis=1)[7 : 7 + coarse_rows + 2]
        ring_pe[t, 0 : 2 * GUARD, :] = jnp.zeros((2 * GUARD, LANES), jnp.float32)
        ring_pe[t, height : height + 2 * GUARD, :] = jnp.zeros((2 * GUARD, LANES), jnp.float32)
        ring_pe[t, pl.ds(GUARD + halo - 2, coarse_rows + 2, stride=2), :] = taken
        ring_pe[t, pl.ds(GUARD + halo - 1, coarse_rows + 2, stride=2), :] = taken

    def climbed(pe, state, start, size, step):
        mid, around = beside_of(pe, state[:2], start, size, step)
        scale, smooth = load(state[2], start, size), load(state[3], start, size)
        return [(smooth[t] + (1.0 - relaxation) * mid[t]) + scale[t] * around[t] for t in range(len(mid))]

    def climb_ring(start, size, level=level, step=step):
        ring = spread(climbed(ring_pe, ring_state, start, size, step), step // 2)
        lane = lane_of(ring[0])
        around = jnp.where(
            lane < LANES // 2,
            jnp.where(lane < HALO, roll(ring[2], HALO), roll(ring[0], HALO)),
            jnp.where(lane < LANES - HALO, roll(ring[1], -HALO), roll(ring[2], -HALO)),
        )
        store_twice(body_pe[level - 1], start, size, ring[:2])
        store_twice(frame_pe[level - 1], start, size, [around])

    for_chunks(height, climb_ring, height, 16)

    for level in range(LEVELS - 2, -1, -1):
        step, height = 2**level, rows >> level
        groups = ((body_pe, body_state, body_final), (frame_pe, frame_state, frame_final))
        for pes, _, _ in groups:
            clear_guards(pes[level], height)

        def climb(start, size, level=level, step=step, groups=groups):
            for pes, states, final in groups:
                value = climbed(pes[level], states[4 * level : 4 * level + 4], start, size, step)
                if level == 0:
                    store(final, start, size, value)
                else:
                    store_twice(pes[level - 1], start, size, spread(value, step // 2))

        for_chunks(height, climb, 144, 72)

    def last(start, size):
        base = start + TOP
        body, around = beside_of(body_final, body_state[:2], base, size, 1)
        frame, frame_around = beside_of(frame_final, frame_state[:2], base, size, 1)
        b, d = load(own_source, base, size), load(own_diagonal, base, size)
        b_frame, d_frame = load(frame_source, base, size), load(frame_diagonal, base, size)
        body = (body, [(b[t] + around[t]) - d[t] * body[t] for t in range(2)])
        frame = (frame[0], (b_frame[0] + frame_around[0]) - d_frame[0] * frame[0])
        lane = lane_of(frame[0])
        near = HALO - 4
        span = pl.ds(start, size)
        for ref, middle, around in ((outs[0], body[0], frame[0]), (outs[1], body[1], frame[1])):
            ref[span, :LANES] = jnp.where(lane < near, roll(around, -HALO), middle[0])
            ref[span, LANES:] = jnp.where(lane >= LANES - near, roll(around, HALO), middle[1])

    parts = sems.shape[0] // 2
    size = out_ref.shape[0] // parts

    def copies(p):
        span = pl.ds(p * size, size)
        return [
            pltpu.make_async_copy(outs[k].at[span], ref.at[span], sems.at[2 * p + k])
            for k, ref in enumerate((out_ref, resid_ref))
        ]

    def finish(p, carry):
        for_parts(p * size, size, last, 16)
        for copy in copies(p):
            copy.start()
        return carry

    lax.fori_loop(0, parts, finish, 0)
    for p in range(parts):
        for copy in copies(p):
            copy.wait()


def call(kernel, out_shape, scratch, flops, moved, **more):
    return pl.pallas_call(
        kernel,
        out_shape=out_shape,
        scratch_shapes=scratch,
        compiler_params=pltpu.CompilerParams(vmem_limit_bytes=VMEM_LIMIT),
        cost_estimate=pl.CostEstimate(flops=flops, bytes_accessed=moved, transcendentals=0),
        **more,
    )


def swap(x, axis, first):
    pairs = [(i, i + 1) for i in range(first, lax.axis_size(axis) - 1, 2)]
    return lax.ppermute(x, axis, pairs + [(j, i) for i, j in pairs])


def local(rhs, pressure, wet_mask, bathy_class):
    rows, columns = rhs.shape
    cells = rows * columns
    total = rows + 2 * TOP
    levels = range(LEVELS - 1)

    def shape(tiles, level):
        return (tiles, (total >> level) + 2 * GUARD, LANES)

    def out(*dims):
        return jax.ShapeDtypeStruct(dims, jnp.float32)

    def vmem(tiles, level):
        return pltpu.VMEM(shape(tiles, level), jnp.float32)

    def fields(r, p, m, c):
        wet = m.astype(jnp.float32)
        return wet * r, wet * p, wet * (1.0 + 0.5 * c.astype(jnp.float32))

    given = (rhs, pressure, wet_mask, bathy_class)

    def edge(start):
        return jnp.stack(fields(*(lax.dynamic_slice_in_dim(x, start, HALO, axis=0) for x in given)))

    even = lax.axis_index("gx") % 2 == 0
    first_rows = swap(edge(jnp.where(even, 0, rows - HALO)), "gx", 1)
    second_rows = swap(edge(jnp.where(even, rows - HALO, 0)), "gx", 0)
    piece = (rows + 2 * HALO) // PIECES
    own_shapes = [out(*shape(2, 0))] * 3
    laid_out = [*own_shapes, out(3, piece, LANES), out(3, piece, LANES)]
    inner = [vmem(2, level) for level in range(1, LEVELS)]
    begun = call(layout_kernel, laid_out, inner, 10 * cells, 10 * cells)(*fields(*given))
    *own, to_cross, to_pair = call(
        halo_kernel, laid_out, (), cells, cells, input_output_aliases={k: k for k in range(5)}
    )(*begun, first_rows, second_rows)
    from_cross = swap(to_cross, "gy", 1)
    from_pair = swap(to_pair, "gy", 0)

    state_count = 4 * (LEVELS - 1)
    *body_state, body_weight, body_source, diagonal, frame_source, frame_guess, frame_weight = call(
        body_kernel,
        [out(*shape(2, level)) for level in levels for _ in range(4)]
        + [out(*shape(2, LEVELS - 1))] * 2
        + [out(*shape(2, 0))]
        + [out(*shape(1, 0))] * 3,
        [vmem(2, 0)] * 3 + [vmem(2, level) for level in levels[1:]] * 3,
        100 * cells,
        40 * cells,
    )(*own)
    nx, ny = lax.axis_size("gx"), lax.axis_size("gy")
    ring = LEVELS - 1
    frame_source, _, _, *state, dense, chunks = call(
        frame_kernel,
        [out(*shape(1, 0))] * 3
        + [out(*shape(1, level)) for level in levels for _ in range(4)]
        + [out(*shape(1, 0))]
        + [out(*shape(3, ring))] * 4
        + [out(8, LANES), out(nx, ny, 4, LANES)],
        [vmem(1, 0)] * 2 + [vmem(3, ring)] * 5 + [vmem(1, level) for level in range(1, LEVELS)] * 3,
        50 * cells,
        20 * cells,
        input_output_aliases={k: k for k in range(3)},
    )(frame_source, frame_guess, frame_weight, from_cross, from_pair, body_weight, body_source)
    frame_state, frame_diagonal, ring_state = state[:state_count], state[state_count], state[state_count + 1 :]
    gathered = lax.all_to_all(chunks.reshape(nx * ny, 4, LANES), ("gx", "gy"), 0, 0).reshape(chunks.shape)
    return call(
        up_kernel,
        (out(rows, columns), out(rows, columns)),
        [vmem(3, ring), vmem(2, 0), vmem(1, 0), pltpu.SemaphoreType.DMA((8,))]
        + [pltpu.VMEM(((rows >> LEVELS) + 2 * TALL + 2 * GUARD, LANES), jnp.float32)]
        + [pltpu.VMEM((rows, columns), jnp.float32)] * 2
        + [vmem(2, level) for level in levels]
        + [vmem(1, level) for level in levels],
        60 * cells,
        40 * cells,
        out_specs=[pl.BlockSpec(memory_space=pl.ANY)] * 2,
    )(gathered, dense, from_cross, from_pair, own[0], frame_source, diagonal, frame_diagonal, *body_state, *frame_state, *ring_state)


def solution(mesh):
    placed = (P("gx", "gy"), P("gx", "gy"), P("gx", "gy"), P("gx", "gy"))
    return jax.shard_map(
        local, mesh=mesh, in_specs=placed, out_specs=(P("gx", "gy"), P("gx", "gy")), check_vma=False
    )
```

profile of v0, /device:TPU:0, one launch (start us, length us, event | category | flops | bytes accessed | tf_op | source)
XLA Modules:
  0.0 38.6 jit_solution(8744882462747268569)
XLA Ops:
  0.6 0.0 copy-start
  0.7 0.9 %multiply_bitcast_fusion.2 = (f32[1,24,256]{2,1,0:T(8,128)S(1)}, f32[1,24,256]{2,1,0:T(8,128)S(1)}, f32[1,24,256]{2,1,0:T(8,128)S(1)}, f32[1,24,256]{2,1,0:T(8,1...) fusion(f32[512,256]{1,0:T(8,128)} %param.4, s32[]{:T(128)S(6)} %select_n.24, s32[512,256]{1,0:T(8,128)} %param.6, ...), kind=kLoop, calls=%fused_computation.7 | loop fusion | flops 86016 | bytes 344072 | tf_op jit(solution)/shard_map/stack | solution.py:566
  1.6 0.7 %collective-permute-start = (f32[3,24,256]{2,1,0:T(8,128)S(1)}, f32[3,24,256]{2,1,0:T(8,128)S(1)}, u32[]{:S(2)}, u32[]{:S(2)}) collective-permute-start(f32[3,24,256]{2,1,0:T(8,128)S(1)} %pad_maximum_fusion), channel_id=1, source_target_pairs={{8,16},{16,8},{9,17},{17,9},{10,18},{18,10},{11,19},{19,11},{12,20... | collective-permute-start | bytes 221192 | tf_op jit(solution)/shard_map/ppermute | solution.py:541
  2.3 5.9 %collective-permute-start.1 = (f32[3,24,256]{2,1,0:T(8,128)S(1)}, f32[3,24,256]{2,1,0:T(8,128)S(1)}, u32[]{:S(2)}, u32[]{:S(2)}) collective-permute-start(f32[3,24,256]{2,1,0:T(8,128)S(1)} %pad_maximum_fusion.1), channel_id=1, source_target_pairs={{0,8},{16,24},{8,0},{24,16},{1,9},{17,25},{9,1},{25,17},{2,10},{18... | collective-permute-start | bytes 221192 | tf_op jit(solution)/shard_map/ppermute | solution.py:541
  8.2 0.0 copy-done
  8.2 1.5 %add_multiply_fusion = (f32[512,256]{1,0:T(8,128)S(1)}, f32[512,256]{1,0:T(8,128)S(1)}, f32[512,256]{1,0:T(8,128)S(1)}) fusion(s32[512,256]{1,0:T(8,128)S(1)} %copy-done, s32[512,256]{1,0:T(8,128)} %param.6, f32[512,256]{1,0:T(8,128)} %param.5, f32[512,256]{1,0:T(8,128)} %param.4), kind=kLoop, calls=%fused_computation | loop fusion | flops 917504 | bytes 3670016 | tf_op jit(solution)/shard_map/mul | solution.py:561
  9.7 0.8 %shard_map.59 = (f32[2,592,128]{2,1,0:T(8,128)S(1)}, f32[2,592,128]{2,1,0:T(8,128)S(1)}, f32[2,592,128]{2,1,0:T(8,128)S(1)}, f32[3,112,128]{2,1,0:T(8,128)S(1)}, f32[3,112,128]{2,1,0:T(8,128)S(1)}) custom-call(f32[512,256]{1,0:T(8,128)S(1)} %get-tuple-element.110.source, f32[512,256]{1,0:T(8,128)S(1)} %get-tuple-element.109.guess, ...), custom_call_target="tpu_custom_call" | custom-call | flops 1310720 | bytes 1310720 | tf_op jit(solution)/shard_map/pallas_call | solution.py:575
  10.5 0.0 collective-permute-done.refs_5_
  10.6 0.0 collective-permute-done.1.refs_6_
  10.6 0.1 shard_map.60
  10.7 0.7 %collective-permute-start.2 = (f32[3,112,128]{2,1,0:T(8,128)S(1)}, f32[3,112,128]{2,1,0:T(8,128)S(1)}, u32[]{:S(2)}, u32[]{:S(2)}) collective-permute-start(f32[3,112,128]{2,1,0:T(8,128)S(1)} %get-tuple-element.61), channel_id=1, source_target_pairs={{1,2},{3,4},{5,6},{2,1},{4,3},{6,5},{9,10},{11,12},{13,14},{10,9},... | collective-permute-start | bytes 516104 | tf_op jit(solution)/shard_map/ppermute | solution.py:541
  11.4 2.9 %collective-permute-start.3 = (f32[3,112,128]{2,1,0:T(8,128)S(1)}, f32[3,112,128]{2,1,0:T(8,128)S(1)}, u32[]{:S(2)}, u32[]{:S(2)}) collective-permute-start(f32[3,112,128]{2,1,0:T(8,128)S(1)} %get-tuple-element.62), channel_id=1, source_target_pairs={{0,1},{2,3},{4,5},{6,7},{1,0},{3,2},{5,4},{7,6},{8,9},{10,11},{12,... | collective-permute-start | bytes 516104 | tf_op jit(solution)/shard_map/ppermute | solution.py:541
  14.3 4.6 %shard_map.61 = (f32[2,592,128]{2,1,0:T(8,128)S(1)}, f32[2,592,128]{2,1,0:T(8,128)S(1)}, f32[2,592,128]{2,1,0:T(8,128)S(1)}, f32[2,592,128]{2,1,0:T(8,128)S(1)},...) custom-call(f32[2,592,128]{2,1,0:T(8,128)S(1)} %get-tuple-element.55, ...), custom_call_target="tpu_custom_call" | custom-call | flops 13107200 | bytes 5242880 | tf_op jit(solution)/shard_map/pallas_call | solution.py:583
  18.9 0.0 collective-permute-done.2.from_cross
  18.9 0.0 collective-permute-done.3.from_pair
  18.9 2.9 %shard_map.62 = (f32[1,592,128]{2,1,0:T(8,128)S(1)}, f32[1,592,128]{2,1,0:T(8,128)S(1)}, f32[1,592,128]{2,1,0:T(8,128)S(1)}, f32[1,592,128]{2,1,0:T(8,128)S(1)},...) custom-call(f32[1,592,128]{2,1,0:T(8,128)S(1)} %get-tuple-element.58, ...), custom_call_target="tpu_custom_call", output_to_operand_aliasing={{0}: (0, {}), {1}: (1, {}), {2}: (2, {})} | custom-call | flops 6553600 | bytes 2621440 | tf_op jit(solution)/shard_map/pallas_call | solution.py:595
  21.9 10.9 %all_to_all.5 = f32[32,4,128]{2,1,0:T(4,128)S(1)} all-to-all(f32[32,4,128]{2,1,0:T(4,128)S(1)} %bitcast.15), channel_id=1, replica_groups=mesh['gx'=4,'gy'=8] {'gx','gy'}, dimensions={0} | all-to-all | bytes 131072 | tf_op jit(solution)/shard_map/all_to_all | solution.py:608
  32.7 5.8 %shard_map.63 = (f32[512,256]{1,0:T(8,128)}, f32[512,256]{1,0:T(8,128)}) custom-call(f32[4,8,4,128]{3,2,1,0:T(4,128)S(1)} %bitcast.14, f32[8,128]{1,0:T(8,128)S(1)} %get-tuple-element.66.dense_ref, f32[3,112,128]{2,1,0:T(8,128)S(1)} %collective-permute-done.2.from_cross, f32[3,112,128]{2,1,0:T(8,128)S(1)} %collective-permute-done.3.from_pair, ...), custom_call_target="tpu_custom_call" | custom-call | flops 7864320 | bytes 5242880 | tf_op jit(solution)/shard_map/pallas_call | solution.py:609
  (2 shorter events, 0.0 us)
Async XLA Ops:
  0.6 7.6 %copy-start = (s32[512,256]{1,0:T(8,128)S(1)}, s32[512,256]{1,0:T(8,128)}, u32[]{:S(2)}) copy-start(s32[512,256]{1,0:T(8,128)} %param.7) | copy-start | bytes 1572868
  1.6 8.9 %collective-permute-start = (f32[3,24,256]{2,1,0:T(8,128)S(1)}, f32[3,24,256]{2,1,0:T(8,128)S(1)}, u32[]{:S(2)}, u32[]{:S(2)}) collective-permute-start(f32[3,24,256]{2,1,0:T(8,128)S(1)} %pad_maximum_fusion), channel_id=1, source_target_pairs={{8,16},{16,8},{9,17},{17,9},{10,18},{18,10},{11,19},{19,11},{12,20... | collective-permute-start | bytes 221192 | tf_op jit(solution)/shard_map/ppermute | solution.py:541
  2.3 8.3 %collective-permute-start.1 = (f32[3,24,256]{2,1,0:T(8,128)S(1)}, f32[3,24,256]{2,1,0:T(8,128)S(1)}, u32[]{:S(2)}, u32[]{:S(2)}) collective-permute-start(f32[3,24,256]{2,1,0:T(8,128)S(1)} %pad_maximum_fusion.1), channel_id=1, source_target_pairs={{0,8},{16,24},{8,0},{24,16},{1,9},{17,25},{9,1},{25,17},{2,10},{18... | collective-permute-start | bytes 221192 | tf_op jit(solution)/shard_map/ppermute | solution.py:541
  10.7 8.2 %collective-permute-start.2 = (f32[3,112,128]{2,1,0:T(8,128)S(1)}, f32[3,112,128]{2,1,0:T(8,128)S(1)}, u32[]{:S(2)}, u32[]{:S(2)}) collective-permute-start(f32[3,112,128]{2,1,0:T(8,128)S(1)} %get-tuple-element.61), channel_id=1, source_target_pairs={{1,2},{3,4},{5,6},{2,1},{4,3},{6,5},{9,10},{11,12},{13,14},{10,9},... | collective-permute-start | bytes 516104 | tf_op jit(solution)/shard_map/ppermute | solution.py:541
  11.4 7.5 %collective-permute-start.3 = (f32[3,112,128]{2,1,0:T(8,128)S(1)}, f32[3,112,128]{2,1,0:T(8,128)S(1)}, u32[]{:S(2)}, u32[]{:S(2)}) collective-permute-start(f32[3,112,128]{2,1,0:T(8,128)S(1)} %get-tuple-element.62), channel_id=1, source_target_pairs={{0,1},{2,3},{4,5},{6,7},{1,0},{3,2},{5,4},{7,6},{8,9},{10,11},{12,... | collective-permute-start | bytes 516104 | tf_op jit(solution)/shard_map/ppermute | solution.py:541
where the time goes:
time: 38.8 us; the launch traced here: 38.6 us
  Pallas kernels  14.3 us (37%)
  blocking collectives  10.9 us (28%)
  starting transfers between devices  10.2 us (26%)
  other arithmetic  2.46 us (6%)
  between operations  0.76 us (2%)
    all_to_all x1, blocking collectives, local(): lax.all_to_all(chunks.reshape(nx * ny, 4, LANES), ('gx', 'gy'), 0, 0)  10.9 us
    ppermute x4, starting transfers between devices, swap(): return lax.ppermute(x, axis, pairs + [(j, i) for i, j in pairs])  10.2 us
    pallas_call x1, Pallas kernels, local(): call(up_kernel, (out(rows, columns), out(rows, columns)), [vmem(3, ring),...  5.84 us
    pallas_call x1, Pallas kernels, local(): call(body_kernel, [out(*shape(2, level)) for level in levels for _ in ran...  4.61 us
    pallas_call x1, Pallas kernels, local(): call(frame_kernel, [out(*shape(1, 0))] * 3 + [out(*shape(1, level)) for l...  2.93 us
    mul x1, other arithmetic, fields(): return (wet * r, wet * p, wet * (1.0 + 0.5 * c.astype(jnp.float32)))  1.51 us
    another operation x3, other arithmetic, edge(): jnp.stack(fields(*(lax.dynamic_slice_in_dim(x, start, HALO, axis=0) for x...  0.95 us
    pallas_call x1, Pallas kernels, local(): call(layout_kernel, laid_out, inner, 10 * cells, 10 * cells)  0.8 us
  transfers between devices with their start and end apart: 4, of which 0 were waited for; matrix products, arithmetic and copies ran while one was open for 4% of the time, Pallas kernels for 14%

commit v1 on v0

--- a/solution.py
+++ b/solution.py
@@ -17,6 +17,8 @@
 TOP = 32
 GUARD = 8
 PIECES = 5
+CHUNK = 144
+LAG = 8
 TALL = 16
 VMEM_LIMIT = 40 * 1024 * 1024
 
@@ -486,10 +488,10 @@
                 else:
                     store_twice(pes[level - 1], start, size, spread(value, step // 2))
 
-        for_chunks(height, climb, 144, 72)
-
-    def last(start, size):
-        base = start + TOP
+        if level > 0:
+            for_chunks(height, climb, CHUNK, CHUNK // 2)
+
+    def last(base, size):
         body, around = beside_of(body_final, body_state[:2], base, size, 1)
         frame, frame_around = beside_of(frame_final, frame_state[:2], base, size, 1)
         b, d = load(own_source, base, size), load(own_diagonal, base, size)
@@ -498,29 +500,38 @@
         frame = (frame[0], (b_frame[0] + frame_around[0]) - d_frame[0] * frame[0])
         lane = lane_of(frame[0])
         near = HALO - 4
-        span = pl.ds(start, size)
+        span = pl.ds(base, size)
         for ref, middle, around in ((outs[0], body[0], frame[0]), (outs[1], body[1], frame[1])):
             ref[span, :LANES] = jnp.where(lane < near, roll(around, -HALO), middle[0])
             ref[span, LANES:] = jnp.where(lane >= LANES - near, roll(around, HALO), middle[1])
 
-    parts = sems.shape[0] // 2
-    size = out_ref.shape[0] // parts
+    count = rows // CHUNK
+    ends = [0] + [CHUNK * (p + 1) - LAG - TOP for p in range(count - 1)] + [out_ref.shape[0]]
 
     def copies(p):
-        span = pl.ds(p * size, size)
+        size = ends[p + 1] - ends[p]
         return [
-            pltpu.make_async_copy(outs[k].at[span], ref.at[span], sems.at[2 * p + k])
+            pltpu.make_async_copy(
+                outs[k].at[pl.ds(TOP + ends[p], size)], ref.at[pl.ds(ends[p], size)], sems.at[2 * p + k]
+            )
             for k, ref in enumerate((out_ref, resid_ref))
         ]
 
-    def finish(p, carry):
-        for_parts(p * size, size, last, 16)
-        for copy in copies(p):
-            copy.start()
+    def finish(i, carry):
+        for_parts(i * CHUNK, CHUNK, climb, CHUNK // 2)
+        base = pl.multiple_of(jnp.maximum(i * CHUNK - LAG, 0), 8)
+        for_parts(base, CHUNK, last, CHUNK // 2)
+        for p in range(count):
+
+            @pl.when(i == p)
+            def _(p=p):
+                for copy in copies(p):
+                    copy.start()
+
         return carry
 
-    lax.fori_loop(0, parts, finish, 0)
-    for p in range(parts):
+    lax.fori_loop(0, count, finish, 0)
+    for p in range(count):
         for copy in copies(p):
             copy.wait()
 
@@ -576,8 +587,8 @@
     *own, to_cross, to_pair = call(
         halo_kernel, laid_out, (), cells, cells, input_output_aliases={k: k for k in range(5)}
     )(*begun, first_rows, second_rows)
+    from_pair = swap(to_pair, "gy", 0)
     from_cross = swap(to_cross, "gy", 1)
-    from_pair = swap(to_pair, "gy", 0)
 
     state_count = 4 * (LEVELS - 1)
     *body_state, body_weight, body_source, diagonal, frame_source, frame_guess, frame_weight = call(
@@ -611,7 +622,7 @@
         (out(rows, columns), out(rows, columns)),
         [vmem(3, ring), vmem(2, 0), vmem(1, 0), pltpu.SemaphoreType.DMA((8,))]
         + [pltpu.VMEM(((rows >> LEVELS) + 2 * TALL + 2 * GUARD, LANES), jnp.float32)]
-        + [pltpu.VMEM((rows, columns), jnp.float32)] * 2
+        + [pltpu.VMEM((total, columns), jnp.float32)] * 2
         + [vmem(2, level) for level in levels]
         + [vmem(1, level) for level in levels],
         60 * cells,

time: 38.8 us -> 38.7 us (level)
  no operation moved by 1% of the time
where the time goes in v1:
time: 38.7 us; the launch traced here: 38.5 us
  Pallas kernels  14.3 us (37%)
  blocking collectives  10.9 us (28%)
  starting transfers between devices  10.2 us (26%)
  other arithmetic  2.46 us (6%)
  between operations  0.76 us (2%)
    all_to_all x1, blocking collectives, local(): lax.all_to_all(chunks.reshape(nx * ny, 4, LANES), ('gx', 'gy'), 0, 0)  10.9 us
    ppermute x4, starting transfers between devices, swap(): return lax.ppermute(x, axis, pairs + [(j, i) for i, j in pairs])  10.2 us
    pallas_call x1, Pallas kernels, local(): call(up_kernel, (out(rows, columns), out(rows, columns)), [vmem(3, ring),...  5.78 us
    pallas_call x1, Pallas kernels, local(): call(body_kernel, [out(*shape(2, level)) for level in levels for _ in ran...  4.61 us
    pallas_call x1, Pallas kernels, local(): call(frame_kernel, [out(*shape(1, 0))] * 3 + [out(*shape(1, level)) for l...  2.93 us
    mul x1, other arithmetic, fields(): return (wet * r, wet * p, wet * (1.0 + 0.5 * c.astype(jnp.float32)))  1.51 us
    another operation x3, other arithmetic, edge(): jnp.stack(fields(*(lax.dynamic_slice_in_dim(x, start, HALO, axis=0) for x...  0.95 us
    pallas_call x1, Pallas kernels, local(): call(layout_kernel, laid_out, inner, 10 * cells, 10 * cells)  0.8 us
  transfers between devices with their start and end apart: 4, of which 0 were waited for; matrix products, arithmetic and copies ran while one was open for 4% of the time, Pallas kernels for 14%

profile of v1, /device:TPU:0, one launch (start us, length us, event | category | flops | bytes accessed | tf_op | source)
XLA Modules:
  0.0 38.5 jit_solution(1443706975376876737)
XLA Ops:
  0.6 0.0 copy-start
  0.7 0.9 %multiply_bitcast_fusion.2 = (f32[1,24,256]{2,1,0:T(8,128)S(1)}, f32[1,24,256]{2,1,0:T(8,128)S(1)}, f32[1,24,256]{2,1,0:T(8,128)S(1)}, f32[1,24,256]{2,1,0:T(8,1...) fusion(f32[512,256]{1,0:T(8,128)} %param.4, s32[]{:T(128)S(6)} %select_n.24, s32[512,256]{1,0:T(8,128)} %param.6, ...), kind=kLoop, calls=%fused_computation.7 | loop fusion | flops 86016 | bytes 344072 | tf_op jit(solution)/shard_map/stack | solution.py:577
  1.6 0.7 %collective-permute-start = (f32[3,24,256]{2,1,0:T(8,128)S(1)}, f32[3,24,256]{2,1,0:T(8,128)S(1)}, u32[]{:S(2)}, u32[]{:S(2)}) collective-permute-start(f32[3,24,256]{2,1,0:T(8,128)S(1)} %pad_maximum_fusion), channel_id=1, source_target_pairs={{8,16},{16,8},{9,17},{17,9},{10,18},{18,10},{11,19},{19,11},{12,20... | collective-permute-start | bytes 221192 | tf_op jit(solution)/shard_map/ppermute | solution.py:552
  2.3 5.9 %collective-permute-start.1 = (f32[3,24,256]{2,1,0:T(8,128)S(1)}, f32[3,24,256]{2,1,0:T(8,128)S(1)}, u32[]{:S(2)}, u32[]{:S(2)}) collective-permute-start(f32[3,24,256]{2,1,0:T(8,128)S(1)} %pad_maximum_fusion.1), channel_id=1, source_target_pairs={{0,8},{16,24},{8,0},{24,16},{1,9},{17,25},{9,1},{25,17},{2,10},{18... | collective-permute-start | bytes 221192 | tf_op jit(solution)/shard_map/ppermute | solution.py:552
  8.2 0.0 copy-done
  8.2 1.5 %add_multiply_fusion = (f32[512,256]{1,0:T(8,128)S(1)}, f32[512,256]{1,0:T(8,128)S(1)}, f32[512,256]{1,0:T(8,128)S(1)}) fusion(s32[512,256]{1,0:T(8,128)S(1)} %copy-done, s32[512,256]{1,0:T(8,128)} %param.6, f32[512,256]{1,0:T(8,128)} %param.5, f32[512,256]{1,0:T(8,128)} %param.4), kind=kLoop, calls=%fused_computation | loop fusion | flops 917504 | bytes 3670016 | tf_op jit(solution)/shard_map/mul | solution.py:572
  9.7 0.8 %shard_map.59 = (f32[2,592,128]{2,1,0:T(8,128)S(1)}, f32[2,592,128]{2,1,0:T(8,128)S(1)}, f32[2,592,128]{2,1,0:T(8,128)S(1)}, f32[3,112,128]{2,1,0:T(8,128)S(1)}, f32[3,112,128]{2,1,0:T(8,128)S(1)}) custom-call(f32[512,256]{1,0:T(8,128)S(1)} %get-tuple-element.110.source, f32[512,256]{1,0:T(8,128)S(1)} %get-tuple-element.109.guess, ...), custom_call_target="tpu_custom_call" | custom-call | flops 1310720 | bytes 1310720 | tf_op jit(solution)/shard_map/pallas_call | solution.py:586
  10.5 0.0 collective-permute-done.refs_5_
  10.6 0.0 collective-permute-done.1.refs_6_
  10.6 0.1 shard_map.60
  10.7 0.7 %collective-permute-start.2 = (f32[3,112,128]{2,1,0:T(8,128)S(1)}, f32[3,112,128]{2,1,0:T(8,128)S(1)}, u32[]{:S(2)}, u32[]{:S(2)}) collective-permute-start(f32[3,112,128]{2,1,0:T(8,128)S(1)} %get-tuple-element.61), channel_id=1, source_target_pairs={{1,2},{3,4},{5,6},{2,1},{4,3},{6,5},{9,10},{11,12},{13,14},{10,9},... | collective-permute-start | bytes 516104 | tf_op jit(solution)/shard_map/ppermute | solution.py:552
  11.4 2.9 %collective-permute-start.3 = (f32[3,112,128]{2,1,0:T(8,128)S(1)}, f32[3,112,128]{2,1,0:T(8,128)S(1)}, u32[]{:S(2)}, u32[]{:S(2)}) collective-permute-start(f32[3,112,128]{2,1,0:T(8,128)S(1)} %get-tuple-element.62), channel_id=1, source_target_pairs={{0,1},{2,3},{4,5},{6,7},{1,0},{3,2},{5,4},{7,6},{8,9},{10,11},{12,... | collective-permute-start | bytes 516104 | tf_op jit(solution)/shard_map/ppermute | solution.py:552
  14.3 4.6 %shard_map.61 = (f32[2,592,128]{2,1,0:T(8,128)S(1)}, f32[2,592,128]{2,1,0:T(8,128)S(1)}, f32[2,592,128]{2,1,0:T(8,128)S(1)}, f32[2,592,128]{2,1,0:T(8,128)S(1)},...) custom-call(f32[2,592,128]{2,1,0:T(8,128)S(1)} %get-tuple-element.55, ...), custom_call_target="tpu_custom_call" | custom-call | flops 13107200 | bytes 5242880 | tf_op jit(solution)/shard_map/pallas_call | solution.py:594
  18.9 0.0 collective-permute-done.2.from_cross
  18.9 0.0 collective-permute-done.3.from_pair
  18.9 2.9 %shard_map.62 = (f32[1,592,128]{2,1,0:T(8,128)S(1)}, f32[1,592,128]{2,1,0:T(8,128)S(1)}, f32[1,592,128]{2,1,0:T(8,128)S(1)}, f32[1,592,128]{2,1,0:T(8,128)S(1)},...) custom-call(f32[1,592,128]{2,1,0:T(8,128)S(1)} %get-tuple-element.58, ...), custom_call_target="tpu_custom_call", output_to_operand_aliasing={{0}: (0, {}), {1}: (1, {}), {2}: (2, {})} | custom-call | flops 6553600 | bytes 2621440 | tf_op jit(solution)/shard_map/pallas_call | solution.py:606
  21.9 10.9 %all_to_all.5 = f32[32,4,128]{2,1,0:T(4,128)S(1)} all-to-all(f32[32,4,128]{2,1,0:T(4,128)S(1)} %bitcast.15), channel_id=1, replica_groups=mesh['gx'=4,'gy'=8] {'gx','gy'}, dimensions={0} | all-to-all | bytes 131072 | tf_op jit(solution)/shard_map/all_to_all | solution.py:619
  32.7 5.8 %shard_map.63 = (f32[512,256]{1,0:T(8,128)}, f32[512,256]{1,0:T(8,128)}) custom-call(f32[4,8,4,128]{3,2,1,0:T(4,128)S(1)} %bitcast.14, f32[8,128]{1,0:T(8,128)S(1)} %get-tuple-element.66.dense_ref, f32[3,112,128]{2,1,0:T(8,128)S(1)} %collective-permute-done.2.from_cross, f32[3,112,128]{2,1,0:T(8,128)S(1)} %collective-permute-done.3.from_pair, ...), custom_call_target="tpu_custom_call" | custom-call | flops 7864320 | bytes 5242880 | tf_op jit(solution)/shard_map/pallas_call | solution.py:620
  (2 shorter events, 0.0 us)
Async XLA Ops:
  0.6 7.6 %copy-start = (s32[512,256]{1,0:T(8,128)S(1)}, s32[512,256]{1,0:T(8,128)}, u32[]{:S(2)}) copy-start(s32[512,256]{1,0:T(8,128)} %param.7) | copy-start | bytes 1572868
  1.6 8.9 %collective-permute-start = (f32[3,24,256]{2,1,0:T(8,128)S(1)}, f32[3,24,256]{2,1,0:T(8,128)S(1)}, u32[]{:S(2)}, u32[]{:S(2)}) collective-permute-start(f32[3,24,256]{2,1,0:T(8,128)S(1)} %pad_maximum_fusion), channel_id=1, source_target_pairs={{8,16},{16,8},{9,17},{17,9},{10,18},{18,10},{11,19},{19,11},{12,20... | collective-permute-start | bytes 221192 | tf_op jit(solution)/shard_map/ppermute | solution.py:552
  2.3 8.3 %collective-permute-start.1 = (f32[3,24,256]{2,1,0:T(8,128)S(1)}, f32[3,24,256]{2,1,0:T(8,128)S(1)}, u32[]{:S(2)}, u32[]{:S(2)}) collective-permute-start(f32[3,24,256]{2,1,0:T(8,128)S(1)} %pad_maximum_fusion.1), channel_id=1, source_target_pairs={{0,8},{16,24},{8,0},{24,16},{1,9},{17,25},{9,1},{25,17},{2,10},{18... | collective-permute-start | bytes 221192 | tf_op jit(solution)/shard_map/ppermute | solution.py:552
  10.7 8.2 %collective-permute-start.2 = (f32[3,112,128]{2,1,0:T(8,128)S(1)}, f32[3,112,128]{2,1,0:T(8,128)S(1)}, u32[]{:S(2)}, u32[]{:S(2)}) collective-permute-start(f32[3,112,128]{2,1,0:T(8,128)S(1)} %get-tuple-element.61), channel_id=1, source_target_pairs={{1,2},{3,4},{5,6},{2,1},{4,3},{6,5},{9,10},{11,12},{13,14},{10,9},... | collective-permute-start | bytes 516104 | tf_op jit(solution)/shard_map/ppermute | solution.py:552
  11.4 7.5 %collective-permute-start.3 = (f32[3,112,128]{2,1,0:T(8,128)S(1)}, f32[3,112,128]{2,1,0:T(8,128)S(1)}, u32[]{:S(2)}, u32[]{:S(2)}) collective-permute-start(f32[3,112,128]{2,1,0:T(8,128)S(1)} %get-tuple-element.62), channel_id=1, source_target_pairs={{0,1},{2,3},{4,5},{6,7},{1,0},{3,2},{5,4},{7,6},{8,9},{10,11},{12,... | collective-permute-start | bytes 516104 | tf_op jit(solution)/shard_map/ppermute | solution.py:552

commit v2 on v1

--- a/solution.py
+++ b/solution.py
@@ -11,12 +11,14 @@
 damping = 0.01
 relaxation = 0.8
 
-HALO = 24
+HALO = 16
+EDGE = 24
+NEAR = 20
 LANES = 128
 INNER = LANES // 2 - HALO
 TOP = 32
 GUARD = 8
-PIECES = 5
+PIECES = 8
 CHUNK = 144
 LAG = 8
 TALL = 16
@@ -50,7 +52,7 @@
 
 
 def clear_rim(ref):
-    rim = GUARD + TOP - HALO
+    rim = GUARD + TOP - EDGE
     zeros = jnp.zeros((rim, LANES), jnp.float32)
     for t in range(ref.shape[0]):
         ref[t, 0:rim, :] = zeros
@@ -193,6 +195,14 @@
         )
 
 
+def group_of(x, west):
+    return (lane_of(x) // HALO + (1 if west else 0)) % PIECES
+
+
+def packed(part, p, west):
+    return roll(part, p * HALO - HALO if west else p * HALO + HALO)
+
+
 def to_sides(west, east, cross_ref, pair_ref, k, rows):
     even = lax.axis_index("gy") % 2 == 0
     cross_ref[k, rows, :] = jnp.where(even, west, east)
@@ -202,21 +212,12 @@
 def layout_kernel(source, guess, weight, own_source, own_guess, own_weight, cross_ref, pair_ref, *inner):
     rows = source.shape[0]
     piece = cross_ref.shape[1]
-    tail = rows - (PIECES - 1) * piece
-    for k, (block, own) in enumerate(zip((source, guess, weight), (own_source, own_guess, own_weight))):
+    whole = rows // piece
+    tail = rows - whole * piece
+    for own, block in zip((own_source, own_guess, own_weight), (source, guess, weight)):
         clear_rim(own)
-        sides = []
         for t in range(2):
             own[t, GUARD + TOP : GUARD + TOP + rows, :] = block[:, t * LANES : (t + 1) * LANES]
-        for tile, first in ((0, 0), (1, LANES - HALO)):
-            columns = slice(tile * LANES, (tile + 1) * LANES)
-            last = roll(block[(PIECES - 1) * piece :, columns], (PIECES - 1) * HALO - first)
-            packed = jnp.concatenate((last, jnp.zeros((piece - tail, LANES), jnp.float32)), axis=0)
-            for p in range(PIECES - 1):
-                part = block[p * piece : (p + 1) * piece, columns]
-                packed = jnp.where(lane_of(part) // HALO == p, roll(part, p * HALO - first), packed)
-            sides.append(packed)
-        to_sides(*sides, cross_ref, pair_ref, k, slice(0, piece))
     weights, start, height = (own_weight, *inner), TOP, rows
     for level in range(LEVELS):
         pooled = [0.125 * w for w in pool_rows(weights[level], start, height, 2**level)]
@@ -224,35 +225,52 @@
         if level < LEVELS - 1:
             store(weights[level + 1], start, height, pooled)
     lane = lane_of(pooled[0])
-    free = PIECES * HALO
-    index = jnp.clip(lane - free, 0, LANES - 1 - free) * 2**LEVELS
-    for t in range(2):
-        taken = jnp.take_along_axis(pooled[t], index, axis=1)
-        span = slice(t * height, (t + 1) * height)
-        for ref in (cross_ref, pair_ref):
-            ref[0, span, :] = jnp.where(lane >= free, taken, ref[0, span, :])
+    width = HALO // 2
+    index = (lane % width) * 2**LEVELS
+    coarse = [jnp.take_along_axis(p, index, axis=1) for p in pooled]
+    coarse = jnp.where(lane % HALO < width, *coarse)
+    for k, block in enumerate((source, guess, weight)):
+        sides = []
+        for west in (True, False):
+            columns = slice(0, LANES) if west else slice(LANES, 2 * LANES)
+            below = jnp.zeros((piece - tail, LANES), jnp.float32)
+            if k < 2:
+                below = jnp.concatenate((below[: 2 * EDGE], coarse[k * height // 2 : (k + 1) * height // 2]), axis=0)
+            last = packed(block[whole * piece :, columns], whole, west)
+            both = jnp.concatenate((last, below), axis=0)
+            for p in range(whole):
+                part = packed(block[p * piece : (p + 1) * piece, columns], p, west)
+                both = jnp.where(group_of(part, west) == p, part, both)
+            sides.append(both)
+        to_sides(*sides, cross_ref, pair_ref, k, slice(0, piece))
 
 
 def halo_kernel(*refs):
     first_rows, second_rows, *own, cross_ref, pair_ref = refs[5:]
     total = own[0].shape[1] - 2 * GUARD
-    piece = cross_ref.shape[1]
-    even = lax.axis_index("gx") % 2 == 0
-    shift = (PIECES - 1) * HALO
+    last = PIECES - 1
+    first = total - 2 * TOP - last * cross_ref.shape[1]
+    even, even_y = lax.axis_index("gx") % 2 == 0, lax.axis_index("gy") % 2 == 0
     for k in range(3):
         above = jnp.where(even, first_rows[k], second_rows[k])
         below = jnp.where(even, second_rows[k], first_rows[k])
-        for rows, row, first in ((above, TOP - HALO, piece - 2 * HALO), (below, total - TOP, piece - HALO)):
+        for side, (rows, row) in enumerate(((above, TOP - EDGE), (below, total - TOP))):
             body = [rows[:, t * LANES : (t + 1) * LANES] for t in range(2)]
             for t in range(2):
-                own[k][t, GUARD + row : GUARD + row + HALO, :] = body[t]
-            span = slice(first, first + HALO)
-            here = lane_of(body[0]) // HALO == PIECES - 1
+                own[k][t, GUARD + row : GUARD + row + EDGE, :] = body[t]
+            span = slice(first + side * EDGE, first + (side + 1) * EDGE)
+            parts = []
+            for part, west in zip(body, (True, False)):
+                here = group_of(part, west) == last
+                parts.append((here, packed(part, last, west)))
+            (here_west, west), (here_east, east) = parts
             cross, pair = cross_ref[k, span, :], pair_ref[k, span, :]
-            west, east = roll(body[0], shift), roll(body[1], shift + HALO - LANES)
-            even_y = lax.axis_index("gy") % 2 == 0
-            cross_ref[k, span, :] = jnp.where(here, jnp.where(even_y, west, east), cross)
-            pair_ref[k, span, :] = jnp.where(here, jnp.where(even_y, east, west), pair)
+            cross_ref[k, span, :] = jnp.where(
+                even_y, jnp.where(here_west, west, cross), jnp.where(here_east, east, cross)
+            )
+            pair_ref[k, span, :] = jnp.where(
+                even_y, jnp.where(here_east, east, pair), jnp.where(here_west, west, pair)
+            )
 
 
 def body_kernel(source, guess, weight, *refs):
@@ -271,7 +289,7 @@
         frame[0] = jnp.where(lane_of(tiles[0]) < LANES // 2, roll(tiles[0], HALO), roll(tiles[1], -HALO))
 
 
-def frame_kernel(_a, _b, _c, from_cross, from_pair, body_weight, body_source, *refs):
+def frame_kernel(_a, _b, _c, from_pair, from_cross, body_weight, body_source, *refs):
     even = lax.axis_index("gy") % 2 == 0
     frames, states, refs = refs[:3], refs[3 : 3 + 4 * (LEVELS - 1)], refs[3 + 4 * (LEVELS - 1) :]
     frame_source, frame_guess, frame_weight = frames
@@ -284,18 +302,20 @@
     diagonals = (first_diagonal, *inner[2 * depth :])
     piece = from_cross.shape[1]
     for k, frame in enumerate(frames):
-        left = jnp.where(even, from_cross[k], from_pair[k])
-        right = jnp.where(even, from_pair[k], from_cross[k])
-        spans = [(p, 0, TOP + p * piece, piece) for p in range(PIECES - 1)]
-        spans.append((PIECES - 1, 0, TOP + (PIECES - 1) * piece, piece - 2 * HALO))
-        spans += [(PIECES - 1, piece - 2 * HALO, TOP - HALO, HALO), (PIECES - 1, piece - HALO, rows - TOP, HALO)]
+        block = rows - 2 * TOP
+        last = PIECES - 1
+        tail = block - last * piece
+        spans = [(p, 0, TOP + p * piece, piece) for p in range(last)]
+        spans += [(last, 0, TOP + last * piece, tail)]
+        spans += [(last, tail, TOP - EDGE, EDGE), (last, tail + EDGE, rows - TOP, EDGE)]
         for p, first, start, size in spans:
             span = slice(GUARD + start, GUARD + start + size)
-            west = roll(left[first : first + size], -p * HALO)
-            east = roll(right[first : first + size], -(p + 1) * HALO)
-            lane = lane_of(west)
-            inside = jnp.where(lane < HALO, west, frame[0, span, :])
-            frame[0, span, :] = jnp.where(lane >= LANES - HALO, east, inside)
+            cross, pair = from_cross[k, first : first + size, :], from_pair[k, first : first + size, :]
+            from_left = group_of(cross, False) == p
+            both = roll(jnp.where(from_left == even, cross, pair), -p * HALO)
+            lane = lane_of(both)
+            outside = (lane < HALO) | (lane >= LANES - HALO)
+            frame[0, span, :] = jnp.where(outside, both, frame[0, span, :])
     descend_all(rows, sources, frame_guess, weights, states, diagonals, field, resid, 288, 288)
 
     level = LEVELS - 1
@@ -349,12 +369,30 @@
                 dense = jnp.where(place == 4 * g + 2 * group + t, taken, dense)
     dense_ref[...] = dense
 
-    index = jnp.minimum(2 * (lane - lane % (2 * per_tile)) + lane % (2 * per_tile), LANES - 1)
-    level_with, above, below = (fold(x) for x in (jnp.take_along_axis(dense, index, axis=1), dense, roll(dense, -LANES // 2)))
-    x = lax.axis_index("gx")
+    width = 2 * per_tile
+    index = jnp.minimum(2 * (lane - lane % width) + lane % width, LANES - 1)
+    smooth = ring_state[3]
+    beside_me = []
+    for tile, edge, free in ((0, 0, width - 3), (1, LANES - step, 0)):
+        chunk = jnp.take_along_axis(dense, index, axis=1)
+        first = GUARD + halo
+        pieces = []
+        for g in range(coarse_rows // 8):
+            for odd in range(2):
+                rows_of = smooth[tile, pl.ds(first + 16 * g + odd, 8, stride=2), :]
+                pieces.append((g * width + free + odd, rows_of))
+        top = lax.broadcasted_iota(jnp.int32, dense.shape, 0) == 0
+        for g, row in ((0, first - 1), (1, first + 2 * coarse_rows)):
+            pieces.append((g * width + free + 2, jnp.where(top, smooth[tile, row : row + 8, :], 0.0)))
+        for place, values in pieces:
+            chunk = jnp.where(lane == place, roll(values, place - edge), chunk)
+        beside_me.append(fold(chunk))
+    above, below = fold(dense), fold(roll(dense, -LANES // 2))
+    x, y = lax.axis_index("gx"), lax.axis_index("gy")
     for i in range(chunks_ref.shape[0]):
-        chunk = jnp.where(i == x, level_with, jnp.where(i < x, above, below))
-        chunks_ref[i] = jnp.broadcast_to(chunk[None], chunks_ref.shape[1:])
+        for j in range(chunks_ref.shape[1]):
+            level_with = jnp.where(j < y, beside_me[0], beside_me[1])
+            chunks_ref[i, j] = jnp.where(i == x, level_with, jnp.where(i < x, above, below))
 
 
 def fold(x):
@@ -365,7 +403,7 @@
     return jnp.concatenate((x, roll(x, LANES // 2)), axis=0)
 
 
-def coarse_solve(all_ref, dense_ref, from_cross, from_pair, e_ref, width, groups):
+def coarse_solve(all_ref, dense_ref, from_cross, from_pair, e_ref, edge_ref, width, groups):
     x, nx = lax.axis_index("gx"), lax.axis_size("gx")
     y, ny = lax.axis_index("gy"), lax.axis_size("gy")
     tiles = {}
@@ -378,30 +416,48 @@
     dense = dense_ref[...]
     lane = lane_of(dense)
     even = y % 2 == 0
-    height = 8 * groups
-    cross, pair = from_cross[0, : 2 * height, :], from_pair[0, : 2 * height, :]
+    half = 4 * groups
+    first = from_cross.shape[1] - half
+    cross, pair = ([ref[k, first:, :] for k in range(2)] for ref in (from_cross, from_pair))
+    cross, pair = jnp.concatenate(cross, axis=0), jnp.concatenate(pair, axis=0)
     weights = {-1: jnp.where(even, cross, pair), 1: jnp.where(even, pair, cross)}
     bands = [(-1, g) for g in range(TALL // 8)] + [(0, g) for g in range(groups)] + [(1, g) for g in range(TALL // 8)]
     b, w = [], []
     for dx, g in bands:
         b_rows = w_rows = jnp.zeros_like(dense)
         for dy in (-1, 0, 1):
-            first = (dy + 1) * width
-            here = (lane >= first) & (lane < first + width)
+            first_lane = (dy + 1) * width
+            here = (lane >= first_lane) & (lane < first_lane + width)
             if dx or not dy:
                 tile = tiles[dx, dy] if dx else dense
-                b_part, w_part = roll(tile, first - 2 * g * width), roll(tile, first - (2 * g + 1) * width)
+                b_part = roll(tile, first_lane - 2 * g * width)
+                w_part = roll(tile, first_lane - (2 * g + 1) * width)
             else:
-                b_part = roll(tiles[dx, dy], first - g * width)
-                free = PIECES * HALO
-                parts = [weights[dy][t * height + 8 * g : t * height + 8 * g + 8] for t in range(2)]
-                parts = [roll(part, first + t * width // 2 - free) for t, part in enumerate(parts)]
-                w_part = jnp.where(lane < first + width // 2, *parts)
+                b_part = roll(tiles[dx, dy], first_lane - g * width)
+                at = (PIECES - 1 - (dy > 0)) * HALO
+                w_part = roll(weights[dy][8 * g : 8 * g + 8], first_lane - at)
             b_rows = jnp.where(here, b_part, b_rows)
             w_rows = jnp.where(here, w_part, w_rows)
         b.append(b_rows)
         w.append(w_rows)
     b, w = jnp.concatenate(b, axis=0), jnp.concatenate(w, axis=0)
+
+    step = 2 ** (LEVELS - 1)
+    start = GUARD + (TOP >> (LEVELS - 1))
+    zeros = jnp.zeros((GUARD, LANES), jnp.float32)
+    for row in range(0, edge_ref.shape[1], GUARD):
+        edge_ref[0, row : row + GUARD, :] = zeros
+    before, after = tiles[0, -1], tiles[0, 1]
+
+    def columns(place):
+        left, right = roll(before, LANES - step - place), roll(after, -(place + width - 3))
+        return jnp.where(lane < step, right, left)
+
+    for g in range(groups):
+        for odd in range(2):
+            edge_ref[0, pl.ds(start + 16 * g + odd, 8, stride=2), :] = columns(g * width + odd)
+    edge_ref[0, start - 1 : start, :] = columns(2)[:1]
+    edge_ref[0, start + 16 * groups : start + 16 * groups + 1, :] = columns(width + 2)[:1]
 
     rows = b.shape[0]
     zeros = jnp.zeros((GUARD, LANES), jnp.float32)
@@ -434,12 +490,12 @@
     count = 4 * (LEVELS - 1)
     body_state, frame_state, ring_state = refs[:count], refs[count : 2 * count], refs[2 * count : 2 * count + 4]
     out_ref, resid_ref = refs[2 * count + 4 : 2 * count + 6]
-    ring_pe, body_final, frame_final, sems, e_ref, *inner = refs[2 * count + 6 :]
+    ring_pe, body_final, frame_final, sems, e_ref, edge_ref, *inner = refs[2 * count + 6 :]
     outs, inner = inner[:2], inner[2:]
     body_pe, frame_pe = inner[: LEVELS - 1], inner[LEVELS - 1 :]
     rows = out_ref.shape[0] + 2 * TOP
     width = out_ref.shape[1] >> LEVELS
-    e = coarse_solve(all_ref, dense_ref, from_cross, from_pair, e_ref, width, (out_ref.shape[0] >> LEVELS) // 8)
+    e = coarse_solve(all_ref, dense_ref, from_cross, from_pair, e_ref, edge_ref, width, (out_ref.shape[0] >> LEVELS) // 8)
 
     level = LEVELS - 1
     step, halo, height = 2**level, TOP >> level, rows >> level
@@ -456,13 +512,15 @@
         ring_pe[t, pl.ds(GUARD + halo - 2, coarse_rows + 2, stride=2), :] = taken
         ring_pe[t, pl.ds(GUARD + halo - 1, coarse_rows + 2, stride=2), :] = taken
 
-    def climbed(pe, state, start, size, step):
+    def climbed(pe, state, start, size, step, edge=None):
         mid, around = beside_of(pe, state[:2], start, size, step)
         scale, smooth = load(state[2], start, size), load(state[3], start, size)
+        if edge is not None:
+            smooth = smooth[:2] + load(edge, start, size)
         return [(smooth[t] + (1.0 - relaxation) * mid[t]) + scale[t] * around[t] for t in range(len(mid))]
 
     def climb_ring(start, size, level=level, step=step):
-        ring = spread(climbed(ring_pe, ring_state, start, size, step), step // 2)
+        ring = spread(climbed(ring_pe, ring_state, start, size, step, edge_ref), step // 2)
         lane = lane_of(ring[0])
         around = jnp.where(
             lane < LANES // 2,
@@ -499,11 +557,10 @@
         body = (body, [(b[t] + around[t]) - d[t] * body[t] for t in range(2)])
         frame = (frame[0], (b_frame[0] + frame_around[0]) - d_frame[0] * frame[0])
         lane = lane_of(frame[0])
-        near = HALO - 4
         span = pl.ds(base, size)
         for ref, middle, around in ((outs[0], body[0], frame[0]), (outs[1], body[1], frame[1])):
-            ref[span, :LANES] = jnp.where(lane < near, roll(around, -HALO), middle[0])
-            ref[span, LANES:] = jnp.where(lane >= LANES - near, roll(around, HALO), middle[1])
+            ref[span, :LANES] = jnp.where(lane < NEAR, roll(around, -HALO), middle[0])
+            ref[span, LANES:] = jnp.where(lane >= LANES - NEAR, roll(around, HALO), middle[1])
 
     count = rows // CHUNK
     ends = [0] + [CHUNK * (p + 1) - LAG - TOP for p in range(count - 1)] + [out_ref.shape[0]]
@@ -574,12 +631,12 @@
     given = (rhs, pressure, wet_mask, bathy_class)
 
     def edge(start):
-        return jnp.stack(fields(*(lax.dynamic_slice_in_dim(x, start, HALO, axis=0) for x in given)))
+        return jnp.stack(fields(*(lax.dynamic_slice_in_dim(x, start, EDGE, axis=0) for x in given)))
 
     even = lax.axis_index("gx") % 2 == 0
-    first_rows = swap(edge(jnp.where(even, 0, rows - HALO)), "gx", 1)
-    second_rows = swap(edge(jnp.where(even, rows - HALO, 0)), "gx", 0)
-    piece = (rows + 2 * HALO) // PIECES
+    first_rows = swap(edge(jnp.where(even, 0, rows - EDGE)), "gx", 1)
+    second_rows = swap(edge(jnp.where(even, rows - EDGE, 0)), "gx", 0)
+    piece = (rows + 2 * EDGE + (rows >> LEVELS) // 2) // PIECES
     own_shapes = [out(*shape(2, 0))] * 3
     laid_out = [*own_shapes, out(3, piece, LANES), out(3, piece, LANES)]
     inner = [vmem(2, level) for level in range(1, LEVELS)]
@@ -614,14 +671,14 @@
         50 * cells,
         20 * cells,
         input_output_aliases={k: k for k in range(3)},
-    )(frame_source, frame_guess, frame_weight, from_cross, from_pair, body_weight, body_source)
+    )(frame_source, frame_guess, frame_weight, from_pair, from_cross, body_weight, body_source)
     frame_state, frame_diagonal, ring_state = state[:state_count], state[state_count], state[state_count + 1 :]
     gathered = lax.all_to_all(chunks.reshape(nx * ny, 4, LANES), ("gx", "gy"), 0, 0).reshape(chunks.shape)
     return call(
         up_kernel,
         (out(rows, columns), out(rows, columns)),
         [vmem(3, ring), vmem(2, 0), vmem(1, 0), pltpu.SemaphoreType.DMA((8,))]
-        + [pltpu.VMEM(((rows >> LEVELS) + 2 * TALL + 2 * GUARD, LANES), jnp.float32)]
+        + [pltpu.VMEM(((rows >> LEVELS) + 2 * TALL + 2 * GUARD, LANES), jnp.float32), vmem(1, ring)]
         + [pltpu.VMEM((total, columns), jnp.float32)] * 2
         + [vmem(2, level) for level in levels]
         + [vmem(1, level) for level in levels],

time: 38.7 us -> 38.3 us (0.990)
  starting transfers between devices: 10.2 us -> 7.31 us
  blocking collectives: 10.9 us -> 13.3 us
    ppermute x4, starting transfers between devices: 10.2 us -> 7.31 us  [swap(): return lax.ppermute(x, axis, pairs + [(j, i) for i, j in pairs])]
    all_to_all x1, blocking collectives: 10.9 us -> 13.3 us  [local(): lax.all_to_all(chunks.reshape(nx * ny, 4, LANES), ('gx', 'gy'), 0, 0)]
  transfers between devices with their start and end apart: 4 -> 4, of which waited for: 0 -> 1; matrix products, arithmetic and copies ran while one was open for 4% -> 4% of each run, Pallas kernels for 14% -> 14%
where the time goes in v2:
time: 38.3 us; the launch traced here: 38.1 us
  Pallas kernels  14.1 us (37%)
  blocking collectives  13.3 us (35%)
  starting transfers between devices  7.31 us (19%)
  other arithmetic  2.46 us (6%)
  between operations  0.75 us (2%)
    all_to_all x1, blocking collectives, local(): lax.all_to_all(chunks.reshape(nx * ny, 4, LANES), ('gx', 'gy'), 0, 0)  13.3 us
    ppermute x4, starting transfers between devices, swap(): return lax.ppermute(x, axis, pairs + [(j, i) for i, j in pairs])  7.31 us
    pallas_call x1, Pallas kernels, local(): call(up_kernel, (out(rows, columns), out(rows, columns)), [vmem(3, ring),...  5.89 us
    pallas_call x1, Pallas kernels, local(): call(body_kernel, [out(*shape(2, level)) for level in levels for _ in ran...  4.61 us
    pallas_call x1, Pallas kernels, local(): call(frame_kernel, [out(*shape(1, 0))] * 3 + [out(*shape(1, level)) for l...  2.79 us
    mul x1, other arithmetic, fields(): return (wet * r, wet * p, wet * (1.0 + 0.5 * c.astype(jnp.float32)))  1.51 us
    another operation x3, other arithmetic, edge(): jnp.stack(fields(*(lax.dynamic_slice_in_dim(x, start, EDGE, axis=0) for x...  0.95 us
  transfers between devices with their start and end apart: 4, of which 1 were waited for; matrix products, arithmetic and copies ran while one was open for 4% of the time, Pallas kernels for 14%

profile of v2, /device:TPU:0, one launch (start us, length us, event | category | flops | bytes accessed | tf_op | source)
XLA Modules:
  0.0 38.1 jit_solution(6153399205778681255)
XLA Ops:
  0.6 0.0 copy-start
  0.7 0.9 %multiply_bitcast_fusion.2 = (f32[1,24,256]{2,1,0:T(8,128)S(1)}, f32[1,24,256]{2,1,0:T(8,128)S(1)}, f32[1,24,256]{2,1,0:T(8,128)S(1)}, f32[1,24,256]{2,1,0:T(8,1...) fusion(f32[512,256]{1,0:T(8,128)} %param.4, s32[]{:T(128)S(6)} %select_n.24, s32[512,256]{1,0:T(8,128)} %param.6, ...), kind=kLoop, calls=%fused_computation.7 | loop fusion | flops 86016 | bytes 344072 | tf_op jit(solution)/shard_map/stack | solution.py:634
  1.6 0.7 %collective-permute-start = (f32[3,24,256]{2,1,0:T(8,128)S(1)}, f32[3,24,256]{2,1,0:T(8,128)S(1)}, u32[]{:S(2)}, u32[]{:S(2)}) collective-permute-start(f32[3,24,256]{2,1,0:T(8,128)S(1)} %pad_maximum_fusion), channel_id=1, source_target_pairs={{8,16},{16,8},{9,17},{17,9},{10,18},{18,10},{11,19},{19,11},{12,20... | collective-permute-start | bytes 221192 | tf_op jit(solution)/shard_map/ppermute | solution.py:609
  2.3 5.9 %collective-permute-start.1 = (f32[3,24,256]{2,1,0:T(8,128)S(1)}, f32[3,24,256]{2,1,0:T(8,128)S(1)}, u32[]{:S(2)}, u32[]{:S(2)}) collective-permute-start(f32[3,24,256]{2,1,0:T(8,128)S(1)} %pad_maximum_fusion.1), channel_id=1, source_target_pairs={{0,8},{16,24},{8,0},{24,16},{1,9},{17,25},{9,1},{25,17},{2,10},{18... | collective-permute-start | bytes 221192 | tf_op jit(solution)/shard_map/ppermute | solution.py:609
  8.2 0.0 copy-done
  8.2 1.5 %add_multiply_fusion = (f32[512,256]{1,0:T(8,128)S(1)}, f32[512,256]{1,0:T(8,128)S(1)}, f32[512,256]{1,0:T(8,128)S(1)}) fusion(s32[512,256]{1,0:T(8,128)S(1)} %copy-done, s32[512,256]{1,0:T(8,128)} %param.6, f32[512,256]{1,0:T(8,128)} %param.5, f32[512,256]{1,0:T(8,128)} %param.4), kind=kLoop, calls=%fused_computation | loop fusion | flops 917504 | bytes 3670016 | tf_op jit(solution)/shard_map/mul | solution.py:629
  9.7 0.7 %shard_map.59 = (f32[2,592,128]{2,1,0:T(8,128)S(1)}, f32[2,592,128]{2,1,0:T(8,128)S(1)}, f32[2,592,128]{2,1,0:T(8,128)S(1)}, f32[3,72,128]{2,1,0:T(8,128)S(1)}, f32[3,72,128]{2,1,0:T(8,128)S(1)}) custom-call(f32[512,256]{1,0:T(8,128)S(1)} %get-tuple-element.110.source, f32[512,256]{1,0:T(8,128)S(1)} %get-tuple-element.109.guess, ...), custom_call_target="tpu_custom_call" | custom-call | flops 1310720 | bytes 1310720 | tf_op jit(solution)/shard_map/pallas_call | solution.py:643
  10.4 0.0 collective-permute-done.refs_5_
  10.5 0.1 collective-permute-done.1.refs_6_
  10.5 0.1 shard_map.60
  10.6 0.1 collective-permute-start.2
  10.7 0.7 %collective-permute-start.3 = (f32[3,72,128]{2,1,0:T(8,128)S(1)}, f32[3,72,128]{2,1,0:T(8,128)S(1)}, u32[]{:S(2)}, u32[]{:S(2)}) collective-permute-start(f32[3,72,128]{2,1,0:T(8,128)S(1)} %get-tuple-element.62), channel_id=1, source_target_pairs={{1,2},{3,4},{5,6},{2,1},{4,3},{6,5},{9,10},{11,12},{13,14},{10,9},... | collective-permute-start | bytes 331784 | tf_op jit(solution)/shard_map/ppermute | solution.py:609
  11.4 4.6 %shard_map.61 = (f32[2,592,128]{2,1,0:T(8,128)S(1)}, f32[2,592,128]{2,1,0:T(8,128)S(1)}, f32[2,592,128]{2,1,0:T(8,128)S(1)}, f32[2,592,128]{2,1,0:T(8,128)S(1)},...) custom-call(f32[2,592,128]{2,1,0:T(8,128)S(1)} %get-tuple-element.55, ...), custom_call_target="tpu_custom_call" | custom-call | flops 13107200 | bytes 5242880 | tf_op jit(solution)/shard_map/pallas_call | solution.py:651
  16.0 0.0 collective-permute-done.2.from_pair
  16.0 0.0 collective-permute-done.3.from_cross
  16.0 2.8 %shard_map.62 = (f32[1,592,128]{2,1,0:T(8,128)S(1)}, f32[1,592,128]{2,1,0:T(8,128)S(1)}, f32[1,592,128]{2,1,0:T(8,128)S(1)}, f32[1,592,128]{2,1,0:T(8,128)S(1)},...) custom-call(f32[1,592,128]{2,1,0:T(8,128)S(1)} %get-tuple-element.58, ...), custom_call_target="tpu_custom_call", output_to_operand_aliasing={{0}: (0, {}), {1}: (1, {}), {2}: (2, {})} | custom-call | flops 6553600 | bytes 2621440 | tf_op jit(solution)/shard_map/pallas_call | solution.py:663
  18.8 13.3 %all_to_all.5 = f32[32,4,128]{2,1,0:T(4,128)S(1)} all-to-all(f32[32,4,128]{2,1,0:T(4,128)S(1)} %bitcast.15), channel_id=1, replica_groups=mesh['gx'=4,'gy'=8] {'gx','gy'}, dimensions={0} | all-to-all | bytes 131072 | tf_op jit(solution)/shard_map/all_to_all | solution.py:676
  32.2 5.9 %shard_map.63 = (f32[512,256]{1,0:T(8,128)}, f32[512,256]{1,0:T(8,128)}) custom-call(f32[4,8,4,128]{3,2,1,0:T(4,128)S(1)} %bitcast.14, f32[8,128]{1,0:T(8,128)S(1)} %get-tuple-element.66.dense_ref, f32[3,72,128]{2,1,0:T(8,128)S(1)} %collective-permute-done.3.from_cross, f32[3,72,128]{2,1,0:T(8,128)S(1)} %collective-permute-done.2.from_pair, ...), custom_call_target="tpu_custom_call" | custom-call | flops 7864320 | bytes 5242880 | tf_op jit(solution)/shard_map/pallas_call | solution.py:677
  (2 shorter events, 0.0 us)
Async XLA Ops:
  0.6 7.6 %copy-start = (s32[512,256]{1,0:T(8,128)S(1)}, s32[512,256]{1,0:T(8,128)}, u32[]{:S(2)}) copy-start(s32[512,256]{1,0:T(8,128)} %param.7) | copy-start | bytes 1572868
  1.6 8.8 %collective-permute-start = (f32[3,24,256]{2,1,0:T(8,128)S(1)}, f32[3,24,256]{2,1,0:T(8,128)S(1)}, u32[]{:S(2)}, u32[]{:S(2)}) collective-permute-start(f32[3,24,256]{2,1,0:T(8,128)S(1)} %pad_maximum_fusion), channel_id=1, source_target_pairs={{8,16},{16,8},{9,17},{17,9},{10,18},{18,10},{11,19},{19,11},{12,20... | collective-permute-start | bytes 221192 | tf_op jit(solution)/shard_map/ppermute | solution.py:609
  2.3 8.2 %collective-permute-start.1 = (f32[3,24,256]{2,1,0:T(8,128)S(1)}, f32[3,24,256]{2,1,0:T(8,128)S(1)}, u32[]{:S(2)}, u32[]{:S(2)}) collective-permute-start(f32[3,24,256]{2,1,0:T(8,128)S(1)} %pad_maximum_fusion.1), channel_id=1, source_target_pairs={{0,8},{16,24},{8,0},{24,16},{1,9},{17,25},{9,1},{25,17},{2,10},{18... | collective-permute-start | bytes 221192 | tf_op jit(solution)/shard_map/ppermute | solution.py:609
  10.6 5.4 %collective-permute-start.2 = (f32[3,72,128]{2,1,0:T(8,128)S(1)}, f32[3,72,128]{2,1,0:T(8,128)S(1)}, u32[]{:S(2)}, u32[]{:S(2)}) collective-permute-start(f32[3,72,128]{2,1,0:T(8,128)S(1)} %get-tuple-element.61), channel_id=1, source_target_pairs={{0,1},{2,3},{4,5},{6,7},{1,0},{3,2},{5,4},{7,6},{8,9},{10,11},{12,... | collective-permute-start | bytes 331784 | tf_op jit(solution)/shard_map/ppermute | solution.py:609
  10.7 5.3 %collective-permute-start.3 = (f32[3,72,128]{2,1,0:T(8,128)S(1)}, f32[3,72,128]{2,1,0:T(8,128)S(1)}, u32[]{:S(2)}, u32[]{:S(2)}) collective-permute-start(f32[3,72,128]{2,1,0:T(8,128)S(1)} %get-tuple-element.62), channel_id=1, source_target_pairs={{1,2},{3,4},{5,6},{2,1},{4,3},{6,5},{9,10},{11,12},{13,14},{10,9},... | collective-permute-start | bytes 331784 | tf_op jit(solution)/shard_map/ppermute | solution.py:609

commit v3 on v2

--- a/solution.py
+++ b/solution.py
@@ -12,14 +12,14 @@
 relaxation = 0.8
 
 HALO = 16
-EDGE = 24
 NEAR = 20
 LANES = 128
 INNER = LANES // 2 - HALO
-TOP = 32
+TOP = 16
 GUARD = 8
 PIECES = 8
-CHUNK = 144
+CHUNK = 136
+PART = 72
 LAG = 8
 TALL = 16
 VMEM_LIMIT = 40 * 1024 * 1024
@@ -49,14 +49,6 @@
         return moved
     edge = lane_of(tiles[0]) >= LANES - step
     return [jnp.where(edge, moved[(i + 1) % count], moved[i]) for i in range(count)]
-
-
-def clear_rim(ref):
-    rim = GUARD + TOP - EDGE
-    zeros = jnp.zeros((rim, LANES), jnp.float32)
-    for t in range(ref.shape[0]):
-        ref[t, 0:rim, :] = zeros
-        ref[t, ref.shape[1] - rim :, :] = zeros
 
 
 def spread(tiles, step):
@@ -215,7 +207,7 @@
     whole = rows // piece
     tail = rows - whole * piece
     for own, block in zip((own_source, own_guess, own_weight), (source, guess, weight)):
-        clear_rim(own)
+        clear_guards(own, rows + 2 * TOP)
         for t in range(2):
             own[t, GUARD + TOP : GUARD + TOP + rows, :] = block[:, t * LANES : (t + 1) * LANES]
     weights, start, height = (own_weight, *inner), TOP, rows
@@ -235,7 +227,8 @@
             columns = slice(0, LANES) if west else slice(LANES, 2 * LANES)
             below = jnp.zeros((piece - tail, LANES), jnp.float32)
             if k < 2:
-                below = jnp.concatenate((below[: 2 * EDGE], coarse[k * height // 2 : (k + 1) * height // 2]), axis=0)
+                half = coarse[k * height // 2 : (k + 1) * height // 2]
+                below = jnp.concatenate((below[: 2 * TOP], half, below[2 * TOP + height // 2 :]), axis=0)
             last = packed(block[whole * piece :, columns], whole, west)
             both = jnp.concatenate((last, below), axis=0)
             for p in range(whole):
@@ -254,11 +247,11 @@
     for k in range(3):
         above = jnp.where(even, first_rows[k], second_rows[k])
         below = jnp.where(even, second_rows[k], first_rows[k])
-        for side, (rows, row) in enumerate(((above, TOP - EDGE), (below, total - TOP))):
+        for side, (rows, row) in enumerate(((above, 0), (below, total - TOP))):
             body = [rows[:, t * LANES : (t + 1) * LANES] for t in range(2)]
             for t in range(2):
-                own[k][t, GUARD + row : GUARD + row + EDGE, :] = body[t]
-            span = slice(first + side * EDGE, first + (side + 1) * EDGE)
+                own[k][t, GUARD + row : GUARD + row + TOP, :] = body[t]
+            span = slice(first + side * TOP, first + (side + 1) * TOP)
             parts = []
             for part, west in zip(body, (True, False)):
                 here = group_of(part, west) == last
@@ -283,7 +276,7 @@
     sources = (source, *inner[depth : 2 * depth], last_source)
     diagonal = (first_diagonal, *inner[2 * depth :])
     weights[0][...] = weight[...]
-    descend_all(rows, sources, guess, weights, states, diagonal, field, resid, 144, 144)
+    descend_all(rows, sources, guess, weights, states, diagonal, field, resid, CHUNK, CHUNK)
     for own, frame in zip((source, guess, weight), frames):
         tiles = [own[t] for t in range(2)]
         frame[0] = jnp.where(lane_of(tiles[0]) < LANES // 2, roll(tiles[0], HALO), roll(tiles[1], -HALO))
@@ -307,7 +300,7 @@
         tail = block - last * piece
         spans = [(p, 0, TOP + p * piece, piece) for p in range(last)]
         spans += [(last, 0, TOP + last * piece, tail)]
-        spans += [(last, tail, TOP - EDGE, EDGE), (last, tail + EDGE, rows - TOP, EDGE)]
+        spans += [(last, tail, 0, TOP), (last, tail + TOP, rows - TOP, TOP)]
         for p, first, start, size in spans:
             span = slice(GUARD + start, GUARD + start + size)
             cross, pair = from_cross[k, first : first + size, :], from_pair[k, first : first + size, :]
@@ -316,7 +309,7 @@
             lane = lane_of(both)
             outside = (lane < HALO) | (lane >= LANES - HALO)
             frame[0, span, :] = jnp.where(outside, both, frame[0, span, :])
-    descend_all(rows, sources, frame_guess, weights, states, diagonals, field, resid, 288, 288)
+    descend_all(rows, sources, frame_guess, weights, states, diagonals, field, resid, 2 * CHUNK, 2 * CHUNK)
 
     level = LEVELS - 1
     step, halo, height = 2**level, TOP >> level, rows >> level
@@ -373,7 +366,7 @@
     index = jnp.minimum(2 * (lane - lane % width) + lane % width, LANES - 1)
     smooth = ring_state[3]
     beside_me = []
-    for tile, edge, free in ((0, 0, width - 3), (1, LANES - step, 0)):
+    for tile, edge, free in ((0, 0, width - 2), (1, LANES - step, 0)):
         chunk = jnp.take_along_axis(dense, index, axis=1)
         first = GUARD + halo
         pieces = []
@@ -381,13 +374,20 @@
             for odd in range(2):
                 rows_of = smooth[tile, pl.ds(first + 16 * g + odd, 8, stride=2), :]
                 pieces.append((g * width + free + odd, rows_of))
-        top = lax.broadcasted_iota(jnp.int32, dense.shape, 0) == 0
-        for g, row in ((0, first - 1), (1, first + 2 * coarse_rows)):
-            pieces.append((g * width + free + 2, jnp.where(top, smooth[tile, row : row + 8, :], 0.0)))
         for place, values in pieces:
             chunk = jnp.where(lane == place, roll(values, place - edge), chunk)
         beside_me.append(fold(chunk))
-    above, below = fold(dense), fold(roll(dense, -LANES // 2))
+    sublane = lax.broadcasted_iota(jnp.int32, dense.shape, 0)
+    beyond = []
+    for row, group, free in ((0, 1, 6), (2 * coarse_rows - 1, 2, 0)):
+        chunk = dense
+        for tile in range(2):
+            values = jnp.broadcast_to(smooth[tile, GUARD + halo + row : GUARD + halo + row + 1, :], dense.shape)
+            values = jnp.take_along_axis(values, (lane % width) * step, axis=1)
+            here = (sublane == free + tile) & (lane // width == 2 * group)
+            chunk = jnp.where(here, values, chunk)
+        beyond.append(chunk)
+    above, below = fold(beyond[0]), fold(roll(beyond[1], -LANES // 2))
     x, y = lax.axis_index("gx"), lax.axis_index("gy")
     for i in range(chunks_ref.shape[0]):
         for j in range(chunks_ref.shape[1]):
@@ -403,7 +403,7 @@
     return jnp.concatenate((x, roll(x, LANES // 2)), axis=0)
 
 
-def coarse_solve(all_ref, dense_ref, from_cross, from_pair, e_ref, edge_ref, width, groups):
+def coarse_solve(all_ref, dense_ref, from_cross, from_pair, e_ref, edge_ref, smooth_ref, rows, width, groups):
     x, nx = lax.axis_index("gx"), lax.axis_size("gx")
     y, ny = lax.axis_index("gy"), lax.axis_size("gy")
     tiles = {}
@@ -417,8 +417,8 @@
     lane = lane_of(dense)
     even = y % 2 == 0
     half = 4 * groups
-    first = from_cross.shape[1] - half
-    cross, pair = ([ref[k, first:, :] for k in range(2)] for ref in (from_cross, from_pair))
+    first = rows % from_cross.shape[1] + 2 * TOP
+    cross, pair = ([ref[k, first : first + half, :] for k in range(2)] for ref in (from_cross, from_pair))
     cross, pair = jnp.concatenate(cross, axis=0), jnp.concatenate(pair, axis=0)
     weights = {-1: jnp.where(even, cross, pair), 1: jnp.where(even, pair, cross)}
     bands = [(-1, g) for g in range(TALL // 8)] + [(0, g) for g in range(groups)] + [(1, g) for g in range(TALL // 8)]
@@ -444,42 +444,50 @@
 
     step = 2 ** (LEVELS - 1)
     start = GUARD + (TOP >> (LEVELS - 1))
-    zeros = jnp.zeros((GUARD, LANES), jnp.float32)
-    for row in range(0, edge_ref.shape[1], GUARD):
-        edge_ref[0, row : row + GUARD, :] = zeros
-    before, after = tiles[0, -1], tiles[0, 1]
+    for t in range(2):
+        edge_ref[t] = smooth_ref[t]
+    edge_ref[2] = jnp.zeros_like(edge_ref[2])
 
     def columns(place):
-        left, right = roll(before, LANES - step - place), roll(after, -(place + width - 3))
+        left = roll(tiles[0, -1], LANES - step - place)
+        right = roll(tiles[0, 1], -(place + width - 2))
         return jnp.where(lane < step, right, left)
 
     for g in range(groups):
         for odd in range(2):
-            edge_ref[0, pl.ds(start + 16 * g + odd, 8, stride=2), :] = columns(g * width + odd)
-    edge_ref[0, start - 1 : start, :] = columns(2)[:1]
-    edge_ref[0, start + 16 * groups : start + 16 * groups + 1, :] = columns(width + 2)[:1]
-
-    rows = b.shape[0]
+            edge_ref[2, pl.ds(start + 16 * g + odd, 8, stride=2), :] = columns(g * width + odd)
+    for dx, row, lanes, free in ((-1, start - 1, 0, 0), (1, start + 16 * groups, 2 * width, 6)):
+        for t in range(2):
+            values = tiles[dx, 0][free + t : free + t + 1]
+            values = jnp.take_along_axis(
+                jnp.broadcast_to(values, dense.shape), lanes + lane // step, axis=1
+            )
+            edge_ref[t, row : row + 1, :] = values[:1]
+        left = roll(tiles[dx, -1][free + 1 : free + 2], LANES - step - (lanes + width - 1))
+        right = roll(tiles[dx, 1][free : free + 1], -lanes)
+        edge_ref[2, row : row + 1, :] = jnp.where(lane[:1] < step, right, left)
+
+    tall = b.shape[0]
     zeros = jnp.zeros((GUARD, LANES), jnp.float32)
     e_ref[0:GUARD, :] = zeros
-    e_ref[GUARD + rows :, :] = zeros
+    e_ref[GUARD + tall :, :] = zeros
 
     def shifted(by):
-        return e_ref[GUARD + by : GUARD + by + rows, :]
-
-    e_ref[GUARD : GUARD + rows, :] = w
+        return e_ref[GUARD + by : GUARD + by + tall, :]
+
+    e_ref[GUARD : GUARD + tall, :] = w
     c_west = jnp.minimum(w, roll(w, 1))
     c_north, c_south = jnp.minimum(w, shifted(-1)), jnp.minimum(w, shifted(1))
     c_east = roll(c_west, -1)
     scale = relaxation / (damping + c_north + c_south + c_west + c_east)
     first = scale * b
     c_west, c_east, c_north, c_south = (scale * c for c in (c_west, c_east, c_north, c_south))
-    e_ref[GUARD : GUARD + rows, :] = first
+    e_ref[GUARD : GUARD + tall, :] = first
 
     def sweep(_, carry):
         e = shifted(0)
         around = (c_west * roll(e, 1) + c_east * roll(e, -1)) + (c_north * shifted(-1) + c_south * shifted(1))
-        e_ref[GUARD : GUARD + rows, :] = ((1.0 - relaxation) * e + first) + around
+        e_ref[GUARD : GUARD + tall, :] = ((1.0 - relaxation) * e + first) + around
         return carry
 
     lax.fori_loop(0, SWEEPS - 1, sweep, 0)
@@ -495,7 +503,7 @@
     body_pe, frame_pe = inner[: LEVELS - 1], inner[LEVELS - 1 :]
     rows = out_ref.shape[0] + 2 * TOP
     width = out_ref.shape[1] >> LEVELS
-    e = coarse_solve(all_ref, dense_ref, from_cross, from_pair, e_ref, edge_ref, width, (out_ref.shape[0] >> LEVELS) // 8)
+    e = coarse_solve(all_ref, dense_ref, from_cross, from_pair, e_ref, edge_ref, ring_state[3], out_ref.shape[0], width, (out_ref.shape[0] >> LEVELS) // 8)
 
     level = LEVELS - 1
     step, halo, height = 2**level, TOP >> level, rows >> level
@@ -516,7 +524,7 @@
         mid, around = beside_of(pe, state[:2], start, size, step)
         scale, smooth = load(state[2], start, size), load(state[3], start, size)
         if edge is not None:
-            smooth = smooth[:2] + load(edge, start, size)
+            smooth = load(edge, start, size)
         return [(smooth[t] + (1.0 - relaxation) * mid[t]) + scale[t] * around[t] for t in range(len(mid))]
 
     def climb_ring(start, size, level=level, step=step):
@@ -547,7 +555,7 @@
                     store_twice(pes[level - 1], start, size, spread(value, step // 2))
 
         if level > 0:
-            for_chunks(height, climb, CHUNK, CHUNK // 2)
+            for_chunks(height, climb, CHUNK, PART)
 
     def last(base, size):
         body, around = beside_of(body_final, body_state[:2], base, size, 1)
@@ -575,9 +583,9 @@
         ]
 
     def finish(i, carry):
-        for_parts(i * CHUNK, CHUNK, climb, CHUNK // 2)
+        for_parts(i * CHUNK, CHUNK, climb, PART)
         base = pl.multiple_of(jnp.maximum(i * CHUNK - LAG, 0), 8)
-        for_parts(base, CHUNK, last, CHUNK // 2)
+        for_parts(base, CHUNK, last, PART)
         for p in range(count):
 
             @pl.when(i == p)
@@ -631,12 +639,12 @@
     given = (rhs, pressure, wet_mask, bathy_class)
 
     def edge(start):
-        return jnp.stack(fields(*(lax.dynamic_slice_in_dim(x, start, EDGE, axis=0) for x in given)))
+        return jnp.stack(fields(*(lax.dynamic_slice_in_dim(x, start, TOP, axis=0) for x in given)))
 
     even = lax.axis_index("gx") % 2 == 0
-    first_rows = swap(edge(jnp.where(even, 0, rows - EDGE)), "gx", 1)
-    second_rows = swap(edge(jnp.where(even, rows - EDGE, 0)), "gx", 0)
-    piece = (rows + 2 * EDGE + (rows >> LEVELS) // 2) // PIECES
+    first_rows = swap(edge(jnp.where(even, 0, rows - TOP)), "gx", 1)
+    second_rows = swap(edge(jnp.where(even, rows - TOP, 0)), "gx", 0)
+    piece = -(-(rows + 2 * TOP + (rows >> LEVELS) // 2) // (8 * PIECES)) * 8
     own_shapes = [out(*shape(2, 0))] * 3
     laid_out = [*own_shapes, out(3, piece, LANES), out(3, piece, LANES)]
     inner = [vmem(2, level) for level in range(1, LEVELS)]
@@ -678,7 +686,7 @@
         up_kernel,
         (out(rows, columns), out(rows, columns)),
         [vmem(3, ring), vmem(2, 0), vmem(1, 0), pltpu.SemaphoreType.DMA((8,))]
-        + [pltpu.VMEM(((rows >> LEVELS) + 2 * TALL + 2 * GUARD, LANES), jnp.float32), vmem(1, ring)]
+        + [pltpu.VMEM(((rows >> LEVELS) + 2 * TALL + 2 * GUARD, LANES), jnp.float32), vmem(3, ring)]
         + [pltpu.VMEM((total, columns), jnp.float32)] * 2
         + [vmem(2, level) for level in levels]
         + [vmem(1, level) for level in levels],

time: 38.3 us -> 37.7 us (0.984)
  transfers between devices with their start and end apart: 4 -> 4, of which waited for: 1 -> 0; matrix products, arithmetic and copies ran while one was open for 4% -> 4% of each run, Pallas kernels for 14% -> 14%
where the time goes in v3:
time: 37.7 us; the launch traced here: 37.4 us
  Pallas kernels  13.8 us (37%)
  blocking collectives  13 us (34%)
  starting transfers between devices  7.31 us (19%)
  other arithmetic  2.54 us (7%)
  between operations  0.75 us (2%)
    all_to_all x1, blocking collectives, local(): lax.all_to_all(chunks.reshape(nx * ny, 4, LANES), ('gx', 'gy'), 0, 0)  13 us
    ppermute x4, starting transfers between devices, swap(): return lax.ppermute(x, axis, pairs + [(j, i) for i, j in pairs])  7.31 us
    pallas_call x1, Pallas kernels, local(): call(up_kernel, (out(rows, columns), out(rows, columns)), [vmem(3, ring),...  5.8 us
    pallas_call x1, Pallas kernels, local(): call(body_kernel, [out(*shape(2, level)) for level in levels for _ in ran...  4.43 us
    pallas_call x1, Pallas kernels, local(): call(frame_kernel, [out(*shape(1, 0))] * 3 + [out(*shape(1, level)) for l...  2.73 us
    mul x1, other arithmetic, fields(): return (wet * r, wet * p, wet * (1.0 + 0.5 * c.astype(jnp.float32)))  1.67 us
    another operation x3, other arithmetic, edge(): jnp.stack(fields(*(lax.dynamic_slice_in_dim(x, start, TOP, axis=0) for x...  0.87 us
  transfers between devices with their start and end apart: 4, of which 0 were waited for; matrix products, arithmetic and copies ran while one was open for 4% of the time, Pallas kernels for 14%

profile of v3, /device:TPU:0, one launch (start us, length us, event | category | flops | bytes accessed | tf_op | source)
XLA Modules:
  0.0 37.4 jit_solution(10948114882211828445)
XLA Ops:
  0.6 0.9 %multiply_bitcast_fusion.2 = (f32[1,16,256]{2,1,0:T(8,128)S(1)}, f32[1,16,256]{2,1,0:T(8,128)S(1)}, f32[1,16,256]{2,1,0:T(8,128)S(1)}, f32[1,16,256]{2,1,0:T(8,1...) fusion(f32[512,256]{1,0:T(8,128)} %param.4, s32[]{:T(128)S(6)} %select_n.24, s32[512,256]{1,0:T(8,128)} %param.6, ...), kind=kLoop, calls=%fused_computation.7 | loop fusion | flops 57344 | bytes 229384 | tf_op jit(solution)/shard_map/stack | solution.py:642
  1.5 0.7 %collective-permute-start = (f32[3,16,256]{2,1,0:T(8,128)S(1)}, f32[3,16,256]{2,1,0:T(8,128)S(1)}, u32[]{:S(2)}, u32[]{:S(2)}) collective-permute-start(f32[3,16,256]{2,1,0:T(8,128)S(1)} %pad_maximum_fusion), channel_id=1, source_target_pairs={{8,16},{16,8},{9,17},{17,9},{10,18},{18,10},{11,19},{19,11},{12,20... | collective-permute-start | bytes 147464 | tf_op jit(solution)/shard_map/ppermute | solution.py:617
  2.2 5.9 %collective-permute-start.1 = (f32[3,16,256]{2,1,0:T(8,128)S(1)}, f32[3,16,256]{2,1,0:T(8,128)S(1)}, u32[]{:S(2)}, u32[]{:S(2)}) collective-permute-start(f32[3,16,256]{2,1,0:T(8,128)S(1)} %pad_maximum_fusion.1), channel_id=1, source_target_pairs={{0,8},{16,24},{8,0},{24,16},{1,9},{17,25},{9,1},{25,17},{2,10},{18... | collective-permute-start | bytes 147464 | tf_op jit(solution)/shard_map/ppermute | solution.py:617
  8.1 1.7 %add_multiply_fusion = (f32[512,256]{1,0:T(8,128)S(1)}, f32[512,256]{1,0:T(8,128)S(1)}, f32[512,256]{1,0:T(8,128)S(1)}) fusion(s32[512,256]{1,0:T(8,128)} %param.7, s32[512,256]{1,0:T(8,128)} %param.6, f32[512,256]{1,0:T(8,128)} %param.5, f32[512,256]{1,0:T(8,128)} %param.4), kind=kLoop, calls=%fused_computation | loop fusion | flops 917504 | bytes 3670016 | tf_op jit(solution)/shard_map/mul | solution.py:637
  9.8 0.7 %shard_map.59 = (f32[2,560,128]{2,1,0:T(8,128)S(1)}, f32[2,560,128]{2,1,0:T(8,128)S(1)}, f32[2,560,128]{2,1,0:T(8,128)S(1)}, f32[3,72,128]{2,1,0:T(8,128)S(1)}, f32[3,72,128]{2,1,0:T(8,128)S(1)}) custom-call(f32[512,256]{1,0:T(8,128)S(1)} %get-tuple-element.110.source, f32[512,256]{1,0:T(8,128)S(1)} %get-tuple-element.109.guess, ...), custom_call_target="tpu_custom_call" | custom-call | flops 1310720 | bytes 1310720 | tf_op jit(solution)/shard_map/pallas_call | solution.py:651
  10.5 0.0 collective-permute-done.refs_5_
  10.5 0.0 collective-permute-done.1.refs_6_
  10.5 0.1 shard_map.60
  10.6 0.1 collective-permute-start.2
  10.7 0.7 %collective-permute-start.3 = (f32[3,72,128]{2,1,0:T(8,128)S(1)}, f32[3,72,128]{2,1,0:T(8,128)S(1)}, u32[]{:S(2)}, u32[]{:S(2)}) collective-permute-start(f32[3,72,128]{2,1,0:T(8,128)S(1)} %get-tuple-element.62), channel_id=1, source_target_pairs={{1,2},{3,4},{5,6},{2,1},{4,3},{6,5},{9,10},{11,12},{13,14},{10,9},... | collective-permute-start | bytes 331784 | tf_op jit(solution)/shard_map/ppermute | solution.py:617
  11.4 4.4 %shard_map.61 = (f32[2,560,128]{2,1,0:T(8,128)S(1)}, f32[2,560,128]{2,1,0:T(8,128)S(1)}, f32[2,560,128]{2,1,0:T(8,128)S(1)}, f32[2,560,128]{2,1,0:T(8,128)S(1)},...) custom-call(f32[2,560,128]{2,1,0:T(8,128)S(1)} %get-tuple-element.55, ...), custom_call_target="tpu_custom_call" | custom-call | flops 13107200 | bytes 5242880 | tf_op jit(solution)/shard_map/pallas_call | solution.py:659
  15.8 0.0 collective-permute-done.2.from_pair
  15.8 0.0 collective-permute-done.3.from_cross
  15.8 2.7 %shard_map.62 = (f32[1,560,128]{2,1,0:T(8,128)S(1)}, f32[1,560,128]{2,1,0:T(8,128)S(1)}, f32[1,560,128]{2,1,0:T(8,128)S(1)}, f32[1,560,128]{2,1,0:T(8,128)S(1)},...) custom-call(f32[1,560,128]{2,1,0:T(8,128)S(1)} %get-tuple-element.58, ...), custom_call_target="tpu_custom_call", output_to_operand_aliasing={{0}: (0, {}), {1}: (1, {}), {2}: (2, {})} | custom-call | flops 6553600 | bytes 2621440 | tf_op jit(solution)/shard_map/pallas_call | solution.py:671
  18.6 13.0 %all_to_all.5 = f32[32,4,128]{2,1,0:T(4,128)S(1)} all-to-all(f32[32,4,128]{2,1,0:T(4,128)S(1)} %bitcast.15), channel_id=1, replica_groups=mesh['gx'=4,'gy'=8] {'gx','gy'}, dimensions={0} | all-to-all | bytes 131072 | tf_op jit(solution)/shard_map/all_to_all | solution.py:684
  31.6 5.8 %shard_map.63 = (f32[512,256]{1,0:T(8,128)}, f32[512,256]{1,0:T(8,128)}) custom-call(f32[4,8,4,128]{3,2,1,0:T(4,128)S(1)} %bitcast.14, f32[8,128]{1,0:T(8,128)S(1)} %get-tuple-element.66.dense_ref, f32[3,72,128]{2,1,0:T(8,128)S(1)} %collective-permute-done.3.from_cross, f32[3,72,128]{2,1,0:T(8,128)S(1)} %collective-permute-done.2.from_pair, ...), custom_call_target="tpu_custom_call" | custom-call | flops 7864320 | bytes 5242880 | tf_op jit(solution)/shard_map/pallas_call | solution.py:685
  (2 shorter events, 0.0 us)
Async XLA Ops:
  1.5 9.0 %collective-permute-start = (f32[3,16,256]{2,1,0:T(8,128)S(1)}, f32[3,16,256]{2,1,0:T(8,128)S(1)}, u32[]{:S(2)}, u32[]{:S(2)}) collective-permute-start(f32[3,16,256]{2,1,0:T(8,128)S(1)} %pad_maximum_fusion), channel_id=1, source_target_pairs={{8,16},{16,8},{9,17},{17,9},{10,18},{18,10},{11,19},{19,11},{12,20... | collective-permute-start | bytes 147464 | tf_op jit(solution)/shard_map/ppermute | solution.py:617
  2.2 8.3 %collective-permute-start.1 = (f32[3,16,256]{2,1,0:T(8,128)S(1)}, f32[3,16,256]{2,1,0:T(8,128)S(1)}, u32[]{:S(2)}, u32[]{:S(2)}) collective-permute-start(f32[3,16,256]{2,1,0:T(8,128)S(1)} %pad_maximum_fusion.1), channel_id=1, source_target_pairs={{0,8},{16,24},{8,0},{24,16},{1,9},{17,25},{9,1},{25,17},{2,10},{18... | collective-permute-start | bytes 147464 | tf_op jit(solution)/shard_map/ppermute | solution.py:617
  10.6 5.2 %collective-permute-start.2 = (f32[3,72,128]{2,1,0:T(8,128)S(1)}, f32[3,72,128]{2,1,0:T(8,128)S(1)}, u32[]{:S(2)}, u32[]{:S(2)}) collective-permute-start(f32[3,72,128]{2,1,0:T(8,128)S(1)} %get-tuple-element.61), channel_id=1, source_target_pairs={{0,1},{2,3},{4,5},{6,7},{1,0},{3,2},{5,4},{7,6},{8,9},{10,11},{12,... | collective-permute-start | bytes 331784 | tf_op jit(solution)/shard_map/ppermute | solution.py:617
  10.7 5.1 %collective-permute-start.3 = (f32[3,72,128]{2,1,0:T(8,128)S(1)}, f32[3,72,128]{2,1,0:T(8,128)S(1)}, u32[]{:S(2)}, u32[]{:S(2)}) collective-permute-start(f32[3,72,128]{2,1,0:T(8,128)S(1)} %get-tuple-element.62), channel_id=1, source_target_pairs={{1,2},{3,4},{5,6},{2,1},{4,3},{6,5},{9,10},{11,12},{13,14},{10,9},... | collective-permute-start | bytes 331784 | tf_op jit(solution)/shard_map/ppermute | solution.py:617

commit v4 on v3

--- a/solution.py
+++ b/solution.py
@@ -19,7 +19,7 @@
 GUARD = 8
 PIECES = 8
 CHUNK = 136
-PART = 72
+PART = CHUNK
 LAG = 8
 TALL = 16
 VMEM_LIMIT = 40 * 1024 * 1024
@@ -201,16 +201,24 @@
     pair_ref[k, rows, :] = jnp.where(even, east, west)
 
 
-def layout_kernel(source, guess, weight, own_source, own_guess, own_weight, cross_ref, pair_ref, *inner):
+def inner_columns(tiles):
+    return jnp.where(lane_of(tiles[0]) < LANES // 2, roll(tiles[0], HALO), roll(tiles[1], -HALO))
+
+
+def layout_kernel(source, guess, weight, *refs):
+    owns, frames, (cross_ref, pair_ref, *inner) = refs[:3], refs[3:6], refs[6:]
     rows = source.shape[0]
     piece = cross_ref.shape[1]
     whole = rows // piece
     tail = rows - whole * piece
-    for own, block in zip((own_source, own_guess, own_weight), (source, guess, weight)):
+    for own, frame, block in zip(owns, frames, (source, guess, weight)):
         clear_guards(own, rows + 2 * TOP)
+        clear_guards(frame, rows + 2 * TOP)
+        tiles = [block[:, t * LANES : (t + 1) * LANES] for t in range(2)]
         for t in range(2):
-            own[t, GUARD + TOP : GUARD + TOP + rows, :] = block[:, t * LANES : (t + 1) * LANES]
-    weights, start, height = (own_weight, *inner), TOP, rows
+            own[t, GUARD + TOP : GUARD + TOP + rows, :] = tiles[t]
+        frame[0, GUARD + TOP : GUARD + TOP + rows, :] = inner_columns(tiles)
+    weights, start, height = (owns[2], *inner), TOP, rows
     for level in range(LEVELS):
         pooled = [0.125 * w for w in pool_rows(weights[level], start, height, 2**level)]
         start, height = start // 2, height // 2
@@ -239,7 +247,8 @@
 
 
 def halo_kernel(*refs):
-    first_rows, second_rows, *own, cross_ref, pair_ref = refs[5:]
+    first_rows, second_rows, *own, cross_ref, pair_ref = refs[8:]
+    own, frames = own[:3], own[3:]
     total = own[0].shape[1] - 2 * GUARD
     last = PIECES - 1
     first = total - 2 * TOP - last * cross_ref.shape[1]
@@ -251,6 +260,7 @@
             body = [rows[:, t * LANES : (t + 1) * LANES] for t in range(2)]
             for t in range(2):
                 own[k][t, GUARD + row : GUARD + row + TOP, :] = body[t]
+            frames[k][0, GUARD + row : GUARD + row + TOP, :] = inner_columns(body)
             span = slice(first + side * TOP, first + (side + 1) * TOP)
             parts = []
             for part, west in zip(body, (True, False)):
@@ -269,7 +279,7 @@
 def body_kernel(source, guess, weight, *refs):
     states = refs[: 4 * (LEVELS - 1)]
     last_weight, last_source, first_diagonal, *refs = refs[4 * (LEVELS - 1) :]
-    frames, (field, resid, weight_in, *inner) = refs[:3], refs[3:]
+    field, resid, weight_in, *inner = refs
     rows = source.shape[1] - 2 * GUARD
     depth = LEVELS - 2
     weights = (weight_in, *inner[:depth], last_weight)
@@ -277,9 +287,6 @@
     diagonal = (first_diagonal, *inner[2 * depth :])
     weights[0][...] = weight[...]
     descend_all(rows, sources, guess, weights, states, diagonal, field, resid, CHUNK, CHUNK)
-    for own, frame in zip((source, guess, weight), frames):
-        tiles = [own[t] for t in range(2)]
-        frame[0] = jnp.where(lane_of(tiles[0]) < LANES // 2, roll(tiles[0], HALO), roll(tiles[1], -HALO))
 
 
 def frame_kernel(_a, _b, _c, from_pair, from_cross, body_weight, body_source, *refs):
@@ -538,7 +545,7 @@
         store_twice(body_pe[level - 1], start, size, ring[:2])
         store_twice(frame_pe[level - 1], start, size, [around])
 
-    for_chunks(height, climb_ring, height, 16)
+    for_chunks(height, climb_ring, height, height)
 
     for level in range(LEVELS - 2, -1, -1):
         step, height = 2**level, rows >> level
@@ -646,22 +653,22 @@
     second_rows = swap(edge(jnp.where(even, rows - TOP, 0)), "gx", 0)
     piece = -(-(rows + 2 * TOP + (rows >> LEVELS) // 2) // (8 * PIECES)) * 8
     own_shapes = [out(*shape(2, 0))] * 3
-    laid_out = [*own_shapes, out(3, piece, LANES), out(3, piece, LANES)]
+    laid_out = [*own_shapes, *[out(*shape(1, 0))] * 3, out(3, piece, LANES), out(3, piece, LANES)]
     inner = [vmem(2, level) for level in range(1, LEVELS)]
     begun = call(layout_kernel, laid_out, inner, 10 * cells, 10 * cells)(*fields(*given))
     *own, to_cross, to_pair = call(
-        halo_kernel, laid_out, (), cells, cells, input_output_aliases={k: k for k in range(5)}
+        halo_kernel, laid_out, (), cells, cells, input_output_aliases={k: k for k in range(8)}
     )(*begun, first_rows, second_rows)
+    own, frames = own[:3], own[3:]
     from_pair = swap(to_pair, "gy", 0)
     from_cross = swap(to_cross, "gy", 1)
 
     state_count = 4 * (LEVELS - 1)
-    *body_state, body_weight, body_source, diagonal, frame_source, frame_guess, frame_weight = call(
+    *body_state, body_weight, body_source, diagonal = call(
         body_kernel,
         [out(*shape(2, level)) for level in levels for _ in range(4)]
         + [out(*shape(2, LEVELS - 1))] * 2
-        + [out(*shape(2, 0))]
-        + [out(*shape(1, 0))] * 3,
+        + [out(*shape(2, 0))],
         [vmem(2, 0)] * 3 + [vmem(2, level) for level in levels[1:]] * 3,
         100 * cells,
         40 * cells,
@@ -679,7 +686,7 @@
         50 * cells,
         20 * cells,
         input_output_aliases={k: k for k in range(3)},
-    )(frame_source, frame_guess, frame_weight, from_pair, from_cross, body_weight, body_source)
+    )(*frames, from_pair, from_cross, body_weight, body_source)
     frame_state, frame_diagonal, ring_state = state[:state_count], state[state_count], state[state_count + 1 :]
     gathered = lax.all_to_all(chunks.reshape(nx * ny, 4, LANES), ("gx", "gy"), 0, 0).reshape(chunks.shape)
     return call(

time: 37.7 us -> 37.7 us (level)
    pallas_call x1, Pallas kernels: 0.71 us -> 1.27 us  [local(): call(layout_kernel, laid_out, inner, 10 * cells, 10 * cells)]
    pallas_call x1, Pallas kernels: 4.43 us -> 4 us  [local(): call(body_kernel, [out(*shape(2, level)) for level in levels for _ in ran...]
where the time goes in v4:
time: 37.7 us; the launch traced here: 37.4 us
  Pallas kernels  13.8 us (37%)
  blocking collectives  13 us (34%)
  starting transfers between devices  7.31 us (19%)
  other arithmetic  2.54 us (7%)
  between operations  0.76 us (2%)
    all_to_all x1, blocking collectives, local(): lax.all_to_all(chunks.reshape(nx * ny, 4, LANES), ('gx', 'gy'), 0, 0)  13 us
    ppermute x4, starting transfers between devices, swap(): return lax.ppermute(x, axis, pairs + [(j, i) for i, j in pairs])  7.31 us
    pallas_call x1, Pallas kernels, local(): call(up_kernel, (out(rows, columns), out(rows, columns)), [vmem(3, ring),...  5.6 us
    pallas_call x1, Pallas kernels, local(): call(body_kernel, [out(*shape(2, level)) for level in levels for _ in ran...  4 us
    pallas_call x1, Pallas kernels, local(): call(frame_kernel, [out(*shape(1, 0))] * 3 + [out(*shape(1, level)) for l...  2.77 us
    mul x1, other arithmetic, fields(): return (wet * r, wet * p, wet * (1.0 + 0.5 * c.astype(jnp.float32)))  1.67 us
    pallas_call x1, Pallas kernels, local(): call(layout_kernel, laid_out, inner, 10 * cells, 10 * cells)  1.27 us
    another operation x3, other arithmetic, edge(): jnp.stack(fields(*(lax.dynamic_slice_in_dim(x, start, TOP, axis=0) for x...  0.87 us
  transfers between devices with their start and end apart: 4, of which 0 were waited for; matrix products, arithmetic and copies ran while one was open for 4% of the time, Pallas kernels for 14%

profile of v4, /device:TPU:0, one launch (start us, length us, event | category | flops | bytes accessed | tf_op | source)
XLA Modules:
  0.0 37.4 jit_solution(12810003438598931354)
XLA Ops:
  0.6 0.9 %multiply_bitcast_fusion.2 = (f32[1,16,256]{2,1,0:T(8,128)S(1)}, f32[1,16,256]{2,1,0:T(8,128)S(1)}, f32[1,16,256]{2,1,0:T(8,128)S(1)}, f32[1,16,256]{2,1,0:T(8,1...) fusion(f32[512,256]{1,0:T(8,128)} %param.4, s32[]{:T(128)S(6)} %select_n.24, s32[512,256]{1,0:T(8,128)} %param.6, ...), kind=kLoop, calls=%fused_computation.7 | loop fusion | flops 57344 | bytes 229384 | tf_op jit(solution)/shard_map/stack | solution.py:649
  1.5 0.7 %collective-permute-start = (f32[3,16,256]{2,1,0:T(8,128)S(1)}, f32[3,16,256]{2,1,0:T(8,128)S(1)}, u32[]{:S(2)}, u32[]{:S(2)}) collective-permute-start(f32[3,16,256]{2,1,0:T(8,128)S(1)} %pad_maximum_fusion), channel_id=1, source_target_pairs={{8,16},{16,8},{9,17},{17,9},{10,18},{18,10},{11,19},{19,11},{12,20... | collective-permute-start | bytes 147464 | tf_op jit(solution)/shard_map/ppermute | solution.py:624
  2.2 5.9 %collective-permute-start.1 = (f32[3,16,256]{2,1,0:T(8,128)S(1)}, f32[3,16,256]{2,1,0:T(8,128)S(1)}, u32[]{:S(2)}, u32[]{:S(2)}) collective-permute-start(f32[3,16,256]{2,1,0:T(8,128)S(1)} %pad_maximum_fusion.1), channel_id=1, source_target_pairs={{0,8},{16,24},{8,0},{24,16},{1,9},{17,25},{9,1},{25,17},{2,10},{18... | collective-permute-start | bytes 147464 | tf_op jit(solution)/shard_map/ppermute | solution.py:624
  8.1 1.7 %add_multiply_fusion = (f32[512,256]{1,0:T(8,128)S(1)}, f32[512,256]{1,0:T(8,128)S(1)}, f32[512,256]{1,0:T(8,128)S(1)}) fusion(s32[512,256]{1,0:T(8,128)} %param.7, s32[512,256]{1,0:T(8,128)} %param.6, f32[512,256]{1,0:T(8,128)} %param.5, f32[512,256]{1,0:T(8,128)} %param.4), kind=kLoop, calls=%fused_computation | loop fusion | flops 917504 | bytes 3670016 | tf_op jit(solution)/shard_map/mul | solution.py:644
  9.8 1.3 %shard_map.59 = (f32[2,560,128]{2,1,0:T(8,128)S(1)}, f32[2,560,128]{2,1,0:T(8,128)S(1)}, f32[2,560,128]{2,1,0:T(8,128)S(1)}, f32[1,560,128]{2,1,0:T(8,128)S(1)},...) custom-call(f32[512,256]{1,0:T(8,128)S(1)} %get-tuple-element.116.so, ...), custom_call_target="tpu_custom_call" | custom-call | flops 1310720 | bytes 1310720 | tf_op jit(solution)/shard_map/pallas_call | solution.py:658
  11.1 0.0 collective-permute-done.refs_8_
  11.1 0.0 collective-permute-done.1.refs_9_
  11.1 0.1 shard_map.60
  11.2 0.1 collective-permute-start.2
  11.3 0.7 %collective-permute-start.3 = (f32[3,72,128]{2,1,0:T(8,128)S(1)}, f32[3,72,128]{2,1,0:T(8,128)S(1)}, u32[]{:S(2)}, u32[]{:S(2)}) collective-permute-start(f32[3,72,128]{2,1,0:T(8,128)S(1)} %get-tuple-element.65), channel_id=1, source_target_pairs={{1,2},{3,4},{5,6},{2,1},{4,3},{6,5},{9,10},{11,12},{13,14},{10,9},... | collective-permute-start | bytes 331784 | tf_op jit(solution)/shard_map/ppermute | solution.py:624
  12.0 4.0 %shard_map.61 = (f32[2,560,128]{2,1,0:T(8,128)S(1)}, f32[2,560,128]{2,1,0:T(8,128)S(1)}, f32[2,560,128]{2,1,0:T(8,128)S(1)}, f32[2,560,128]{2,1,0:T(8,128)S(1)},...) custom-call(f32[2,560,128]{2,1,0:T(8,128)S(1)} %get-tuple-element.66, ...), custom_call_target="tpu_custom_call" | custom-call | flops 13107200 | bytes 5242880 | tf_op jit(solution)/shard_map/pallas_call | solution.py:667
  16.0 0.0 collective-permute-done.2.from_pair
  16.0 0.0 collective-permute-done.3.from_cross
  16.0 2.8 %shard_map.62 = (f32[1,560,128]{2,1,0:T(8,128)S(1)}, f32[1,560,128]{2,1,0:T(8,128)S(1)}, f32[1,560,128]{2,1,0:T(8,128)S(1)}, f32[1,560,128]{2,1,0:T(8,128)S(1)},...) custom-call(f32[1,560,128]{2,1,0:T(8,128)S(1)} %get-tuple-element.61, ...), custom_call_target="tpu_custom_call", output_to_operand_aliasing={{0}: (0, {}), {1}: (1, {}), {2}: (2, {})} | custom-call | flops 6553600 | bytes 2621440 | tf_op jit(solution)/shard_map/pallas_call | solution.py:678
  18.8 13.0 %all_to_all.5 = f32[32,4,128]{2,1,0:T(4,128)S(1)} all-to-all(f32[32,4,128]{2,1,0:T(4,128)S(1)} %bitcast.15), channel_id=1, replica_groups=mesh['gx'=4,'gy'=8] {'gx','gy'}, dimensions={0} | all-to-all | bytes 131072 | tf_op jit(solution)/shard_map/all_to_all | solution.py:691
  31.8 5.6 %shard_map.63 = (f32[512,256]{1,0:T(8,128)}, f32[512,256]{1,0:T(8,128)}) custom-call(f32[4,8,4,128]{3,2,1,0:T(4,128)S(1)} %bitcast.14, f32[8,128]{1,0:T(8,128)S(1)} %get-tuple-element.72.dense_ref, f32[3,72,128]{2,1,0:T(8,128)S(1)} %collective-permute-done.3.from_cross, f32[3,72,128]{2,1,0:T(8,128)S(1)} %collective-permute-done.2.from_pair, ...), custom_call_target="tpu_custom_call" | custom-call | flops 7864320 | bytes 5242880 | tf_op jit(solution)/shard_map/pallas_call | solution.py:692
  (2 shorter events, 0.0 us)
Async XLA Ops:
  1.5 9.6 %collective-permute-start = (f32[3,16,256]{2,1,0:T(8,128)S(1)}, f32[3,16,256]{2,1,0:T(8,128)S(1)}, u32[]{:S(2)}, u32[]{:S(2)}) collective-permute-start(f32[3,16,256]{2,1,0:T(8,128)S(1)} %pad_maximum_fusion), channel_id=1, source_target_pairs={{8,16},{16,8},{9,17},{17,9},{10,18},{18,10},{11,19},{19,11},{12,20... | collective-permute-start | bytes 147464 | tf_op jit(solution)/shard_map/ppermute | solution.py:624
  2.2 8.9 %collective-permute-start.1 = (f32[3,16,256]{2,1,0:T(8,128)S(1)}, f32[3,16,256]{2,1,0:T(8,128)S(1)}, u32[]{:S(2)}, u32[]{:S(2)}) collective-permute-start(f32[3,16,256]{2,1,0:T(8,128)S(1)} %pad_maximum_fusion.1), channel_id=1, source_target_pairs={{0,8},{16,24},{8,0},{24,16},{1,9},{17,25},{9,1},{25,17},{2,10},{18... | collective-permute-start | bytes 147464 | tf_op jit(solution)/shard_map/ppermute | solution.py:624
  11.2 4.8 %collective-permute-start.2 = (f32[3,72,128]{2,1,0:T(8,128)S(1)}, f32[3,72,128]{2,1,0:T(8,128)S(1)}, u32[]{:S(2)}, u32[]{:S(2)}) collective-permute-start(f32[3,72,128]{2,1,0:T(8,128)S(1)} %get-tuple-element.64), channel_id=1, source_target_pairs={{0,1},{2,3},{4,5},{6,7},{1,0},{3,2},{5,4},{7,6},{8,9},{10,11},{12,... | collective-permute-start | bytes 331784 | tf_op jit(solution)/shard_map/ppermute | solution.py:624
  11.3 4.7 %collective-permute-start.3 = (f32[3,72,128]{2,1,0:T(8,128)S(1)}, f32[3,72,128]{2,1,0:T(8,128)S(1)}, u32[]{:S(2)}, u32[]{:S(2)}) collective-permute-start(f32[3,72,128]{2,1,0:T(8,128)S(1)} %get-tuple-element.65), channel_id=1, source_target_pairs={{1,2},{3,4},{5,6},{2,1},{4,3},{6,5},{9,10},{11,12},{13,14},{10,9},... | collective-permute-start | bytes 331784 | tf_op jit(solution)/shard_map/ppermute | solution.py:624

commit v5 on v4

--- a/solution.py
+++ b/solution.py
@@ -562,7 +562,7 @@
                     store_twice(pes[level - 1], start, size, spread(value, step // 2))
 
         if level > 0:
-            for_chunks(height, climb, CHUNK, PART)
+            for_chunks(height, climb, 2 * CHUNK, PART)
 
     def last(base, size):
         body, around = beside_of(body_final, body_state[:2], base, size, 1)
@@ -577,22 +577,26 @@
             ref[span, :LANES] = jnp.where(lane < NEAR, roll(around, -HALO), middle[0])
             ref[span, LANES:] = jnp.where(lane >= LANES - NEAR, roll(around, HALO), middle[1])
 
-    count = rows // CHUNK
-    ends = [0] + [CHUNK * (p + 1) - LAG - TOP for p in range(count - 1)] + [out_ref.shape[0]]
+    size = 2 * CHUNK
+    count = rows // size
+    ends = [0] + [size * (p + 1) - LAG - TOP for p in range(count - 1)] + [out_ref.shape[0]]
 
     def copies(p):
-        size = ends[p + 1] - ends[p]
+        middle = (ends[p] + ends[p + 1]) // 16 * 8
         return [
             pltpu.make_async_copy(
-                outs[k].at[pl.ds(TOP + ends[p], size)], ref.at[pl.ds(ends[p], size)], sems.at[2 * p + k]
+                outs[k].at[pl.ds(TOP + first, last - first)],
+                ref.at[pl.ds(first, last - first)],
+                sems.at[4 * p + 2 * h + k],
             )
+            for h, (first, last) in enumerate(((ends[p], middle), (middle, ends[p + 1])))
             for k, ref in enumerate((out_ref, resid_ref))
         ]
 
     def finish(i, carry):
-        for_parts(i * CHUNK, CHUNK, climb, PART)
-        base = pl.multiple_of(jnp.maximum(i * CHUNK - LAG, 0), 8)
-        for_parts(base, CHUNK, last, PART)
+        for_parts(i * size, size, climb, PART)
+        base = pl.multiple_of(jnp.maximum(i * size - LAG, 0), 8)
+        for_parts(base, size, last, PART)
         for p in range(count):
 
             @pl.when(i == p)

time: 37.7 us -> 37.5 us (level)
  transfers between devices with their start and end apart: 4 -> 4, of which waited for: 0 -> 0; matrix products, arithmetic and copies ran while one was open for 4% -> 5% of each run, Pallas kernels for 14% -> 14%
where the time goes in v5:
time: 37.5 us; the launch traced here: 37.2 us
  Pallas kernels  13.6 us (36%)
  blocking collectives  13 us (35%)
  starting transfers between devices  7.31 us (19%)
  other arithmetic  2.54 us (7%)
  between operations  0.76 us (2%)
    all_to_all x1, blocking collectives, local(): lax.all_to_all(chunks.reshape(nx * ny, 4, LANES), ('gx', 'gy'), 0, 0)  13 us
    ppermute x4, starting transfers between devices, swap(): return lax.ppermute(x, axis, pairs + [(j, i) for i, j in pairs])  7.31 us
    pallas_call x1, Pallas kernels, local(): call(up_kernel, (out(rows, columns), out(rows, columns)), [vmem(3, ring),...  5.41 us
    pallas_call x1, Pallas kernels, local(): call(body_kernel, [out(*shape(2, level)) for level in levels for _ in ran...  4 us
    pallas_call x1, Pallas kernels, local(): call(frame_kernel, [out(*shape(1, 0))] * 3 + [out(*shape(1, level)) for l...  2.77 us
    mul x1, other arithmetic, fields(): return (wet * r, wet * p, wet * (1.0 + 0.5 * c.astype(jnp.float32)))  1.67 us
    pallas_call x1, Pallas kernels, local(): call(layout_kernel, laid_out, inner, 10 * cells, 10 * cells)  1.27 us
    another operation x3, other arithmetic, edge(): jnp.stack(fields(*(lax.dynamic_slice_in_dim(x, start, TOP, axis=0) for x...  0.87 us
  transfers between devices with their start and end apart: 4, of which 0 were waited for; matrix products, arithmetic and copies ran while one was open for 5% of the time, Pallas kernels for 14%

profile of v5, /device:TPU:0, one launch (start us, length us, event | category | flops | bytes accessed | tf_op | source)
XLA Modules:
  0.0 37.2 jit_solution(7118588451449525112)
XLA Ops:
  0.6 0.9 %multiply_bitcast_fusion.2 = (f32[1,16,256]{2,1,0:T(8,128)S(1)}, f32[1,16,256]{2,1,0:T(8,128)S(1)}, f32[1,16,256]{2,1,0:T(8,128)S(1)}, f32[1,16,256]{2,1,0:T(8,1...) fusion(f32[512,256]{1,0:T(8,128)} %param.4, s32[]{:T(128)S(6)} %select_n.24, s32[512,256]{1,0:T(8,128)} %param.6, ...), kind=kLoop, calls=%fused_computation.7 | loop fusion | flops 57344 | bytes 229384 | tf_op jit(solution)/shard_map/stack | solution.py:653
  1.5 0.7 %collective-permute-start = (f32[3,16,256]{2,1,0:T(8,128)S(1)}, f32[3,16,256]{2,1,0:T(8,128)S(1)}, u32[]{:S(2)}, u32[]{:S(2)}) collective-permute-start(f32[3,16,256]{2,1,0:T(8,128)S(1)} %pad_maximum_fusion), channel_id=1, source_target_pairs={{8,16},{16,8},{9,17},{17,9},{10,18},{18,10},{11,19},{19,11},{12,20... | collective-permute-start | bytes 147464 | tf_op jit(solution)/shard_map/ppermute | solution.py:628
  2.2 5.9 %collective-permute-start.1 = (f32[3,16,256]{2,1,0:T(8,128)S(1)}, f32[3,16,256]{2,1,0:T(8,128)S(1)}, u32[]{:S(2)}, u32[]{:S(2)}) collective-permute-start(f32[3,16,256]{2,1,0:T(8,128)S(1)} %pad_maximum_fusion.1), channel_id=1, source_target_pairs={{0,8},{16,24},{8,0},{24,16},{1,9},{17,25},{9,1},{25,17},{2,10},{18... | collective-permute-start | bytes 147464 | tf_op jit(solution)/shard_map/ppermute | solution.py:628
  8.1 1.7 %add_multiply_fusion = (f32[512,256]{1,0:T(8,128)S(1)}, f32[512,256]{1,0:T(8,128)S(1)}, f32[512,256]{1,0:T(8,128)S(1)}) fusion(s32[512,256]{1,0:T(8,128)} %param.7, s32[512,256]{1,0:T(8,128)} %param.6, f32[512,256]{1,0:T(8,128)} %param.5, f32[512,256]{1,0:T(8,128)} %param.4), kind=kLoop, calls=%fused_computation | loop fusion | flops 917504 | bytes 3670016 | tf_op jit(solution)/shard_map/mul | solution.py:648
  9.8 1.3 %shard_map.59 = (f32[2,560,128]{2,1,0:T(8,128)S(1)}, f32[2,560,128]{2,1,0:T(8,128)S(1)}, f32[2,560,128]{2,1,0:T(8,128)S(1)}, f32[1,560,128]{2,1,0:T(8,128)S(1)},...) custom-call(f32[512,256]{1,0:T(8,128)S(1)} %get-tuple-element.116.so, ...), custom_call_target="tpu_custom_call" | custom-call | flops 1310720 | bytes 1310720 | tf_op jit(solution)/shard_map/pallas_call | solution.py:662
  11.1 0.0 collective-permute-done.refs_8_
  11.1 0.0 collective-permute-done.1.refs_9_
  11.1 0.1 shard_map.60
  11.2 0.1 collective-permute-start.2
  11.3 0.7 %collective-permute-start.3 = (f32[3,72,128]{2,1,0:T(8,128)S(1)}, f32[3,72,128]{2,1,0:T(8,128)S(1)}, u32[]{:S(2)}, u32[]{:S(2)}) collective-permute-start(f32[3,72,128]{2,1,0:T(8,128)S(1)} %get-tuple-element.65), channel_id=1, source_target_pairs={{1,2},{3,4},{5,6},{2,1},{4,3},{6,5},{9,10},{11,12},{13,14},{10,9},... | collective-permute-start | bytes 331784 | tf_op jit(solution)/shard_map/ppermute | solution.py:628
  12.0 4.0 %shard_map.61 = (f32[2,560,128]{2,1,0:T(8,128)S(1)}, f32[2,560,128]{2,1,0:T(8,128)S(1)}, f32[2,560,128]{2,1,0:T(8,128)S(1)}, f32[2,560,128]{2,1,0:T(8,128)S(1)},...) custom-call(f32[2,560,128]{2,1,0:T(8,128)S(1)} %get-tuple-element.66, ...), custom_call_target="tpu_custom_call" | custom-call | flops 13107200 | bytes 5242880 | tf_op jit(solution)/shard_map/pallas_call | solution.py:671
  16.0 0.0 collective-permute-done.2.from_pair
  16.0 0.0 collective-permute-done.3.from_cross
  16.0 2.8 %shard_map.62 = (f32[1,560,128]{2,1,0:T(8,128)S(1)}, f32[1,560,128]{2,1,0:T(8,128)S(1)}, f32[1,560,128]{2,1,0:T(8,128)S(1)}, f32[1,560,128]{2,1,0:T(8,128)S(1)},...) custom-call(f32[1,560,128]{2,1,0:T(8,128)S(1)} %get-tuple-element.61, ...), custom_call_target="tpu_custom_call", output_to_operand_aliasing={{0}: (0, {}), {1}: (1, {}), {2}: (2, {})} | custom-call | flops 6553600 | bytes 2621440 | tf_op jit(solution)/shard_map/pallas_call | solution.py:682
  18.8 13.0 %all_to_all.5 = f32[32,4,128]{2,1,0:T(4,128)S(1)} all-to-all(f32[32,4,128]{2,1,0:T(4,128)S(1)} %bitcast.15), channel_id=1, replica_groups=mesh['gx'=4,'gy'=8] {'gx','gy'}, dimensions={0} | all-to-all | bytes 131072 | tf_op jit(solution)/shard_map/all_to_all | solution.py:695
  31.8 5.4 %shard_map.63 = (f32[512,256]{1,0:T(8,128)}, f32[512,256]{1,0:T(8,128)}) custom-call(f32[4,8,4,128]{3,2,1,0:T(4,128)S(1)} %bitcast.14, f32[8,128]{1,0:T(8,128)S(1)} %get-tuple-element.72.dense_ref, f32[3,72,128]{2,1,0:T(8,128)S(1)} %collective-permute-done.3.from_cross, f32[3,72,128]{2,1,0:T(8,128)S(1)} %collective-permute-done.2.from_pair, ...), custom_call_target="tpu_custom_call" | custom-call | flops 7864320 | bytes 5242880 | tf_op jit(solution)/shard_map/pallas_call | solution.py:696
  (2 shorter events, 0.0 us)
Async XLA Ops:
  1.5 9.6 %collective-permute-start = (f32[3,16,256]{2,1,0:T(8,128)S(1)}, f32[3,16,256]{2,1,0:T(8,128)S(1)}, u32[]{:S(2)}, u32[]{:S(2)}) collective-permute-start(f32[3,16,256]{2,1,0:T(8,128)S(1)} %pad_maximum_fusion), channel_id=1, source_target_pairs={{8,16},{16,8},{9,17},{17,9},{10,18},{18,10},{11,19},{19,11},{12,20... | collective-permute-start | bytes 147464 | tf_op jit(solution)/shard_map/ppermute | solution.py:628
  2.2 8.9 %collective-permute-start.1 = (f32[3,16,256]{2,1,0:T(8,128)S(1)}, f32[3,16,256]{2,1,0:T(8,128)S(1)}, u32[]{:S(2)}, u32[]{:S(2)}) collective-permute-start(f32[3,16,256]{2,1,0:T(8,128)S(1)} %pad_maximum_fusion.1), channel_id=1, source_target_pairs={{0,8},{16,24},{8,0},{24,16},{1,9},{17,25},{9,1},{25,17},{2,10},{18... | collective-permute-start | bytes 147464 | tf_op jit(solution)/shard_map/ppermute | solution.py:628
  11.2 4.8 %collective-permute-start.2 = (f32[3,72,128]{2,1,0:T(8,128)S(1)}, f32[3,72,128]{2,1,0:T(8,128)S(1)}, u32[]{:S(2)}, u32[]{:S(2)}) collective-permute-start(f32[3,72,128]{2,1,0:T(8,128)S(1)} %get-tuple-element.64), channel_id=1, source_target_pairs={{0,1},{2,3},{4,5},{6,7},{1,0},{3,2},{5,4},{7,6},{8,9},{10,11},{12,... | collective-permute-start | bytes 331784 | tf_op jit(solution)/shard_map/ppermute | solution.py:628
  11.3 4.7 %collective-permute-start.3 = (f32[3,72,128]{2,1,0:T(8,128)S(1)}, f32[3,72,128]{2,1,0:T(8,128)S(1)}, u32[]{:S(2)}, u32[]{:S(2)}) collective-permute-start(f32[3,72,128]{2,1,0:T(8,128)S(1)} %get-tuple-element.65), channel_id=1, source_target_pairs={{1,2},{3,4},{5,6},{2,1},{4,3},{6,5},{9,10},{11,12},{13,14},{10,9},... | collective-permute-start | bytes 331784 | tf_op jit(solution)/shard_map/ppermute | solution.py:628

commit v6 on v5

--- a/solution.py
+++ b/solution.py
@@ -286,7 +286,7 @@
     sources = (source, *inner[depth : 2 * depth], last_source)
     diagonal = (first_diagonal, *inner[2 * depth :])
     weights[0][...] = weight[...]
-    descend_all(rows, sources, guess, weights, states, diagonal, field, resid, CHUNK, CHUNK)
+    descend_all(rows, sources, guess, weights, states, diagonal, field, resid, 2 * CHUNK, CHUNK)
 
 
 def frame_kernel(_a, _b, _c, from_pair, from_cross, body_weight, body_source, *refs):
@@ -316,7 +316,7 @@
             lane = lane_of(both)
             outside = (lane < HALO) | (lane >= LANES - HALO)
             frame[0, span, :] = jnp.where(outside, both, frame[0, span, :])
-    descend_all(rows, sources, frame_guess, weights, states, diagonals, field, resid, 2 * CHUNK, 2 * CHUNK)
+    descend_all(rows, sources, frame_guess, weights, states, diagonals, field, resid, 4 * CHUNK, 2 * CHUNK)
 
     level = LEVELS - 1
     step, halo, height = 2**level, TOP >> level, rows >> level
@@ -491,14 +491,13 @@
     c_west, c_east, c_north, c_south = (scale * c for c in (c_west, c_east, c_north, c_south))
     e_ref[GUARD : GUARD + tall, :] = first
 
-    def sweep(_, carry):
-        e = shifted(0)
-        around = (c_west * roll(e, 1) + c_east * roll(e, -1)) + (c_north * shifted(-1) + c_south * shifted(1))
-        e_ref[GUARD : GUARD + tall, :] = ((1.0 - relaxation) * e + first) + around
-        return carry
-
-    lax.fori_loop(0, SWEEPS - 1, sweep, 0)
-    return shifted(0)
+    def sweep(_, e):
+        own = ((1.0 - relaxation) * e + first) + (c_north * shifted(-1) + c_south * shifted(1))
+        e = (own + c_west * roll(e, 1)) + c_east * roll(e, -1)
+        e_ref[GUARD : GUARD + tall, :] = e
+        return e
+
+    return lax.fori_loop(0, SWEEPS - 1, sweep, first)
 
 
 def up_kernel(all_ref, dense_ref, from_cross, from_pair, own_source, frame_source, own_diagonal, frame_diagonal, *refs):

time: 37.5 us -> 37.1 us (0.989)
  Pallas kernels: 13.6 us -> 12.6 us
  blocking collectives: 13 us -> 13.5 us
    pallas_call x1, Pallas kernels: 4 us -> 3.49 us  [local(): call(body_kernel, [out(*shape(2, level)) for level in levels for _ in ran...]
    all_to_all x1, blocking collectives: 13 us -> 13.5 us  [local(): lax.all_to_all(chunks.reshape(nx * ny, 4, LANES), ('gx', 'gy'), 0, 0)]
    pallas_call x1, Pallas kernels: 2.77 us -> 2.38 us  [local(): call(frame_kernel, [out(*shape(1, 0))] * 3 + [out(*shape(1, level)) for l...]
  transfers between devices with their start and end apart: 4 -> 4, of which waited for: 0 -> 0; matrix products, arithmetic and copies ran while one was open for 5% -> 5% of each run, Pallas kernels for 14% -> 13%
where the time goes in v6:
time: 37.1 us; the launch traced here: 36.8 us
  blocking collectives  13.5 us (36%)
  Pallas kernels  12.6 us (34%)
  starting transfers between devices  7.31 us (20%)
  other arithmetic  2.54 us (7%)
  between operations  0.75 us (2%)
    all_to_all x1, blocking collectives, local(): lax.all_to_all(chunks.reshape(nx * ny, 4, LANES), ('gx', 'gy'), 0, 0)  13.5 us
    ppermute x4, starting transfers between devices, swap(): return lax.ppermute(x, axis, pairs + [(j, i) for i, j in pairs])  7.31 us
    pallas_call x1, Pallas kernels, local(): call(up_kernel, (out(rows, columns), out(rows, columns)), [vmem(3, ring),...  5.36 us
    pallas_call x1, Pallas kernels, local(): call(body_kernel, [out(*shape(2, level)) for level in levels for _ in ran...  3.49 us
    pallas_call x1, Pallas kernels, local(): call(frame_kernel, [out(*shape(1, 0))] * 3 + [out(*shape(1, level)) for l...  2.38 us
    mul x1, other arithmetic, fields(): return (wet * r, wet * p, wet * (1.0 + 0.5 * c.astype(jnp.float32)))  1.67 us
    pallas_call x1, Pallas kernels, local(): call(layout_kernel, laid_out, inner, 10 * cells, 10 * cells)  1.27 us
    another operation x3, other arithmetic, edge(): jnp.stack(fields(*(lax.dynamic_slice_in_dim(x, start, TOP, axis=0) for x...  0.87 us
  transfers between devices with their start and end apart: 4, of which 0 were waited for; matrix products, arithmetic and copies ran while one was open for 5% of the time, Pallas kernels for 13%

profile of v6, /device:TPU:0, one launch (start us, length us, event | category | flops | bytes accessed | tf_op | source)
XLA Modules:
  0.0 36.8 jit_solution(13336603746192981853)
XLA Ops:
  0.6 0.9 %multiply_bitcast_fusion.2 = (f32[1,16,256]{2,1,0:T(8,128)S(1)}, f32[1,16,256]{2,1,0:T(8,128)S(1)}, f32[1,16,256]{2,1,0:T(8,128)S(1)}, f32[1,16,256]{2,1,0:T(8,1...) fusion(f32[512,256]{1,0:T(8,128)} %param.4, s32[]{:T(128)S(6)} %select_n.24, s32[512,256]{1,0:T(8,128)} %param.6, ...), kind=kLoop, calls=%fused_computation.7 | loop fusion | flops 57344 | bytes 229384 | tf_op jit(solution)/shard_map/stack | solution.py:652
  1.5 0.7 %collective-permute-start = (f32[3,16,256]{2,1,0:T(8,128)S(1)}, f32[3,16,256]{2,1,0:T(8,128)S(1)}, u32[]{:S(2)}, u32[]{:S(2)}) collective-permute-start(f32[3,16,256]{2,1,0:T(8,128)S(1)} %pad_maximum_fusion), channel_id=1, source_target_pairs={{8,16},{16,8},{9,17},{17,9},{10,18},{18,10},{11,19},{19,11},{12,20... | collective-permute-start | bytes 147464 | tf_op jit(solution)/shard_map/ppermute | solution.py:627
  2.2 5.9 %collective-permute-start.1 = (f32[3,16,256]{2,1,0:T(8,128)S(1)}, f32[3,16,256]{2,1,0:T(8,128)S(1)}, u32[]{:S(2)}, u32[]{:S(2)}) collective-permute-start(f32[3,16,256]{2,1,0:T(8,128)S(1)} %pad_maximum_fusion.1), channel_id=1, source_target_pairs={{0,8},{16,24},{8,0},{24,16},{1,9},{17,25},{9,1},{25,17},{2,10},{18... | collective-permute-start | bytes 147464 | tf_op jit(solution)/shard_map/ppermute | solution.py:627
  8.1 1.7 %add_multiply_fusion = (f32[512,256]{1,0:T(8,128)S(1)}, f32[512,256]{1,0:T(8,128)S(1)}, f32[512,256]{1,0:T(8,128)S(1)}) fusion(s32[512,256]{1,0:T(8,128)} %param.7, s32[512,256]{1,0:T(8,128)} %param.6, f32[512,256]{1,0:T(8,128)} %param.5, f32[512,256]{1,0:T(8,128)} %param.4), kind=kLoop, calls=%fused_computation | loop fusion | flops 917504 | bytes 3670016 | tf_op jit(solution)/shard_map/mul | solution.py:647
  9.8 1.3 %shard_map.59 = (f32[2,560,128]{2,1,0:T(8,128)S(1)}, f32[2,560,128]{2,1,0:T(8,128)S(1)}, f32[2,560,128]{2,1,0:T(8,128)S(1)}, f32[1,560,128]{2,1,0:T(8,128)S(1)},...) custom-call(f32[512,256]{1,0:T(8,128)S(1)} %get-tuple-element.116.so, ...), custom_call_target="tpu_custom_call" | custom-call | flops 1310720 | bytes 1310720 | tf_op jit(solution)/shard_map/pallas_call | solution.py:661
  11.1 0.0 collective-permute-done.refs_8_
  11.1 0.0 collective-permute-done.1.refs_9_
  11.1 0.1 shard_map.60
  11.2 0.1 collective-permute-start.2
  11.3 0.7 %collective-permute-start.3 = (f32[3,72,128]{2,1,0:T(8,128)S(1)}, f32[3,72,128]{2,1,0:T(8,128)S(1)}, u32[]{:S(2)}, u32[]{:S(2)}) collective-permute-start(f32[3,72,128]{2,1,0:T(8,128)S(1)} %get-tuple-element.65), channel_id=1, source_target_pairs={{1,2},{3,4},{5,6},{2,1},{4,3},{6,5},{9,10},{11,12},{13,14},{10,9},... | collective-permute-start | bytes 331784 | tf_op jit(solution)/shard_map/ppermute | solution.py:627
  12.0 3.5 %shard_map.61 = (f32[2,560,128]{2,1,0:T(8,128)S(1)}, f32[2,560,128]{2,1,0:T(8,128)S(1)}, f32[2,560,128]{2,1,0:T(8,128)S(1)}, f32[2,560,128]{2,1,0:T(8,128)S(1)},...) custom-call(f32[2,560,128]{2,1,0:T(8,128)S(1)} %get-tuple-element.66, ...), custom_call_target="tpu_custom_call" | custom-call | flops 13107200 | bytes 5242880 | tf_op jit(solution)/shard_map/pallas_call | solution.py:670
  15.5 0.0 collective-permute-done.2.from_pair
  15.5 0.0 collective-permute-done.3.from_cross
  15.5 2.4 %shard_map.62 = (f32[1,560,128]{2,1,0:T(8,128)S(1)}, f32[1,560,128]{2,1,0:T(8,128)S(1)}, f32[1,560,128]{2,1,0:T(8,128)S(1)}, f32[1,560,128]{2,1,0:T(8,128)S(1)},...) custom-call(f32[1,560,128]{2,1,0:T(8,128)S(1)} %get-tuple-element.61, ...), custom_call_target="tpu_custom_call", output_to_operand_aliasing={{0}: (0, {}), {1}: (1, {}), {2}: (2, {})} | custom-call | flops 6553600 | bytes 2621440 | tf_op jit(solution)/shard_map/pallas_call | solution.py:681
  17.9 13.5 %all_to_all.5 = f32[32,4,128]{2,1,0:T(4,128)S(1)} all-to-all(f32[32,4,128]{2,1,0:T(4,128)S(1)} %bitcast.15), channel_id=1, replica_groups=mesh['gx'=4,'gy'=8] {'gx','gy'}, dimensions={0} | all-to-all | bytes 131072 | tf_op jit(solution)/shard_map/all_to_all | solution.py:694
  31.4 5.4 %shard_map.63 = (f32[512,256]{1,0:T(8,128)}, f32[512,256]{1,0:T(8,128)}) custom-call(f32[4,8,4,128]{3,2,1,0:T(4,128)S(1)} %bitcast.14, f32[8,128]{1,0:T(8,128)S(1)} %get-tuple-element.72.dense_ref, f32[3,72,128]{2,1,0:T(8,128)S(1)} %collective-permute-done.3.from_cross, f32[3,72,128]{2,1,0:T(8,128)S(1)} %collective-permute-done.2.from_pair, ...), custom_call_target="tpu_custom_call" | custom-call | flops 7864320 | bytes 5242880 | tf_op jit(solution)/shard_map/pallas_call | solution.py:695
  (2 shorter events, 0.0 us)
Async XLA Ops:
  1.5 9.6 %collective-permute-start = (f32[3,16,256]{2,1,0:T(8,128)S(1)}, f32[3,16,256]{2,1,0:T(8,128)S(1)}, u32[]{:S(2)}, u32[]{:S(2)}) collective-permute-start(f32[3,16,256]{2,1,0:T(8,128)S(1)} %pad_maximum_fusion), channel_id=1, source_target_pairs={{8,16},{16,8},{9,17},{17,9},{10,18},{18,10},{11,19},{19,11},{12,20... | collective-permute-start | bytes 147464 | tf_op jit(solution)/shard_map/ppermute | solution.py:627
  2.2 8.9 %collective-permute-start.1 = (f32[3,16,256]{2,1,0:T(8,128)S(1)}, f32[3,16,256]{2,1,0:T(8,128)S(1)}, u32[]{:S(2)}, u32[]{:S(2)}) collective-permute-start(f32[3,16,256]{2,1,0:T(8,128)S(1)} %pad_maximum_fusion.1), channel_id=1, source_target_pairs={{0,8},{16,24},{8,0},{24,16},{1,9},{17,25},{9,1},{25,17},{2,10},{18... | collective-permute-start | bytes 147464 | tf_op jit(solution)/shard_map/ppermute | solution.py:627
  11.2 4.3 %collective-permute-start.2 = (f32[3,72,128]{2,1,0:T(8,128)S(1)}, f32[3,72,128]{2,1,0:T(8,128)S(1)}, u32[]{:S(2)}, u32[]{:S(2)}) collective-permute-start(f32[3,72,128]{2,1,0:T(8,128)S(1)} %get-tuple-element.64), channel_id=1, source_target_pairs={{0,1},{2,3},{4,5},{6,7},{1,0},{3,2},{5,4},{7,6},{8,9},{10,11},{12,... | collective-permute-start | bytes 331784 | tf_op jit(solution)/shard_map/ppermute | solution.py:627
  11.3 4.2 %collective-permute-start.3 = (f32[3,72,128]{2,1,0:T(8,128)S(1)}, f32[3,72,128]{2,1,0:T(8,128)S(1)}, u32[]{:S(2)}, u32[]{:S(2)}) collective-permute-start(f32[3,72,128]{2,1,0:T(8,128)S(1)} %get-tuple-element.65), channel_id=1, source_target_pairs={{1,2},{3,4},{5,6},{2,1},{4,3},{6,5},{9,10},{11,12},{13,14},{10,9},... | collective-permute-start | bytes 331784 | tf_op jit(solution)/shard_map/ppermute | solution.py:627

commit v7 on v5

--- a/solution.py
+++ b/solution.py
@@ -286,7 +286,7 @@
     sources = (source, *inner[depth : 2 * depth], last_source)
     diagonal = (first_diagonal, *inner[2 * depth :])
     weights[0][...] = weight[...]
-    descend_all(rows, sources, guess, weights, states, diagonal, field, resid, CHUNK, CHUNK)
+    descend_all(rows, sources, guess, weights, states, diagonal, field, resid, 2 * CHUNK, CHUNK)
 
 
 def frame_kernel(_a, _b, _c, from_pair, from_cross, body_weight, body_source, *refs):
@@ -316,7 +316,7 @@
             lane = lane_of(both)
             outside = (lane < HALO) | (lane >= LANES - HALO)
             frame[0, span, :] = jnp.where(outside, both, frame[0, span, :])
-    descend_all(rows, sources, frame_guess, weights, states, diagonals, field, resid, 2 * CHUNK, 2 * CHUNK)
+    descend_all(rows, sources, frame_guess, weights, states, diagonals, field, resid, 4 * CHUNK, 2 * CHUNK)
 
     level = LEVELS - 1
     step, halo, height = 2**level, TOP >> level, rows >> level
@@ -577,9 +577,8 @@
             ref[span, :LANES] = jnp.where(lane < NEAR, roll(around, -HALO), middle[0])
             ref[span, LANES:] = jnp.where(lane >= LANES - NEAR, roll(around, HALO), middle[1])
 
-    size = 2 * CHUNK
-    count = rows // size
-    ends = [0] + [size * (p + 1) - LAG - TOP for p in range(count - 1)] + [out_ref.shape[0]]
+    count = rows // CHUNK
+    ends = [0] + [CHUNK * (p + 1) - LAG - TOP for p in range(count - 1)] + [out_ref.shape[0]]
 
     def copies(p):
         middle = (ends[p] + ends[p + 1]) // 16 * 8
@@ -593,20 +592,11 @@
             for k, ref in enumerate((out_ref, resid_ref))
         ]
 
-    def finish(i, carry):
-        for_parts(i * size, size, climb, PART)
-        base = pl.multiple_of(jnp.maximum(i * size - LAG, 0), 8)
-        for_parts(base, size, last, PART)
-        for p in range(count):
-
-            @pl.when(i == p)
-            def _(p=p):
-                for copy in copies(p):
-                    copy.start()
-
-        return carry
-
-    lax.fori_loop(0, count, finish, 0)
+    for p in range(count):
+        climb(p * CHUNK, CHUNK)
+        last(max(p * CHUNK - LAG, 0), CHUNK)
+        for copy in copies(p):
+            copy.start()
     for p in range(count):
         for copy in copies(p):
             copy.wait()
@@ -696,7 +686,7 @@
     return call(
         up_kernel,
         (out(rows, columns), out(rows, columns)),
-        [vmem(3, ring), vmem(2, 0), vmem(1, 0), pltpu.SemaphoreType.DMA((8,))]
+        [vmem(3, ring), vmem(2, 0), vmem(1, 0), pltpu.SemaphoreType.DMA((16,))]
         + [pltpu.VMEM(((rows >> LEVELS) + 2 * TALL + 2 * GUARD, LANES), jnp.float32), vmem(3, ring)]
         + [pltpu.VMEM((total, columns), jnp.float32)] * 2
         + [vmem(2, level) for level in levels]

time: 37.5 us -> 37 us (0.987)
  Pallas kernels: 13.6 us -> 12.6 us
  blocking collectives: 13 us -> 13.5 us
    pallas_call x1, Pallas kernels: 4 us -> 3.49 us  [local(): call(body_kernel, [out(*shape(2, level)) for level in levels for _ in ran...]
    all_to_all x1, blocking collectives: 13 us -> 13.5 us  [local(): lax.all_to_all(chunks.reshape(nx * ny, 4, LANES), ('gx', 'gy'), 0, 0)]
    pallas_call x1, Pallas kernels: 2.77 us -> 2.38 us  [local(): call(frame_kernel, [out(*shape(1, 0))] * 3 + [out(*shape(1, level)) for l...]
  transfers between devices with their start and end apart: 4 -> 4, of which waited for: 0 -> 0; matrix products, arithmetic and copies ran while one was open for 5% -> 5% of each run, Pallas kernels for 14% -> 13%
where the time goes in v7:
time: 37 us; the launch traced here: 36.7 us
  blocking collectives  13.5 us (36%)
  Pallas kernels  12.6 us (34%)
  starting transfers between devices  7.31 us (20%)
  other arithmetic  2.54 us (7%)
  between operations  0.75 us (2%)
    all_to_all x1, blocking collectives, local(): lax.all_to_all(chunks.reshape(nx * ny, 4, LANES), ('gx', 'gy'), 0, 0)  13.5 us
    ppermute x4, starting transfers between devices, swap(): return lax.ppermute(x, axis, pairs + [(j, i) for i, j in pairs])  7.31 us
    pallas_call x1, Pallas kernels, local(): call(up_kernel, (out(rows, columns), out(rows, columns)), [vmem(3, ring),...  5.31 us
    pallas_call x1, Pallas kernels, local(): call(body_kernel, [out(*shape(2, level)) for level in levels for _ in ran...  3.49 us
    pallas_call x1, Pallas kernels, local(): call(frame_kernel, [out(*shape(1, 0))] * 3 + [out(*shape(1, level)) for l...  2.38 us
    mul x1, other arithmetic, fields(): return (wet * r, wet * p, wet * (1.0 + 0.5 * c.astype(jnp.float32)))  1.67 us
    pallas_call x1, Pallas kernels, local(): call(layout_kernel, laid_out, inner, 10 * cells, 10 * cells)  1.27 us
    another operation x3, other arithmetic, edge(): jnp.stack(fields(*(lax.dynamic_slice_in_dim(x, start, TOP, axis=0) for x...  0.87 us
  transfers between devices with their start and end apart: 4, of which 0 were waited for; matrix products, arithmetic and copies ran while one was open for 5% of the time, Pallas kernels for 13%

profile of v7, /device:TPU:0, one launch (start us, length us, event | category | flops | bytes accessed | tf_op | source)
XLA Modules:
  0.0 36.7 jit_solution(1424445459995524917)
XLA Ops:
  0.6 0.9 %multiply_bitcast_fusion.2 = (f32[1,16,256]{2,1,0:T(8,128)S(1)}, f32[1,16,256]{2,1,0:T(8,128)S(1)}, f32[1,16,256]{2,1,0:T(8,128)S(1)}, f32[1,16,256]{2,1,0:T(8,1...) fusion(f32[512,256]{1,0:T(8,128)} %param.4, s32[]{:T(128)S(6)} %select_n.24, s32[512,256]{1,0:T(8,128)} %param.6, ...), kind=kLoop, calls=%fused_computation.7 | loop fusion | flops 57344 | bytes 229384 | tf_op jit(solution)/shard_map/stack | solution.py:643
  1.5 0.7 %collective-permute-start = (f32[3,16,256]{2,1,0:T(8,128)S(1)}, f32[3,16,256]{2,1,0:T(8,128)S(1)}, u32[]{:S(2)}, u32[]{:S(2)}) collective-permute-start(f32[3,16,256]{2,1,0:T(8,128)S(1)} %pad_maximum_fusion), channel_id=1, source_target_pairs={{8,16},{16,8},{9,17},{17,9},{10,18},{18,10},{11,19},{19,11},{12,20... | collective-permute-start | bytes 147464 | tf_op jit(solution)/shard_map/ppermute | solution.py:618
  2.2 5.9 %collective-permute-start.1 = (f32[3,16,256]{2,1,0:T(8,128)S(1)}, f32[3,16,256]{2,1,0:T(8,128)S(1)}, u32[]{:S(2)}, u32[]{:S(2)}) collective-permute-start(f32[3,16,256]{2,1,0:T(8,128)S(1)} %pad_maximum_fusion.1), channel_id=1, source_target_pairs={{0,8},{16,24},{8,0},{24,16},{1,9},{17,25},{9,1},{25,17},{2,10},{18... | collective-permute-start | bytes 147464 | tf_op jit(solution)/shard_map/ppermute | solution.py:618
  8.1 1.7 %add_multiply_fusion = (f32[512,256]{1,0:T(8,128)S(1)}, f32[512,256]{1,0:T(8,128)S(1)}, f32[512,256]{1,0:T(8,128)S(1)}) fusion(s32[512,256]{1,0:T(8,128)} %param.7, s32[512,256]{1,0:T(8,128)} %param.6, f32[512,256]{1,0:T(8,128)} %param.5, f32[512,256]{1,0:T(8,128)} %param.4), kind=kLoop, calls=%fused_computation | loop fusion | flops 917504 | bytes 3670016 | tf_op jit(solution)/shard_map/mul | solution.py:638
  9.8 1.3 %shard_map.59 = (f32[2,560,128]{2,1,0:T(8,128)S(1)}, f32[2,560,128]{2,1,0:T(8,128)S(1)}, f32[2,560,128]{2,1,0:T(8,128)S(1)}, f32[1,560,128]{2,1,0:T(8,128)S(1)},...) custom-call(f32[512,256]{1,0:T(8,128)S(1)} %get-tuple-element.116.so, ...), custom_call_target="tpu_custom_call" | custom-call | flops 1310720 | bytes 1310720 | tf_op jit(solution)/shard_map/pallas_call | solution.py:652
  11.1 0.0 collective-permute-done.refs_8_
  11.1 0.0 collective-permute-done.1.refs_9_
  11.1 0.1 shard_map.60
  11.2 0.1 collective-permute-start.2
  11.3 0.7 %collective-permute-start.3 = (f32[3,72,128]{2,1,0:T(8,128)S(1)}, f32[3,72,128]{2,1,0:T(8,128)S(1)}, u32[]{:S(2)}, u32[]{:S(2)}) collective-permute-start(f32[3,72,128]{2,1,0:T(8,128)S(1)} %get-tuple-element.65), channel_id=1, source_target_pairs={{1,2},{3,4},{5,6},{2,1},{4,3},{6,5},{9,10},{11,12},{13,14},{10,9},... | collective-permute-start | bytes 331784 | tf_op jit(solution)/shard_map/ppermute | solution.py:618
  12.0 3.5 %shard_map.61 = (f32[2,560,128]{2,1,0:T(8,128)S(1)}, f32[2,560,128]{2,1,0:T(8,128)S(1)}, f32[2,560,128]{2,1,0:T(8,128)S(1)}, f32[2,560,128]{2,1,0:T(8,128)S(1)},...) custom-call(f32[2,560,128]{2,1,0:T(8,128)S(1)} %get-tuple-element.66, ...), custom_call_target="tpu_custom_call" | custom-call | flops 13107200 | bytes 5242880 | tf_op jit(solution)/shard_map/pallas_call | solution.py:661
  15.5 0.0 collective-permute-done.2.from_pair
  15.5 0.0 collective-permute-done.3.from_cross
  15.5 2.4 %shard_map.62 = (f32[1,560,128]{2,1,0:T(8,128)S(1)}, f32[1,560,128]{2,1,0:T(8,128)S(1)}, f32[1,560,128]{2,1,0:T(8,128)S(1)}, f32[1,560,128]{2,1,0:T(8,128)S(1)},...) custom-call(f32[1,560,128]{2,1,0:T(8,128)S(1)} %get-tuple-element.61, ...), custom_call_target="tpu_custom_call", output_to_operand_aliasing={{0}: (0, {}), {1}: (1, {}), {2}: (2, {})} | custom-call | flops 6553600 | bytes 2621440 | tf_op jit(solution)/shard_map/pallas_call | solution.py:672
  17.9 13.5 %all_to_all.5 = f32[32,4,128]{2,1,0:T(4,128)S(1)} all-to-all(f32[32,4,128]{2,1,0:T(4,128)S(1)} %bitcast.15), channel_id=1, replica_groups=mesh['gx'=4,'gy'=8] {'gx','gy'}, dimensions={0} | all-to-all | bytes 131072 | tf_op jit(solution)/shard_map/all_to_all | solution.py:685
  31.4 5.3 %shard_map.63 = (f32[512,256]{1,0:T(8,128)}, f32[512,256]{1,0:T(8,128)}) custom-call(f32[4,8,4,128]{3,2,1,0:T(4,128)S(1)} %bitcast.14, f32[8,128]{1,0:T(8,128)S(1)} %get-tuple-element.72.dense_ref, f32[3,72,128]{2,1,0:T(8,128)S(1)} %collective-permute-done.3.from_cross, f32[3,72,128]{2,1,0:T(8,128)S(1)} %collective-permute-done.2.from_pair, ...), custom_call_target="tpu_custom_call" | custom-call | flops 7864320 | bytes 5242880 | tf_op jit(solution)/shard_map/pallas_call | solution.py:686
  (2 shorter events, 0.0 us)
Async XLA Ops:
  1.5 9.6 %collective-permute-start = (f32[3,16,256]{2,1,0:T(8,128)S(1)}, f32[3,16,256]{2,1,0:T(8,128)S(1)}, u32[]{:S(2)}, u32[]{:S(2)}) collective-permute-start(f32[3,16,256]{2,1,0:T(8,128)S(1)} %pad_maximum_fusion), channel_id=1, source_target_pairs={{8,16},{16,8},{9,17},{17,9},{10,18},{18,10},{11,19},{19,11},{12,20... | collective-permute-start | bytes 147464 | tf_op jit(solution)/shard_map/ppermute | solution.py:618
  2.2 8.9 %collective-permute-start.1 = (f32[3,16,256]{2,1,0:T(8,128)S(1)}, f32[3,16,256]{2,1,0:T(8,128)S(1)}, u32[]{:S(2)}, u32[]{:S(2)}) collective-permute-start(f32[3,16,256]{2,1,0:T(8,128)S(1)} %pad_maximum_fusion.1), channel_id=1, source_target_pairs={{0,8},{16,24},{8,0},{24,16},{1,9},{17,25},{9,1},{25,17},{2,10},{18... | collective-permute-start | bytes 147464 | tf_op jit(solution)/shard_map/ppermute | solution.py:618
  11.2 4.3 %collective-permute-start.2 = (f32[3,72,128]{2,1,0:T(8,128)S(1)}, f32[3,72,128]{2,1,0:T(8,128)S(1)}, u32[]{:S(2)}, u32[]{:S(2)}) collective-permute-start(f32[3,72,128]{2,1,0:T(8,128)S(1)} %get-tuple-element.64), channel_id=1, source_target_pairs={{0,1},{2,3},{4,5},{6,7},{1,0},{3,2},{5,4},{7,6},{8,9},{10,11},{12,... | collective-permute-start | bytes 331784 | tf_op jit(solution)/shard_map/ppermute | solution.py:618
  11.3 4.2 %collective-permute-start.3 = (f32[3,72,128]{2,1,0:T(8,128)S(1)}, f32[3,72,128]{2,1,0:T(8,128)S(1)}, u32[]{:S(2)}, u32[]{:S(2)}) collective-permute-start(f32[3,72,128]{2,1,0:T(8,128)S(1)} %get-tuple-element.65), channel_id=1, source_target_pairs={{1,2},{3,4},{5,6},{2,1},{4,3},{6,5},{9,10},{11,12},{13,14},{10,9},... | collective-permute-start | bytes 331784 | tf_op jit(solution)/shard_map/ppermute | solution.py:618

commit v8 on v7

--- a/solution.py
+++ b/solution.py
@@ -580,26 +580,23 @@
     count = rows // CHUNK
     ends = [0] + [CHUNK * (p + 1) - LAG - TOP for p in range(count - 1)] + [out_ref.shape[0]]
 
-    def copies(p):
-        middle = (ends[p] + ends[p + 1]) // 16 * 8
-        return [
-            pltpu.make_async_copy(
-                outs[k].at[pl.ds(TOP + first, last - first)],
-                ref.at[pl.ds(first, last - first)],
-                sems.at[4 * p + 2 * h + k],
-            )
-            for h, (first, last) in enumerate(((ends[p], middle), (middle, ends[p + 1])))
-            for k, ref in enumerate((out_ref, resid_ref))
-        ]
-
+    spans = [*zip(ends[:-2], ends[1:-1])]
+    middle = (ends[-2] + ends[-1]) // 16 * 8
+    spans += [(ends[-2], middle), (middle, ends[-1])]
+    sent = []
     for p in range(count):
-        climb(p * CHUNK, CHUNK)
-        last(max(p * CHUNK - LAG, 0), CHUNK)
-        for copy in copies(p):
-            copy.start()
-    for p in range(count):
-        for copy in copies(p):
-            copy.wait()
+        start, stop = max(p * CHUNK, TOP - 8), min((p + 1) * CHUNK, rows - TOP + 8)
+        climb(start, stop - start)
+        for first, end in spans[p : p + 1] if p < count - 1 else spans[p:]:
+            last(TOP + first, end - first)
+            for k, ref in enumerate((out_ref, resid_ref)):
+                size = end - first
+                source = outs[k].at[pl.ds(TOP + first, size)]
+                copy = pltpu.make_async_copy(source, ref.at[pl.ds(first, size)], sems.at[len(sent)])
+                copy.start()
+                sent.append(copy)
+    for copy in sent:
+        copy.wait()
 
 
 def call(kernel, out_shape, scratch, flops, moved, **more):

time: 37 us -> 36.9 us (level)
  no operation moved by 1% of the time
where the time goes in v8:
time: 36.9 us; the launch traced here: 36.6 us
  blocking collectives  13.5 us (37%)
  Pallas kernels  12.5 us (34%)
  starting transfers between devices  7.31 us (20%)
  other arithmetic  2.54 us (7%)
  between operations  0.75 us (2%)
    all_to_all x1, blocking collectives, local(): lax.all_to_all(chunks.reshape(nx * ny, 4, LANES), ('gx', 'gy'), 0, 0)  13.5 us
    ppermute x4, starting transfers between devices, swap(): return lax.ppermute(x, axis, pairs + [(j, i) for i, j in pairs])  7.31 us
    pallas_call x1, Pallas kernels, local(): call(up_kernel, (out(rows, columns), out(rows, columns)), [vmem(3, ring),...  5.19 us
    pallas_call x1, Pallas kernels, local(): call(body_kernel, [out(*shape(2, level)) for level in levels for _ in ran...  3.49 us
    pallas_call x1, Pallas kernels, local(): call(frame_kernel, [out(*shape(1, 0))] * 3 + [out(*shape(1, level)) for l...  2.38 us
    mul x1, other arithmetic, fields(): return (wet * r, wet * p, wet * (1.0 + 0.5 * c.astype(jnp.float32)))  1.67 us
    pallas_call x1, Pallas kernels, local(): call(layout_kernel, laid_out, inner, 10 * cells, 10 * cells)  1.27 us
    another operation x3, other arithmetic, edge(): jnp.stack(fields(*(lax.dynamic_slice_in_dim(x, start, TOP, axis=0) for x...  0.87 us
  transfers between devices with their start and end apart: 4, of which 0 were waited for; matrix products, arithmetic and copies ran while one was open for 5% of the time, Pallas kernels for 13%

profile of v8, /device:TPU:0, one launch (start us, length us, event | category | flops | bytes accessed | tf_op | source)
XLA Modules:
  0.0 36.6 jit_solution(15347458711828634668)
XLA Ops:
  0.6 0.9 %multiply_bitcast_fusion.2 = (f32[1,16,256]{2,1,0:T(8,128)S(1)}, f32[1,16,256]{2,1,0:T(8,128)S(1)}, f32[1,16,256]{2,1,0:T(8,128)S(1)}, f32[1,16,256]{2,1,0:T(8,1...) fusion(f32[512,256]{1,0:T(8,128)} %param.4, s32[]{:T(128)S(6)} %select_n.24, s32[512,256]{1,0:T(8,128)} %param.6, ...), kind=kLoop, calls=%fused_computation.7 | loop fusion | flops 57344 | bytes 229384 | tf_op jit(solution)/shard_map/stack | solution.py:640
  1.5 0.7 %collective-permute-start = (f32[3,16,256]{2,1,0:T(8,128)S(1)}, f32[3,16,256]{2,1,0:T(8,128)S(1)}, u32[]{:S(2)}, u32[]{:S(2)}) collective-permute-start(f32[3,16,256]{2,1,0:T(8,128)S(1)} %pad_maximum_fusion), channel_id=1, source_target_pairs={{8,16},{16,8},{9,17},{17,9},{10,18},{18,10},{11,19},{19,11},{12,20... | collective-permute-start | bytes 147464 | tf_op jit(solution)/shard_map/ppermute | solution.py:615
  2.2 5.9 %collective-permute-start.1 = (f32[3,16,256]{2,1,0:T(8,128)S(1)}, f32[3,16,256]{2,1,0:T(8,128)S(1)}, u32[]{:S(2)}, u32[]{:S(2)}) collective-permute-start(f32[3,16,256]{2,1,0:T(8,128)S(1)} %pad_maximum_fusion.1), channel_id=1, source_target_pairs={{0,8},{16,24},{8,0},{24,16},{1,9},{17,25},{9,1},{25,17},{2,10},{18... | collective-permute-start | bytes 147464 | tf_op jit(solution)/shard_map/ppermute | solution.py:615
  8.1 1.7 %add_multiply_fusion = (f32[512,256]{1,0:T(8,128)S(1)}, f32[512,256]{1,0:T(8,128)S(1)}, f32[512,256]{1,0:T(8,128)S(1)}) fusion(s32[512,256]{1,0:T(8,128)} %param.7, s32[512,256]{1,0:T(8,128)} %param.6, f32[512,256]{1,0:T(8,128)} %param.5, f32[512,256]{1,0:T(8,128)} %param.4), kind=kLoop, calls=%fused_computation | loop fusion | flops 917504 | bytes 3670016 | tf_op jit(solution)/shard_map/mul | solution.py:635
  9.8 1.3 %shard_map.59 = (f32[2,560,128]{2,1,0:T(8,128)S(1)}, f32[2,560,128]{2,1,0:T(8,128)S(1)}, f32[2,560,128]{2,1,0:T(8,128)S(1)}, f32[1,560,128]{2,1,0:T(8,128)S(1)},...) custom-call(f32[512,256]{1,0:T(8,128)S(1)} %get-tuple-element.116.so, ...), custom_call_target="tpu_custom_call" | custom-call | flops 1310720 | bytes 1310720 | tf_op jit(solution)/shard_map/pallas_call | solution.py:649
  11.1 0.0 collective-permute-done.refs_8_
  11.1 0.0 collective-permute-done.1.refs_9_
  11.1 0.1 shard_map.60
  11.2 0.1 collective-permute-start.2
  11.3 0.7 %collective-permute-start.3 = (f32[3,72,128]{2,1,0:T(8,128)S(1)}, f32[3,72,128]{2,1,0:T(8,128)S(1)}, u32[]{:S(2)}, u32[]{:S(2)}) collective-permute-start(f32[3,72,128]{2,1,0:T(8,128)S(1)} %get-tuple-element.65), channel_id=1, source_target_pairs={{1,2},{3,4},{5,6},{2,1},{4,3},{6,5},{9,10},{11,12},{13,14},{10,9},... | collective-permute-start | bytes 331784 | tf_op jit(solution)/shard_map/ppermute | solution.py:615
  12.0 3.5 %shard_map.61 = (f32[2,560,128]{2,1,0:T(8,128)S(1)}, f32[2,560,128]{2,1,0:T(8,128)S(1)}, f32[2,560,128]{2,1,0:T(8,128)S(1)}, f32[2,560,128]{2,1,0:T(8,128)S(1)},...) custom-call(f32[2,560,128]{2,1,0:T(8,128)S(1)} %get-tuple-element.66, ...), custom_call_target="tpu_custom_call" | custom-call | flops 13107200 | bytes 5242880 | tf_op jit(solution)/shard_map/pallas_call | solution.py:658
  15.5 0.0 collective-permute-done.2.from_pair
  15.5 0.0 collective-permute-done.3.from_cross
  15.5 2.4 %shard_map.62 = (f32[1,560,128]{2,1,0:T(8,128)S(1)}, f32[1,560,128]{2,1,0:T(8,128)S(1)}, f32[1,560,128]{2,1,0:T(8,128)S(1)}, f32[1,560,128]{2,1,0:T(8,128)S(1)},...) custom-call(f32[1,560,128]{2,1,0:T(8,128)S(1)} %get-tuple-element.61, ...), custom_call_target="tpu_custom_call", output_to_operand_aliasing={{0}: (0, {}), {1}: (1, {}), {2}: (2, {})} | custom-call | flops 6553600 | bytes 2621440 | tf_op jit(solution)/shard_map/pallas_call | solution.py:669
  17.9 13.5 %all_to_all.5 = f32[32,4,128]{2,1,0:T(4,128)S(1)} all-to-all(f32[32,4,128]{2,1,0:T(4,128)S(1)} %bitcast.15), channel_id=1, replica_groups=mesh['gx'=4,'gy'=8] {'gx','gy'}, dimensions={0} | all-to-all | bytes 131072 | tf_op jit(solution)/shard_map/all_to_all | solution.py:682
  31.4 5.2 %shard_map.63 = (f32[512,256]{1,0:T(8,128)}, f32[512,256]{1,0:T(8,128)}) custom-call(f32[4,8,4,128]{3,2,1,0:T(4,128)S(1)} %bitcast.14, f32[8,128]{1,0:T(8,128)S(1)} %get-tuple-element.72.dense_ref, f32[3,72,128]{2,1,0:T(8,128)S(1)} %collective-permute-done.3.from_cross, f32[3,72,128]{2,1,0:T(8,128)S(1)} %collective-permute-done.2.from_pair, ...), custom_call_target="tpu_custom_call" | custom-call | flops 7864320 | bytes 5242880 | tf_op jit(solution)/shard_map/pallas_call | solution.py:683
  (2 shorter events, 0.0 us)
Async XLA Ops:
  1.5 9.6 %collective-permute-start = (f32[3,16,256]{2,1,0:T(8,128)S(1)}, f32[3,16,256]{2,1,0:T(8,128)S(1)}, u32[]{:S(2)}, u32[]{:S(2)}) collective-permute-start(f32[3,16,256]{2,1,0:T(8,128)S(1)} %pad_maximum_fusion), channel_id=1, source_target_pairs={{8,16},{16,8},{9,17},{17,9},{10,18},{18,10},{11,19},{19,11},{12,20... | collective-permute-start | bytes 147464 | tf_op jit(solution)/shard_map/ppermute | solution.py:615
  2.2 8.9 %collective-permute-start.1 = (f32[3,16,256]{2,1,0:T(8,128)S(1)}, f32[3,16,256]{2,1,0:T(8,128)S(1)}, u32[]{:S(2)}, u32[]{:S(2)}) collective-permute-start(f32[3,16,256]{2,1,0:T(8,128)S(1)} %pad_maximum_fusion.1), channel_id=1, source_target_pairs={{0,8},{16,24},{8,0},{24,16},{1,9},{17,25},{9,1},{25,17},{2,10},{18... | collective-permute-start | bytes 147464 | tf_op jit(solution)/shard_map/ppermute | solution.py:615
  11.2 4.3 %collective-permute-start.2 = (f32[3,72,128]{2,1,0:T(8,128)S(1)}, f32[3,72,128]{2,1,0:T(8,128)S(1)}, u32[]{:S(2)}, u32[]{:S(2)}) collective-permute-start(f32[3,72,128]{2,1,0:T(8,128)S(1)} %get-tuple-element.64), channel_id=1, source_target_pairs={{0,1},{2,3},{4,5},{6,7},{1,0},{3,2},{5,4},{7,6},{8,9},{10,11},{12,... | collective-permute-start | bytes 331784 | tf_op jit(solution)/shard_map/ppermute | solution.py:615
  11.3 4.2 %collective-permute-start.3 = (f32[3,72,128]{2,1,0:T(8,128)S(1)}, f32[3,72,128]{2,1,0:T(8,128)S(1)}, u32[]{:S(2)}, u32[]{:S(2)}) collective-permute-start(f32[3,72,128]{2,1,0:T(8,128)S(1)} %get-tuple-element.65), channel_id=1, source_target_pairs={{1,2},{3,4},{5,6},{2,1},{4,3},{6,5},{9,10},{11,12},{13,14},{10,9},... | collective-permute-start | bytes 331784 | tf_op jit(solution)/shard_map/ppermute | solution.py:615

commit v9 on v8

--- a/solution.py
+++ b/solution.py
@@ -476,29 +476,27 @@
 
     tall = b.shape[0]
     zeros = jnp.zeros((GUARD, LANES), jnp.float32)
-    e_ref[0:GUARD, :] = zeros
-    e_ref[GUARD + tall :, :] = zeros
-
-    def shifted(by):
-        return e_ref[GUARD + by : GUARD + by + tall, :]
-
-    e_ref[GUARD : GUARD + tall, :] = w
+    for k in range(2):
+        e_ref[k, 0:GUARD, :] = zeros
+        e_ref[k, GUARD + tall :, :] = zeros
+
+    def shifted(k, by):
+        return e_ref[k, GUARD + by : GUARD + by + tall, :]
+
+    e_ref[1, GUARD : GUARD + tall, :] = w
     c_west = jnp.minimum(w, roll(w, 1))
-    c_north, c_south = jnp.minimum(w, shifted(-1)), jnp.minimum(w, shifted(1))
+    c_north, c_south = jnp.minimum(w, shifted(1, -1)), jnp.minimum(w, shifted(1, 1))
     c_east = roll(c_west, -1)
     scale = relaxation / (damping + c_north + c_south + c_west + c_east)
     first = scale * b
     c_west, c_east, c_north, c_south = (scale * c for c in (c_west, c_east, c_north, c_south))
-    e_ref[GUARD : GUARD + tall, :] = first
-
-    def sweep(_, carry):
-        e = shifted(0)
-        around = (c_west * roll(e, 1) + c_east * roll(e, -1)) + (c_north * shifted(-1) + c_south * shifted(1))
-        e_ref[GUARD : GUARD + tall, :] = ((1.0 - relaxation) * e + first) + around
-        return carry
-
-    lax.fori_loop(0, SWEEPS - 1, sweep, 0)
-    return shifted(0)
+    e_ref[0, GUARD : GUARD + tall, :] = first
+    for sweep in range(SWEEPS - 1):
+        k = sweep % 2
+        e = shifted(k, 0)
+        around = (c_west * roll(e, 1) + c_east * roll(e, -1)) + (c_north * shifted(k, -1) + c_south * shifted(k, 1))
+        e_ref[1 - k, GUARD : GUARD + tall, :] = ((1.0 - relaxation) * e + first) + around
+    return shifted((SWEEPS - 1) % 2, 0)
 
 
 def up_kernel(all_ref, dense_ref, from_cross, from_pair, own_source, frame_source, own_diagonal, frame_diagonal, *refs):
@@ -684,7 +682,7 @@
         up_kernel,
         (out(rows, columns), out(rows, columns)),
         [vmem(3, ring), vmem(2, 0), vmem(1, 0), pltpu.SemaphoreType.DMA((16,))]
-        + [pltpu.VMEM(((rows >> LEVELS) + 2 * TALL + 2 * GUARD, LANES), jnp.float32), vmem(3, ring)]
+        + [pltpu.VMEM((2, (rows >> LEVELS) + 2 * TALL + 2 * GUARD, LANES), jnp.float32), vmem(3, ring)]
         + [pltpu.VMEM((total, columns), jnp.float32)] * 2
         + [vmem(2, level) for level in levels]
         + [vmem(1, level) for level in levels],

time: 36.9 us -> 36.7 us (level)
  no operation moved by 1% of the time
where the time goes in v9:
time: 36.7 us; the launch traced here: 36.4 us
  blocking collectives  13.5 us (37%)
  Pallas kernels  12.2 us (33%)
  starting transfers between devices  7.31 us (20%)
  other arithmetic  2.54 us (7%)
  between operations  0.75 us (2%)
    all_to_all x1, blocking collectives, local(): lax.all_to_all(chunks.reshape(nx * ny, 4, LANES), ('gx', 'gy'), 0, 0)  13.5 us
    ppermute x4, starting transfers between devices, swap(): return lax.ppermute(x, axis, pairs + [(j, i) for i, j in pairs])  7.31 us
    pallas_call x1, Pallas kernels, local(): call(up_kernel, (out(rows, columns), out(rows, columns)), [vmem(3, ring),...  4.95 us
    pallas_call x1, Pallas kernels, local(): call(body_kernel, [out(*shape(2, level)) for level in levels for _ in ran...  3.49 us
    pallas_call x1, Pallas kernels, local(): call(frame_kernel, [out(*shape(1, 0))] * 3 + [out(*shape(1, level)) for l...  2.38 us
    mul x1, other arithmetic, fields(): return (wet * r, wet * p, wet * (1.0 + 0.5 * c.astype(jnp.float32)))  1.67 us
    pallas_call x1, Pallas kernels, local(): call(layout_kernel, laid_out, inner, 10 * cells, 10 * cells)  1.27 us
    another operation x3, other arithmetic, edge(): jnp.stack(fields(*(lax.dynamic_slice_in_dim(x, start, TOP, axis=0) for x...  0.87 us
  transfers between devices with their start and end apart: 4, of which 0 were waited for; matrix products, arithmetic and copies ran while one was open for 5% of the time, Pallas kernels for 13%

profile of v9, /device:TPU:0, one launch (start us, length us, event | category | flops | bytes accessed | tf_op | source)
XLA Modules:
  0.0 36.4 jit_solution(4847203188650392791)
XLA Ops:
  0.6 0.9 %multiply_bitcast_fusion.2 = (f32[1,16,256]{2,1,0:T(8,128)S(1)}, f32[1,16,256]{2,1,0:T(8,128)S(1)}, f32[1,16,256]{2,1,0:T(8,128)S(1)}, f32[1,16,256]{2,1,0:T(8,1...) fusion(f32[512,256]{1,0:T(8,128)} %param.4, s32[]{:T(128)S(6)} %select_n.24, s32[512,256]{1,0:T(8,128)} %param.6, ...), kind=kLoop, calls=%fused_computation.7 | loop fusion | flops 57344 | bytes 229384 | tf_op jit(solution)/shard_map/stack | solution.py:638
  1.5 0.7 %collective-permute-start = (f32[3,16,256]{2,1,0:T(8,128)S(1)}, f32[3,16,256]{2,1,0:T(8,128)S(1)}, u32[]{:S(2)}, u32[]{:S(2)}) collective-permute-start(f32[3,16,256]{2,1,0:T(8,128)S(1)} %pad_maximum_fusion), channel_id=1, source_target_pairs={{8,16},{16,8},{9,17},{17,9},{10,18},{18,10},{11,19},{19,11},{12,20... | collective-permute-start | bytes 147464 | tf_op jit(solution)/shard_map/ppermute | solution.py:613
  2.2 5.9 %collective-permute-start.1 = (f32[3,16,256]{2,1,0:T(8,128)S(1)}, f32[3,16,256]{2,1,0:T(8,128)S(1)}, u32[]{:S(2)}, u32[]{:S(2)}) collective-permute-start(f32[3,16,256]{2,1,0:T(8,128)S(1)} %pad_maximum_fusion.1), channel_id=1, source_target_pairs={{0,8},{16,24},{8,0},{24,16},{1,9},{17,25},{9,1},{25,17},{2,10},{18... | collective-permute-start | bytes 147464 | tf_op jit(solution)/shard_map/ppermute | solution.py:613
  8.1 1.7 %add_multiply_fusion = (f32[512,256]{1,0:T(8,128)S(1)}, f32[512,256]{1,0:T(8,128)S(1)}, f32[512,256]{1,0:T(8,128)S(1)}) fusion(s32[512,256]{1,0:T(8,128)} %param.7, s32[512,256]{1,0:T(8,128)} %param.6, f32[512,256]{1,0:T(8,128)} %param.5, f32[512,256]{1,0:T(8,128)} %param.4), kind=kLoop, calls=%fused_computation | loop fusion | flops 917504 | bytes 3670016 | tf_op jit(solution)/shard_map/mul | solution.py:633
  9.8 1.3 %shard_map.59 = (f32[2,560,128]{2,1,0:T(8,128)S(1)}, f32[2,560,128]{2,1,0:T(8,128)S(1)}, f32[2,560,128]{2,1,0:T(8,128)S(1)}, f32[1,560,128]{2,1,0:T(8,128)S(1)},...) custom-call(f32[512,256]{1,0:T(8,128)S(1)} %get-tuple-element.116.so, ...), custom_call_target="tpu_custom_call" | custom-call | flops 1310720 | bytes 1310720 | tf_op jit(solution)/shard_map/pallas_call | solution.py:647
  11.1 0.0 collective-permute-done.refs_8_
  11.1 0.0 collective-permute-done.1.refs_9_
  11.1 0.1 shard_map.60
  11.2 0.1 collective-permute-start.2
  11.3 0.7 %collective-permute-start.3 = (f32[3,72,128]{2,1,0:T(8,128)S(1)}, f32[3,72,128]{2,1,0:T(8,128)S(1)}, u32[]{:S(2)}, u32[]{:S(2)}) collective-permute-start(f32[3,72,128]{2,1,0:T(8,128)S(1)} %get-tuple-element.65), channel_id=1, source_target_pairs={{1,2},{3,4},{5,6},{2,1},{4,3},{6,5},{9,10},{11,12},{13,14},{10,9},... | collective-permute-start | bytes 331784 | tf_op jit(solution)/shard_map/ppermute | solution.py:613
  12.0 3.5 %shard_map.61 = (f32[2,560,128]{2,1,0:T(8,128)S(1)}, f32[2,560,128]{2,1,0:T(8,128)S(1)}, f32[2,560,128]{2,1,0:T(8,128)S(1)}, f32[2,560,128]{2,1,0:T(8,128)S(1)},...) custom-call(f32[2,560,128]{2,1,0:T(8,128)S(1)} %get-tuple-element.66, ...), custom_call_target="tpu_custom_call" | custom-call | flops 13107200 | bytes 5242880 | tf_op jit(solution)/shard_map/pallas_call | solution.py:656
  15.5 0.0 collective-permute-done.2.from_pair
  15.5 0.0 collective-permute-done.3.from_cross
  15.5 2.4 %shard_map.62 = (f32[1,560,128]{2,1,0:T(8,128)S(1)}, f32[1,560,128]{2,1,0:T(8,128)S(1)}, f32[1,560,128]{2,1,0:T(8,128)S(1)}, f32[1,560,128]{2,1,0:T(8,128)S(1)},...) custom-call(f32[1,560,128]{2,1,0:T(8,128)S(1)} %get-tuple-element.61, ...), custom_call_target="tpu_custom_call", output_to_operand_aliasing={{0}: (0, {}), {1}: (1, {}), {2}: (2, {})} | custom-call | flops 6553600 | bytes 2621440 | tf_op jit(solution)/shard_map/pallas_call | solution.py:667
  17.9 13.5 %all_to_all.5 = f32[32,4,128]{2,1,0:T(4,128)S(1)} all-to-all(f32[32,4,128]{2,1,0:T(4,128)S(1)} %bitcast.15), channel_id=1, replica_groups=mesh['gx'=4,'gy'=8] {'gx','gy'}, dimensions={0} | all-to-all | bytes 131072 | tf_op jit(solution)/shard_map/all_to_all | solution.py:680
  31.4 5.0 %shard_map.63 = (f32[512,256]{1,0:T(8,128)}, f32[512,256]{1,0:T(8,128)}) custom-call(f32[4,8,4,128]{3,2,1,0:T(4,128)S(1)} %bitcast.14, f32[8,128]{1,0:T(8,128)S(1)} %get-tuple-element.72.dense_ref, f32[3,72,128]{2,1,0:T(8,128)S(1)} %collective-permute-done.3.from_cross, f32[3,72,128]{2,1,0:T(8,128)S(1)} %collective-permute-done.2.from_pair, ...), custom_call_target="tpu_custom_call" | custom-call | flops 7864320 | bytes 5242880 | tf_op jit(solution)/shard_map/pallas_call | solution.py:681
  (2 shorter events, 0.0 us)
Async XLA Ops:
  1.5 9.6 %collective-permute-start = (f32[3,16,256]{2,1,0:T(8,128)S(1)}, f32[3,16,256]{2,1,0:T(8,128)S(1)}, u32[]{:S(2)}, u32[]{:S(2)}) collective-permute-start(f32[3,16,256]{2,1,0:T(8,128)S(1)} %pad_maximum_fusion), channel_id=1, source_target_pairs={{8,16},{16,8},{9,17},{17,9},{10,18},{18,10},{11,19},{19,11},{12,20... | collective-permute-start | bytes 147464 | tf_op jit(solution)/shard_map/ppermute | solution.py:613
  2.2 8.9 %collective-permute-start.1 = (f32[3,16,256]{2,1,0:T(8,128)S(1)}, f32[3,16,256]{2,1,0:T(8,128)S(1)}, u32[]{:S(2)}, u32[]{:S(2)}) collective-permute-start(f32[3,16,256]{2,1,0:T(8,128)S(1)} %pad_maximum_fusion.1), channel_id=1, source_target_pairs={{0,8},{16,24},{8,0},{24,16},{1,9},{17,25},{9,1},{25,17},{2,10},{18... | collective-permute-start | bytes 147464 | tf_op jit(solution)/shard_map/ppermute | solution.py:613
  11.2 4.3 %collective-permute-start.2 = (f32[3,72,128]{2,1,0:T(8,128)S(1)}, f32[3,72,128]{2,1,0:T(8,128)S(1)}, u32[]{:S(2)}, u32[]{:S(2)}) collective-permute-start(f32[3,72,128]{2,1,0:T(8,128)S(1)} %get-tuple-element.64), channel_id=1, source_target_pairs={{0,1},{2,3},{4,5},{6,7},{1,0},{3,2},{5,4},{7,6},{8,9},{10,11},{12,... | collective-permute-start | bytes 331784 | tf_op jit(solution)/shard_map/ppermute | solution.py:613
  11.3 4.2 %collective-permute-start.3 = (f32[3,72,128]{2,1,0:T(8,128)S(1)}, f32[3,72,128]{2,1,0:T(8,128)S(1)}, u32[]{:S(2)}, u32[]{:S(2)}) collective-permute-start(f32[3,72,128]{2,1,0:T(8,128)S(1)} %get-tuple-element.65), channel_id=1, source_target_pairs={{1,2},{3,4},{5,6},{2,1},{4,3},{6,5},{9,10},{11,12},{13,14},{10,9},... | collective-permute-start | bytes 331784 | tf_op jit(solution)/shard_map/ppermute | solution.py:613

commit v10 on v9

--- a/solution.py
+++ b/solution.py
@@ -491,11 +491,14 @@
     first = scale * b
     c_west, c_east, c_north, c_south = (scale * c for c in (c_west, c_east, c_north, c_south))
     e_ref[0, GUARD : GUARD + tall, :] = first
+    trim = TALL // 2
     for sweep in range(SWEEPS - 1):
         k = sweep % 2
-        e = shifted(k, 0)
-        around = (c_west * roll(e, 1) + c_east * roll(e, -1)) + (c_north * shifted(k, -1) + c_south * shifted(k, 1))
-        e_ref[1 - k, GUARD : GUARD + tall, :] = ((1.0 - relaxation) * e + first) + around
+        cut = trim if SWEEPS - 1 - sweep <= TALL - trim else 0
+        here = slice(cut, tall - cut)
+        e, north, south = (shifted(k, by)[here] for by in (0, -1, 1))
+        around = (c_west[here] * roll(e, 1) + c_east[here] * roll(e, -1)) + (c_north[here] * north + c_south[here] * south)
+        e_ref[1 - k, GUARD + cut : GUARD + tall - cut, :] = ((1.0 - relaxation) * e + first[here]) + around
     return shifted((SWEEPS - 1) % 2, 0)
 
 

time: 36.7 us -> 36.8 us (level)
  no operation moved by 1% of the time
where the time goes in v10:
time: 36.8 us; the launch traced here: 36.5 us
  blocking collectives  13.5 us (37%)
  Pallas kernels  12.3 us (33%)
  starting transfers between devices  7.31 us (20%)
  other arithmetic  2.54 us (7%)
  between operations  0.75 us (2%)
    all_to_all x1, blocking collectives, local(): lax.all_to_all(chunks.reshape(nx * ny, 4, LANES), ('gx', 'gy'), 0, 0)  13.5 us
    ppermute x4, starting transfers between devices, swap(): return lax.ppermute(x, axis, pairs + [(j, i) for i, j in pairs])  7.31 us
    pallas_call x1, Pallas kernels, local(): call(up_kernel, (out(rows, columns), out(rows, columns)), [vmem(3, ring),...  5.04 us
    pallas_call x1, Pallas kernels, local(): call(body_kernel, [out(*shape(2, level)) for level in levels for _ in ran...  3.49 us
    pallas_call x1, Pallas kernels, local(): call(frame_kernel, [out(*shape(1, 0))] * 3 + [out(*shape(1, level)) for l...  2.38 us
    mul x1, other arithmetic, fields(): return (wet * r, wet * p, wet * (1.0 + 0.5 * c.astype(jnp.float32)))  1.67 us
    pallas_call x1, Pallas kernels, local(): call(layout_kernel, laid_out, inner, 10 * cells, 10 * cells)  1.27 us
    another operation x3, other arithmetic, edge(): jnp.stack(fields(*(lax.dynamic_slice_in_dim(x, start, TOP, axis=0) for x...  0.87 us
  transfers between devices with their start and end apart: 4, of which 0 were waited for; matrix products, arithmetic and copies ran while one was open for 5% of the time, Pallas kernels for 13%

profile of v10, /device:TPU:0, one launch (start us, length us, event | category | flops | bytes accessed | tf_op | source)
XLA Modules:
  0.0 36.5 jit_solution(14450773356864994721)
XLA Ops:
  0.6 0.9 %multiply_bitcast_fusion.2 = (f32[1,16,256]{2,1,0:T(8,128)S(1)}, f32[1,16,256]{2,1,0:T(8,128)S(1)}, f32[1,16,256]{2,1,0:T(8,128)S(1)}, f32[1,16,256]{2,1,0:T(8,1...) fusion(f32[512,256]{1,0:T(8,128)} %param.4, s32[]{:T(128)S(6)} %select_n.24, s32[512,256]{1,0:T(8,128)} %param.6, ...), kind=kLoop, calls=%fused_computation.7 | loop fusion | flops 57344 | bytes 229384 | tf_op jit(solution)/shard_map/stack | solution.py:641
  1.5 0.7 %collective-permute-start = (f32[3,16,256]{2,1,0:T(8,128)S(1)}, f32[3,16,256]{2,1,0:T(8,128)S(1)}, u32[]{:S(2)}, u32[]{:S(2)}) collective-permute-start(f32[3,16,256]{2,1,0:T(8,128)S(1)} %pad_maximum_fusion), channel_id=1, source_target_pairs={{8,16},{16,8},{9,17},{17,9},{10,18},{18,10},{11,19},{19,11},{12,20... | collective-permute-start | bytes 147464 | tf_op jit(solution)/shard_map/ppermute | solution.py:616
  2.2 5.9 %collective-permute-start.1 = (f32[3,16,256]{2,1,0:T(8,128)S(1)}, f32[3,16,256]{2,1,0:T(8,128)S(1)}, u32[]{:S(2)}, u32[]{:S(2)}) collective-permute-start(f32[3,16,256]{2,1,0:T(8,128)S(1)} %pad_maximum_fusion.1), channel_id=1, source_target_pairs={{0,8},{16,24},{8,0},{24,16},{1,9},{17,25},{9,1},{25,17},{2,10},{18... | collective-permute-start | bytes 147464 | tf_op jit(solution)/shard_map/ppermute | solution.py:616
  8.1 1.7 %add_multiply_fusion = (f32[512,256]{1,0:T(8,128)S(1)}, f32[512,256]{1,0:T(8,128)S(1)}, f32[512,256]{1,0:T(8,128)S(1)}) fusion(s32[512,256]{1,0:T(8,128)} %param.7, s32[512,256]{1,0:T(8,128)} %param.6, f32[512,256]{1,0:T(8,128)} %param.5, f32[512,256]{1,0:T(8,128)} %param.4), kind=kLoop, calls=%fused_computation | loop fusion | flops 917504 | bytes 3670016 | tf_op jit(solution)/shard_map/mul | solution.py:636
  9.8 1.3 %shard_map.59 = (f32[2,560,128]{2,1,0:T(8,128)S(1)}, f32[2,560,128]{2,1,0:T(8,128)S(1)}, f32[2,560,128]{2,1,0:T(8,128)S(1)}, f32[1,560,128]{2,1,0:T(8,128)S(1)},...) custom-call(f32[512,256]{1,0:T(8,128)S(1)} %get-tuple-element.116.so, ...), custom_call_target="tpu_custom_call" | custom-call | flops 1310720 | bytes 1310720 | tf_op jit(solution)/shard_map/pallas_call | solution.py:650
  11.1 0.0 collective-permute-done.refs_8_
  11.1 0.0 collective-permute-done.1.refs_9_
  11.1 0.1 shard_map.60
  11.2 0.1 collective-permute-start.2
  11.3 0.7 %collective-permute-start.3 = (f32[3,72,128]{2,1,0:T(8,128)S(1)}, f32[3,72,128]{2,1,0:T(8,128)S(1)}, u32[]{:S(2)}, u32[]{:S(2)}) collective-permute-start(f32[3,72,128]{2,1,0:T(8,128)S(1)} %get-tuple-element.65), channel_id=1, source_target_pairs={{1,2},{3,4},{5,6},{2,1},{4,3},{6,5},{9,10},{11,12},{13,14},{10,9},... | collective-permute-start | bytes 331784 | tf_op jit(solution)/shard_map/ppermute | solution.py:616
  12.0 3.5 %shard_map.61 = (f32[2,560,128]{2,1,0:T(8,128)S(1)}, f32[2,560,128]{2,1,0:T(8,128)S(1)}, f32[2,560,128]{2,1,0:T(8,128)S(1)}, f32[2,560,128]{2,1,0:T(8,128)S(1)},...) custom-call(f32[2,560,128]{2,1,0:T(8,128)S(1)} %get-tuple-element.66, ...), custom_call_target="tpu_custom_call" | custom-call | flops 13107200 | bytes 5242880 | tf_op jit(solution)/shard_map/pallas_call | solution.py:659
  15.5 0.0 collective-permute-done.2.from_pair
  15.5 0.0 collective-permute-done.3.from_cross
  15.5 2.4 %shard_map.62 = (f32[1,560,128]{2,1,0:T(8,128)S(1)}, f32[1,560,128]{2,1,0:T(8,128)S(1)}, f32[1,560,128]{2,1,0:T(8,128)S(1)}, f32[1,560,128]{2,1,0:T(8,128)S(1)},...) custom-call(f32[1,560,128]{2,1,0:T(8,128)S(1)} %get-tuple-element.61, ...), custom_call_target="tpu_custom_call", output_to_operand_aliasing={{0}: (0, {}), {1}: (1, {}), {2}: (2, {})} | custom-call | flops 6553600 | bytes 2621440 | tf_op jit(solution)/shard_map/pallas_call | solution.py:670
  17.9 13.5 %all_to_all.5 = f32[32,4,128]{2,1,0:T(4,128)S(1)} all-to-all(f32[32,4,128]{2,1,0:T(4,128)S(1)} %bitcast.15), channel_id=1, replica_groups=mesh['gx'=4,'gy'=8] {'gx','gy'}, dimensions={0} | all-to-all | bytes 131072 | tf_op jit(solution)/shard_map/all_to_all | solution.py:683
  31.4 5.0 %shard_map.63 = (f32[512,256]{1,0:T(8,128)}, f32[512,256]{1,0:T(8,128)}) custom-call(f32[4,8,4,128]{3,2,1,0:T(4,128)S(1)} %bitcast.14, f32[8,128]{1,0:T(8,128)S(1)} %get-tuple-element.72.dense_ref, f32[3,72,128]{2,1,0:T(8,128)S(1)} %collective-permute-done.3.from_cross, f32[3,72,128]{2,1,0:T(8,128)S(1)} %collective-permute-done.2.from_pair, ...), custom_call_target="tpu_custom_call" | custom-call | flops 7864320 | bytes 5242880 | tf_op jit(solution)/shard_map/pallas_call | solution.py:684
  (2 shorter events, 0.0 us)
Async XLA Ops:
  1.5 9.6 %collective-permute-start = (f32[3,16,256]{2,1,0:T(8,128)S(1)}, f32[3,16,256]{2,1,0:T(8,128)S(1)}, u32[]{:S(2)}, u32[]{:S(2)}) collective-permute-start(f32[3,16,256]{2,1,0:T(8,128)S(1)} %pad_maximum_fusion), channel_id=1, source_target_pairs={{8,16},{16,8},{9,17},{17,9},{10,18},{18,10},{11,19},{19,11},{12,20... | collective-permute-start | bytes 147464 | tf_op jit(solution)/shard_map/ppermute | solution.py:616
  2.2 8.9 %collective-permute-start.1 = (f32[3,16,256]{2,1,0:T(8,128)S(1)}, f32[3,16,256]{2,1,0:T(8,128)S(1)}, u32[]{:S(2)}, u32[]{:S(2)}) collective-permute-start(f32[3,16,256]{2,1,0:T(8,128)S(1)} %pad_maximum_fusion.1), channel_id=1, source_target_pairs={{0,8},{16,24},{8,0},{24,16},{1,9},{17,25},{9,1},{25,17},{2,10},{18... | collective-permute-start | bytes 147464 | tf_op jit(solution)/shard_map/ppermute | solution.py:616
  11.2 4.3 %collective-permute-start.2 = (f32[3,72,128]{2,1,0:T(8,128)S(1)}, f32[3,72,128]{2,1,0:T(8,128)S(1)}, u32[]{:S(2)}, u32[]{:S(2)}) collective-permute-start(f32[3,72,128]{2,1,0:T(8,128)S(1)} %get-tuple-element.64), channel_id=1, source_target_pairs={{0,1},{2,3},{4,5},{6,7},{1,0},{3,2},{5,4},{7,6},{8,9},{10,11},{12,... | collective-permute-start | bytes 331784 | tf_op jit(solution)/shard_map/ppermute | solution.py:616
  11.3 4.2 %collective-permute-start.3 = (f32[3,72,128]{2,1,0:T(8,128)S(1)}, f32[3,72,128]{2,1,0:T(8,128)S(1)}, u32[]{:S(2)}, u32[]{:S(2)}) collective-permute-start(f32[3,72,128]{2,1,0:T(8,128)S(1)} %get-tuple-element.65), channel_id=1, source_target_pairs={{1,2},{3,4},{5,6},{2,1},{4,3},{6,5},{9,10},{11,12},{13,14},{10,9},... | collective-permute-start | bytes 331784 | tf_op jit(solution)/shard_map/ppermute | solution.py:616

commit v11 on v9

--- a/solution.py
+++ b/solution.py
@@ -316,7 +316,7 @@
             lane = lane_of(both)
             outside = (lane < HALO) | (lane >= LANES - HALO)
             frame[0, span, :] = jnp.where(outside, both, frame[0, span, :])
-    descend_all(rows, sources, frame_guess, weights, states, diagonals, field, resid, 4 * CHUNK, 2 * CHUNK)
+    descend_all(rows, sources, frame_guess, weights, states, diagonals, field, resid, 4 * CHUNK, CHUNK)
 
     level = LEVELS - 1
     step, halo, height = 2**level, TOP >> level, rows >> level

time: 36.7 us -> 36.9 us (level)
  no operation moved by 1% of the time
where the time goes in v11:
time: 36.9 us; the launch traced here: 36.6 us
  blocking collectives  13.5 us (37%)
  Pallas kernels  12.4 us (34%)
  starting transfers between devices  7.31 us (20%)
  other arithmetic  2.54 us (7%)
  between operations  0.75 us (2%)
    all_to_all x1, blocking collectives, local(): lax.all_to_all(chunks.reshape(nx * ny, 4, LANES), ('gx', 'gy'), 0, 0)  13.5 us
    ppermute x4, starting transfers between devices, swap(): return lax.ppermute(x, axis, pairs + [(j, i) for i, j in pairs])  7.31 us
    pallas_call x1, Pallas kernels, local(): call(up_kernel, (out(rows, columns), out(rows, columns)), [vmem(3, ring),...  4.95 us
    pallas_call x1, Pallas kernels, local(): call(body_kernel, [out(*shape(2, level)) for level in levels for _ in ran...  3.49 us
    pallas_call x1, Pallas kernels, local(): call(frame_kernel, [out(*shape(1, 0))] * 3 + [out(*shape(1, level)) for l...  2.57 us
    mul x1, other arithmetic, fields(): return (wet * r, wet * p, wet * (1.0 + 0.5 * c.astype(jnp.float32)))  1.67 us
    pallas_call x1, Pallas kernels, local(): call(layout_kernel, laid_out, inner, 10 * cells, 10 * cells)  1.27 us
    another operation x3, other arithmetic, edge(): jnp.stack(fields(*(lax.dynamic_slice_in_dim(x, start, TOP, axis=0) for x...  0.87 us
  transfers between devices with their start and end apart: 4, of which 0 were waited for; matrix products, arithmetic and copies ran while one was open for 5% of the time, Pallas kernels for 13%

profile of v11, /device:TPU:0, one launch (start us, length us, event | category | flops | bytes accessed | tf_op | source)
XLA Modules:
  0.0 36.6 jit_solution(15738949780730094872)
XLA Ops:
  0.6 0.9 %multiply_bitcast_fusion.2 = (f32[1,16,256]{2,1,0:T(8,128)S(1)}, f32[1,16,256]{2,1,0:T(8,128)S(1)}, f32[1,16,256]{2,1,0:T(8,128)S(1)}, f32[1,16,256]{2,1,0:T(8,1...) fusion(f32[512,256]{1,0:T(8,128)} %param.4, s32[]{:T(128)S(6)} %select_n.24, s32[512,256]{1,0:T(8,128)} %param.6, ...), kind=kLoop, calls=%fused_computation.7 | loop fusion | flops 57344 | bytes 229384 | tf_op jit(solution)/shard_map/stack | solution.py:638
  1.5 0.7 %collective-permute-start = (f32[3,16,256]{2,1,0:T(8,128)S(1)}, f32[3,16,256]{2,1,0:T(8,128)S(1)}, u32[]{:S(2)}, u32[]{:S(2)}) collective-permute-start(f32[3,16,256]{2,1,0:T(8,128)S(1)} %pad_maximum_fusion), channel_id=1, source_target_pairs={{8,16},{16,8},{9,17},{17,9},{10,18},{18,10},{11,19},{19,11},{12,20... | collective-permute-start | bytes 147464 | tf_op jit(solution)/shard_map/ppermute | solution.py:613
  2.2 5.9 %collective-permute-start.1 = (f32[3,16,256]{2,1,0:T(8,128)S(1)}, f32[3,16,256]{2,1,0:T(8,128)S(1)}, u32[]{:S(2)}, u32[]{:S(2)}) collective-permute-start(f32[3,16,256]{2,1,0:T(8,128)S(1)} %pad_maximum_fusion.1), channel_id=1, source_target_pairs={{0,8},{16,24},{8,0},{24,16},{1,9},{17,25},{9,1},{25,17},{2,10},{18... | collective-permute-start | bytes 147464 | tf_op jit(solution)/shard_map/ppermute | solution.py:613
  8.1 1.7 %add_multiply_fusion = (f32[512,256]{1,0:T(8,128)S(1)}, f32[512,256]{1,0:T(8,128)S(1)}, f32[512,256]{1,0:T(8,128)S(1)}) fusion(s32[512,256]{1,0:T(8,128)} %param.7, s32[512,256]{1,0:T(8,128)} %param.6, f32[512,256]{1,0:T(8,128)} %param.5, f32[512,256]{1,0:T(8,128)} %param.4), kind=kLoop, calls=%fused_computation | loop fusion | flops 917504 | bytes 3670016 | tf_op jit(solution)/shard_map/mul | solution.py:633
  9.8 1.3 %shard_map.59 = (f32[2,560,128]{2,1,0:T(8,128)S(1)}, f32[2,560,128]{2,1,0:T(8,128)S(1)}, f32[2,560,128]{2,1,0:T(8,128)S(1)}, f32[1,560,128]{2,1,0:T(8,128)S(1)},...) custom-call(f32[512,256]{1,0:T(8,128)S(1)} %get-tuple-element.116.so, ...), custom_call_target="tpu_custom_call" | custom-call | flops 1310720 | bytes 1310720 | tf_op jit(solution)/shard_map/pallas_call | solution.py:647
  11.1 0.0 collective-permute-done.refs_8_
  11.1 0.0 collective-permute-done.1.refs_9_
  11.1 0.1 shard_map.60
  11.2 0.1 collective-permute-start.2
  11.3 0.7 %collective-permute-start.3 = (f32[3,72,128]{2,1,0:T(8,128)S(1)}, f32[3,72,128]{2,1,0:T(8,128)S(1)}, u32[]{:S(2)}, u32[]{:S(2)}) collective-permute-start(f32[3,72,128]{2,1,0:T(8,128)S(1)} %get-tuple-element.65), channel_id=1, source_target_pairs={{1,2},{3,4},{5,6},{2,1},{4,3},{6,5},{9,10},{11,12},{13,14},{10,9},... | collective-permute-start | bytes 331784 | tf_op jit(solution)/shard_map/ppermute | solution.py:613
  12.0 3.5 %shard_map.61 = (f32[2,560,128]{2,1,0:T(8,128)S(1)}, f32[2,560,128]{2,1,0:T(8,128)S(1)}, f32[2,560,128]{2,1,0:T(8,128)S(1)}, f32[2,560,128]{2,1,0:T(8,128)S(1)},...) custom-call(f32[2,560,128]{2,1,0:T(8,128)S(1)} %get-tuple-element.66, ...), custom_call_target="tpu_custom_call" | custom-call | flops 13107200 | bytes 5242880 | tf_op jit(solution)/shard_map/pallas_call | solution.py:656
  15.5 0.0 collective-permute-done.2.from_pair
  15.5 0.0 collective-permute-done.3.from_cross
  15.5 2.6 %shard_map.62 = (f32[1,560,128]{2,1,0:T(8,128)S(1)}, f32[1,560,128]{2,1,0:T(8,128)S(1)}, f32[1,560,128]{2,1,0:T(8,128)S(1)}, f32[1,560,128]{2,1,0:T(8,128)S(1)},...) custom-call(f32[1,560,128]{2,1,0:T(8,128)S(1)} %get-tuple-element.61, ...), custom_call_target="tpu_custom_call", output_to_operand_aliasing={{0}: (0, {}), {1}: (1, {}), {2}: (2, {})} | custom-call | flops 6553600 | bytes 2621440 | tf_op jit(solution)/shard_map/pallas_call | solution.py:667
  18.1 13.5 %all_to_all.5 = f32[32,4,128]{2,1,0:T(4,128)S(1)} all-to-all(f32[32,4,128]{2,1,0:T(4,128)S(1)} %bitcast.15), channel_id=1, replica_groups=mesh['gx'=4,'gy'=8] {'gx','gy'}, dimensions={0} | all-to-all | bytes 131072 | tf_op jit(solution)/shard_map/all_to_all | solution.py:680
  31.6 5.0 %shard_map.63 = (f32[512,256]{1,0:T(8,128)}, f32[512,256]{1,0:T(8,128)}) custom-call(f32[4,8,4,128]{3,2,1,0:T(4,128)S(1)} %bitcast.14, f32[8,128]{1,0:T(8,128)S(1)} %get-tuple-element.72.dense_ref, f32[3,72,128]{2,1,0:T(8,128)S(1)} %collective-permute-done.3.from_cross, f32[3,72,128]{2,1,0:T(8,128)S(1)} %collective-permute-done.2.from_pair, ...), custom_call_target="tpu_custom_call" | custom-call | flops 7864320 | bytes 5242880 | tf_op jit(solution)/shard_map/pallas_call | solution.py:681
  (2 shorter events, 0.0 us)
Async XLA Ops:
  1.5 9.6 %collective-permute-start = (f32[3,16,256]{2,1,0:T(8,128)S(1)}, f32[3,16,256]{2,1,0:T(8,128)S(1)}, u32[]{:S(2)}, u32[]{:S(2)}) collective-permute-start(f32[3,16,256]{2,1,0:T(8,128)S(1)} %pad_maximum_fusion), channel_id=1, source_target_pairs={{8,16},{16,8},{9,17},{17,9},{10,18},{18,10},{11,19},{19,11},{12,20... | collective-permute-start | bytes 147464 | tf_op jit(solution)/shard_map/ppermute | solution.py:613
  2.2 8.9 %collective-permute-start.1 = (f32[3,16,256]{2,1,0:T(8,128)S(1)}, f32[3,16,256]{2,1,0:T(8,128)S(1)}, u32[]{:S(2)}, u32[]{:S(2)}) collective-permute-start(f32[3,16,256]{2,1,0:T(8,128)S(1)} %pad_maximum_fusion.1), channel_id=1, source_target_pairs={{0,8},{16,24},{8,0},{24,16},{1,9},{17,25},{9,1},{25,17},{2,10},{18... | collective-permute-start | bytes 147464 | tf_op jit(solution)/shard_map/ppermute | solution.py:613
  11.2 4.3 %collective-permute-start.2 = (f32[3,72,128]{2,1,0:T(8,128)S(1)}, f32[3,72,128]{2,1,0:T(8,128)S(1)}, u32[]{:S(2)}, u32[]{:S(2)}) collective-permute-start(f32[3,72,128]{2,1,0:T(8,128)S(1)} %get-tuple-element.64), channel_id=1, source_target_pairs={{0,1},{2,3},{4,5},{6,7},{1,0},{3,2},{5,4},{7,6},{8,9},{10,11},{12,... | collective-permute-start | bytes 331784 | tf_op jit(solution)/shard_map/ppermute | solution.py:613
  11.3 4.2 %collective-permute-start.3 = (f32[3,72,128]{2,1,0:T(8,128)S(1)}, f32[3,72,128]{2,1,0:T(8,128)S(1)}, u32[]{:S(2)}, u32[]{:S(2)}) collective-permute-start(f32[3,72,128]{2,1,0:T(8,128)S(1)} %get-tuple-element.65), channel_id=1, source_target_pairs={{1,2},{3,4},{5,6},{2,1},{4,3},{6,5},{9,10},{11,12},{13,14},{10,9},... | collective-permute-start | bytes 331784 | tf_op jit(solution)/shard_map/ppermute | solution.py:613

commit v12 on v11

--- a/solution.py
+++ b/solution.py
@@ -316,7 +316,7 @@
             lane = lane_of(both)
             outside = (lane < HALO) | (lane >= LANES - HALO)
             frame[0, span, :] = jnp.where(outside, both, frame[0, span, :])
-    descend_all(rows, sources, frame_guess, weights, states, diagonals, field, resid, 4 * CHUNK, CHUNK)
+    descend_all(rows, sources, frame_guess, weights, states, diagonals, field, resid, 4 * CHUNK, 4 * CHUNK)
 
     level = LEVELS - 1
     step, halo, height = 2**level, TOP >> level, rows >> level

time: 36.9 us -> 36.6 us (level)
  no operation moved by 1% of the time
where the time goes in v12:
time: 36.6 us; the launch traced here: 36.3 us
  blocking collectives  13.5 us (37%)
  Pallas kernels  12.1 us (33%)
  starting transfers between devices  7.31 us (20%)
  other arithmetic  2.54 us (7%)
  between operations  0.75 us (2%)
    all_to_all x1, blocking collectives, local(): lax.all_to_all(chunks.reshape(nx * ny, 4, LANES), ('gx', 'gy'), 0, 0)  13.5 us
    ppermute x4, starting transfers between devices, swap(): return lax.ppermute(x, axis, pairs + [(j, i) for i, j in pairs])  7.31 us
    pallas_call x1, Pallas kernels, local(): call(up_kernel, (out(rows, columns), out(rows, columns)), [vmem(3, ring),...  4.95 us
    pallas_call x1, Pallas kernels, local(): call(body_kernel, [out(*shape(2, level)) for level in levels for _ in ran...  3.49 us
    pallas_call x1, Pallas kernels, local(): call(frame_kernel, [out(*shape(1, 0))] * 3 + [out(*shape(1, level)) for l...  2.3 us
    mul x1, other arithmetic, fields(): return (wet * r, wet * p, wet * (1.0 + 0.5 * c.astype(jnp.float32)))  1.67 us
    pallas_call x1, Pallas kernels, local(): call(layout_kernel, laid_out, inner, 10 * cells, 10 * cells)  1.27 us
    another operation x3, other arithmetic, edge(): jnp.stack(fields(*(lax.dynamic_slice_in_dim(x, start, TOP, axis=0) for x...  0.87 us
  transfers between devices with their start and end apart: 4, of which 0 were waited for; matrix products, arithmetic and copies ran while one was open for 5% of the time, Pallas kernels for 13%

profile of v12, /device:TPU:0, one launch (start us, length us, event | category | flops | bytes accessed | tf_op | source)
XLA Modules:
  0.0 36.3 jit_solution(16487225148938544714)
XLA Ops:
  0.6 0.9 %multiply_bitcast_fusion.2 = (f32[1,16,256]{2,1,0:T(8,128)S(1)}, f32[1,16,256]{2,1,0:T(8,128)S(1)}, f32[1,16,256]{2,1,0:T(8,128)S(1)}, f32[1,16,256]{2,1,0:T(8,1...) fusion(f32[512,256]{1,0:T(8,128)} %param.4, s32[]{:T(128)S(6)} %select_n.24, s32[512,256]{1,0:T(8,128)} %param.6, ...), kind=kLoop, calls=%fused_computation.7 | loop fusion | flops 57344 | bytes 229384 | tf_op jit(solution)/shard_map/stack | solution.py:638
  1.5 0.7 %collective-permute-start = (f32[3,16,256]{2,1,0:T(8,128)S(1)}, f32[3,16,256]{2,1,0:T(8,128)S(1)}, u32[]{:S(2)}, u32[]{:S(2)}) collective-permute-start(f32[3,16,256]{2,1,0:T(8,128)S(1)} %pad_maximum_fusion), channel_id=1, source_target_pairs={{8,16},{16,8},{9,17},{17,9},{10,18},{18,10},{11,19},{19,11},{12,20... | collective-permute-start | bytes 147464 | tf_op jit(solution)/shard_map/ppermute | solution.py:613
  2.2 5.9 %collective-permute-start.1 = (f32[3,16,256]{2,1,0:T(8,128)S(1)}, f32[3,16,256]{2,1,0:T(8,128)S(1)}, u32[]{:S(2)}, u32[]{:S(2)}) collective-permute-start(f32[3,16,256]{2,1,0:T(8,128)S(1)} %pad_maximum_fusion.1), channel_id=1, source_target_pairs={{0,8},{16,24},{8,0},{24,16},{1,9},{17,25},{9,1},{25,17},{2,10},{18... | collective-permute-start | bytes 147464 | tf_op jit(solution)/shard_map/ppermute | solution.py:613
  8.1 1.7 %add_multiply_fusion = (f32[512,256]{1,0:T(8,128)S(1)}, f32[512,256]{1,0:T(8,128)S(1)}, f32[512,256]{1,0:T(8,128)S(1)}) fusion(s32[512,256]{1,0:T(8,128)} %param.7, s32[512,256]{1,0:T(8,128)} %param.6, f32[512,256]{1,0:T(8,128)} %param.5, f32[512,256]{1,0:T(8,128)} %param.4), kind=kLoop, calls=%fused_computation | loop fusion | flops 917504 | bytes 3670016 | tf_op jit(solution)/shard_map/mul | solution.py:633
  9.8 1.3 %shard_map.59 = (f32[2,560,128]{2,1,0:T(8,128)S(1)}, f32[2,560,128]{2,1,0:T(8,128)S(1)}, f32[2,560,128]{2,1,0:T(8,128)S(1)}, f32[1,560,128]{2,1,0:T(8,128)S(1)},...) custom-call(f32[512,256]{1,0:T(8,128)S(1)} %get-tuple-element.116.so, ...), custom_call_target="tpu_custom_call" | custom-call | flops 1310720 | bytes 1310720 | tf_op jit(solution)/shard_map/pallas_call | solution.py:647
  11.1 0.0 collective-permute-done.refs_8_
  11.1 0.0 collective-permute-done.1.refs_9_
  11.1 0.1 shard_map.60
  11.2 0.1 collective-permute-start.2
  11.3 0.7 %collective-permute-start.3 = (f32[3,72,128]{2,1,0:T(8,128)S(1)}, f32[3,72,128]{2,1,0:T(8,128)S(1)}, u32[]{:S(2)}, u32[]{:S(2)}) collective-permute-start(f32[3,72,128]{2,1,0:T(8,128)S(1)} %get-tuple-element.65), channel_id=1, source_target_pairs={{1,2},{3,4},{5,6},{2,1},{4,3},{6,5},{9,10},{11,12},{13,14},{10,9},... | collective-permute-start | bytes 331784 | tf_op jit(solution)/shard_map/ppermute | solution.py:613
  12.0 3.5 %shard_map.61 = (f32[2,560,128]{2,1,0:T(8,128)S(1)}, f32[2,560,128]{2,1,0:T(8,128)S(1)}, f32[2,560,128]{2,1,0:T(8,128)S(1)}, f32[2,560,128]{2,1,0:T(8,128)S(1)},...) custom-call(f32[2,560,128]{2,1,0:T(8,128)S(1)} %get-tuple-element.66, ...), custom_call_target="tpu_custom_call" | custom-call | flops 13107200 | bytes 5242880 | tf_op jit(solution)/shard_map/pallas_call | solution.py:656
  15.5 0.0 collective-permute-done.2.from_pair
  15.5 0.0 collective-permute-done.3.from_cross
  15.5 2.3 %shard_map.62 = (f32[1,560,128]{2,1,0:T(8,128)S(1)}, f32[1,560,128]{2,1,0:T(8,128)S(1)}, f32[1,560,128]{2,1,0:T(8,128)S(1)}, f32[1,560,128]{2,1,0:T(8,128)S(1)},...) custom-call(f32[1,560,128]{2,1,0:T(8,128)S(1)} %get-tuple-element.61, ...), custom_call_target="tpu_custom_call", output_to_operand_aliasing={{0}: (0, {}), {1}: (1, {}), {2}: (2, {})} | custom-call | flops 6553600 | bytes 2621440 | tf_op jit(solution)/shard_map/pallas_call | solution.py:667
  17.8 13.5 %all_to_all.5 = f32[32,4,128]{2,1,0:T(4,128)S(1)} all-to-all(f32[32,4,128]{2,1,0:T(4,128)S(1)} %bitcast.15), channel_id=1, replica_groups=mesh['gx'=4,'gy'=8] {'gx','gy'}, dimensions={0} | all-to-all | bytes 131072 | tf_op jit(solution)/shard_map/all_to_all | solution.py:680
  31.3 5.0 %shard_map.63 = (f32[512,256]{1,0:T(8,128)}, f32[512,256]{1,0:T(8,128)}) custom-call(f32[4,8,4,128]{3,2,1,0:T(4,128)S(1)} %bitcast.14, f32[8,128]{1,0:T(8,128)S(1)} %get-tuple-element.72.dense_ref, f32[3,72,128]{2,1,0:T(8,128)S(1)} %collective-permute-done.3.from_cross, f32[3,72,128]{2,1,0:T(8,128)S(1)} %collective-permute-done.2.from_pair, ...), custom_call_target="tpu_custom_call" | custom-call | flops 7864320 | bytes 5242880 | tf_op jit(solution)/shard_map/pallas_call | solution.py:681
  (2 shorter events, 0.0 us)
Async XLA Ops:
  1.5 9.6 %collective-permute-start = (f32[3,16,256]{2,1,0:T(8,128)S(1)}, f32[3,16,256]{2,1,0:T(8,128)S(1)}, u32[]{:S(2)}, u32[]{:S(2)}) collective-permute-start(f32[3,16,256]{2,1,0:T(8,128)S(1)} %pad_maximum_fusion), channel_id=1, source_target_pairs={{8,16},{16,8},{9,17},{17,9},{10,18},{18,10},{11,19},{19,11},{12,20... | collective-permute-start | bytes 147464 | tf_op jit(solution)/shard_map/ppermute | solution.py:613
  2.2 8.9 %collective-permute-start.1 = (f32[3,16,256]{2,1,0:T(8,128)S(1)}, f32[3,16,256]{2,1,0:T(8,128)S(1)}, u32[]{:S(2)}, u32[]{:S(2)}) collective-permute-start(f32[3,16,256]{2,1,0:T(8,128)S(1)} %pad_maximum_fusion.1), channel_id=1, source_target_pairs={{0,8},{16,24},{8,0},{24,16},{1,9},{17,25},{9,1},{25,17},{2,10},{18... | collective-permute-start | bytes 147464 | tf_op jit(solution)/shard_map/ppermute | solution.py:613
  11.2 4.3 %collective-permute-start.2 = (f32[3,72,128]{2,1,0:T(8,128)S(1)}, f32[3,72,128]{2,1,0:T(8,128)S(1)}, u32[]{:S(2)}, u32[]{:S(2)}) collective-permute-start(f32[3,72,128]{2,1,0:T(8,128)S(1)} %get-tuple-element.64), channel_id=1, source_target_pairs={{0,1},{2,3},{4,5},{6,7},{1,0},{3,2},{5,4},{7,6},{8,9},{10,11},{12,... | collective-permute-start | bytes 331784 | tf_op jit(solution)/shard_map/ppermute | solution.py:613
  11.3 4.2 %collective-permute-start.3 = (f32[3,72,128]{2,1,0:T(8,128)S(1)}, f32[3,72,128]{2,1,0:T(8,128)S(1)}, u32[]{:S(2)}, u32[]{:S(2)}) collective-permute-start(f32[3,72,128]{2,1,0:T(8,128)S(1)} %get-tuple-element.65), channel_id=1, source_target_pairs={{1,2},{3,4},{5,6},{2,1},{4,3},{6,5},{9,10},{11,12},{13,14},{10,9},... | collective-permute-start | bytes 331784 | tf_op jit(solution)/shard_map/ppermute | solution.py:613
